TPU v7x, 256 devices: a whole 4x4x8 slice. The times are simulated.
256 devices in a mesh: ctx: 4 (over y), sp: 32 (over z, x_lo, core), dp: 2 (over x_hi).
Axes of the slice: x: 4 (x_hi: 2, x_lo: 2; x = x_hi * 2 + x_lo), y: 4, z: 8, core: 2. Of those that a mesh axis runs over, the one named last changes fastest.
Arguments:
- resid: bfloat16 [32768, 2048], P(('dp', 'ctx', 'sp')), parts along dimension 0, may hold values from -6 to 6
- conv_weight: bfloat16 [4, 2048], replicated, may hold values from -3 to 3
- queries: bfloat16 [32768, 2048], P(('dp', 'ctx', 'sp')), parts along dimension 0, may hold values from -100 to 100
- keys: bfloat16 [32768, 256], P(('dp', 'ctx', 'sp')), parts along dimension 0, may hold values from -5 to 5
- values: bfloat16 [32768, 256], P(('dp', 'ctx', 'sp')), parts along dimension 0, may hold values from -6 to 6
- gates: bfloat16 [32768, 2048], P(('dp', 'ctx', 'sp')), parts along dimension 0, may hold values from -6 to 6
- out_weight: bfloat16 [2048, 2048], P('sp'), may hold values from -0.125 to 0.125
- norm_gain: float32 [2048], replicated, may hold values from 0.5 to 1.5
- lens_weight: bfloat16 [2048, 81920], P(None, ('ctx', 'sp')), may hold values from -0.41992188 to 0.41992188
Outputs:
- mixed: bfloat16 [32768, 2048], P(('dp', 'ctx', 'sp')), parts along dimension 0
- lens_logits: float32 [2048, 81920], P('dp', ('ctx', 'sp')), parts along dimension 0
There are 2 independent parts, one for each index of `dp`. A program takes and returns all parts, laid end to end along the dimension named above; an argument that names none is the same for every part. Nothing has to cross between parts.
All inputs are finite; a program needn't handle non-finite values.
Results may differ from a plain program's by a relative error of at most 0.013.
Values may be sent and summed in bfloat16 or wider, within the bound.
No kernel may reach another device: no remote copies, remote signals or barrier semaphores. Data moves between devices by JAX's collectives and lax.ppermute only.
A program may use at most 128 MiB of HBM per device.

v0:
```python
import math

import jax
import jax.numpy as jnp
from jax import lax
from jax.sharding import PartitionSpec as P

LENS_DEV = 8


NEG_FILL = -1e30


def padded_2(block, sides, width):
    for axis, dim in sides:
        count = lax.axis_size(axis)
        forward = [(i, i + 1) for i in range(count - 1)]
        backward = [(target, source) for source, target in forward]
        low = lax.ppermute(
            lax.slice_in_dim(block, block.shape[dim] - width, None, axis=dim), axis, forward
        )
        high = lax.ppermute(lax.slice_in_dim(block, 0, width, axis=dim), axis, backward)
        block = jnp.concatenate([low, block, high], axis=dim)
    return block


def stretch_base(stretch_id, dev_count, half_len):
    holder = stretch_id // 2
    return jnp.where(
        stretch_id % 2 == 0, holder * half_len, (2 * dev_count - 1 - holder) * half_len
    )


def short_conv(prefix, block_rows, taps):
    extended = jnp.concatenate([prefix, block_rows], 0).astype(jnp.float32)
    row_total = block_rows.shape[0]
    lag_rows = taps.shape[0] - 1
    conv_sum = jnp.zeros(block_rows.shape, jnp.float32)
    for tap_index in range(lag_rows + 1):
        conv_sum = (
            conv_sum
            + taps[tap_index].astype(jnp.float32)
            * extended[lag_rows - tap_index : lag_rows - tap_index + row_total]
        )
    return conv_sum


def attend_block(
    state_in, key_block, value_block, key_place, query_rows, query_base, head_count, masked
):
    row_max, running, accumulated = state_in
    scores = lax.dot_general(
        key_block, query_rows, (((1,), (1,)), ((), ())), preferred_element_type=jnp.float32
    )
    scores = scores * (1.0 / math.sqrt(key_block.shape[1]))
    if masked:
        query_place = (
            query_base + (jnp.arange(query_rows.shape[0], dtype=jnp.int32) // head_count)[None, :]
        )
        scores = jnp.where(key_place[:, None] <= query_place, scores, NEG_FILL)
    new_max = jnp.maximum(row_max, jnp.max(scores, axis=0))
    weights = jnp.exp(scores - new_max[None, :])
    factor = jnp.exp(row_max - new_max)
    running = running * factor + jnp.sum(weights, axis=0)
    rounded = weights.astype(jnp.bfloat16)
    product = lax.dot_general(
        rounded, value_block, (((0,), (0,)), ((), ())), preferred_element_type=jnp.float32
    )
    accumulated = accumulated * factor[:, None] + product
    return (new_max, running, accumulated)


def body(resid, conv_weight, queries, keys, values, gates, out_weight, norm_gain, lens_weight):
    tok_rows, feat_width = resid.shape
    half_len = tok_rows // 2
    lag_rows = conv_weight.shape[0] - 1
    dev_count = lax.axis_size(("ctx", "sp"))
    my_index = lax.axis_index(("ctx", "sp"))
    rims = jnp.concatenate([resid[tok_rows - lag_rows :], resid[half_len - lag_rows : half_len]], 0)
    padded = padded_2(rims, ((("ctx", "sp"), 0),), lag_rows)
    before_first = padded[:lag_rows]
    before_second = jnp.where(
        my_index == dev_count - 1, resid[half_len - lag_rows : half_len], padded[3 * lag_rows :]
    )
    conv_first = short_conv(before_first, resid[:half_len], conv_weight)
    conv_second = short_conv(before_second, resid[half_len:], conv_weight)
    conv_all = jnp.concatenate([conv_first, conv_second], 0)
    hidden = (resid.astype(jnp.float32) + jax.nn.silu(conv_all)).astype(jnp.bfloat16)
    head_size = keys.shape[1]
    head_count = queries.shape[1] // head_size
    query_pair = (
        queries[:half_len].reshape(half_len * head_count, head_size),
        queries[half_len:].reshape(half_len * head_count, head_size),
    )
    query_bases = (my_index * half_len, (2 * dev_count - 1 - my_index) * half_len)
    query_total = half_len * head_count
    empty_state = (
        jnp.full((query_total,), NEG_FILL, jnp.float32),
        jnp.zeros((query_total,), jnp.float32),
        jnp.zeros((query_total, head_size), jnp.float32),
    )
    initial = (empty_state, empty_state)

    def fold_keys(states_in, key_piece):
        piece_keys, piece_values = key_piece
        stretch_total = piece_keys.shape[0] // half_len
        group_size = math.gcd(stretch_total, 16)
        group_total = stretch_total // group_size
        key_groups = piece_keys.reshape(group_total, group_size * half_len, head_size)
        value_groups = piece_values.reshape(group_total, group_size * half_len, head_size)
        span_rows = jnp.arange(half_len, dtype=jnp.int32)

        def run_group(group_id, states):
            key_block = lax.dynamic_index_in_dim(key_groups, group_id, 0, keepdims=False)
            value_block = lax.dynamic_index_in_dim(value_groups, group_id, 0, keepdims=False)
            stretch_ids = group_id * group_size + jnp.arange(group_size, dtype=jnp.int32)
            bases = stretch_base(stretch_ids, dev_count, half_len)
            key_place = (bases[:, None] + span_rows[None, :]).reshape(group_size * half_len)
            lowest = jnp.min(bases)
            highest = jnp.max(bases) + half_len - 1
            results = []
            for which_half in range(2):
                query_base = query_bases[which_half]

                def skip(state_now):
                    return state_now

                def partial_view(state_now, which_half=which_half):
                    return attend_block(
                        state_now,
                        key_block,
                        value_block,
                        key_place,
                        query_pair[which_half],
                        query_bases[which_half],
                        head_count,
                        True,
                    )

                def full_view(state_now, which_half=which_half):
                    return attend_block(
                        state_now,
                        key_block,
                        value_block,
                        key_place,
                        query_pair[which_half],
                        query_bases[which_half],
                        head_count,
                        False,
                    )

                branch = jnp.where(
                    lowest > query_base, 0, jnp.where(highest <= query_base, 2, 1)
                ).astype(jnp.int32)
                results.append(
                    lax.switch(branch, [skip, partial_view, full_view], states[which_half])
                )
            return (results[0], results[1])

        return lax.fori_loop(0, group_total, run_group, states_in)

    final_states = fold_keys(
        initial,
        (
            lax.all_gather(keys, ("ctx", "sp"), axis=0, tiled=True),
            lax.all_gather(values, ("ctx", "sp"), axis=0, tiled=True),
        ),
    )
    halves = []
    for which_half in range(2):
        row_max, running, accumulated = final_states[which_half]
        halves.append((accumulated / running[:, None]).reshape(half_len, head_count * head_size))
    att = jnp.concatenate(halves, 0)
    gated_rows = (jax.nn.sigmoid(gates.astype(jnp.float32)) * att).astype(jnp.bfloat16)
    projected = jnp.dot(
        gated_rows,
        lax.all_gather(out_weight, "sp", axis=0, tiled=True),
        preferred_element_type=jnp.float32,
    )
    mixed = (hidden.astype(jnp.float32) + projected).astype(jnp.bfloat16)
    stride = tok_rows // LENS_DEV
    selected = mixed.reshape(LENS_DEV, stride, feat_width)[:, stride - 1].astype(jnp.float32)
    normed = (
        selected
        * lax.rsqrt(jnp.mean(selected * selected, axis=-1, keepdims=True) + 1e-06)
        * norm_gain
    ).astype(jnp.bfloat16)
    lens_logits = jnp.dot(
        lax.all_gather(normed, ("ctx", "sp"), axis=0, tiled=True),
        lens_weight,
        preferred_element_type=jnp.float32,
    )
    return (mixed, lens_logits)


def solution(mesh):
    return jax.shard_map(
        body,
        mesh=mesh,
        in_specs=(
            P(("dp", "ctx", "sp"), None),
            P(),
            P(("dp", "ctx", "sp"), None),
            P(("dp", "ctx", "sp"), None),
            P(("dp", "ctx", "sp"), None),
            P(("dp", "ctx", "sp"), None),
            P("sp", None),
            P(),
            P(None, ("ctx", "sp")),
        ),
        out_specs=(P(("dp", "ctx", "sp"), None), P("dp", ("ctx", "sp"))),
        check_vma=False,
    )
```

profile of v0, /device:TPU:1, one launch (start us, length us, event | category | flops | bytes accessed | tf_op | source)
XLA Modules:
  0.0 894.0 jit_solution(193645836955241758)
XLA Ops:
  10.2 5.1 collective-permute-start.1
  16.5 1.9 fusion.49
  18.4 1.1 reshape.113
  19.4 1.8 reshape.114
  22.0 1.9 collective-permute-start
  25.1 1.4 fusion.38
  26.6 206.9 %all-gather.5.cloned.1.call-done = bf16[16384,256]{1,0:T(8,128)(2,1)} async-done(((bf16[128,256]{1,0:T(8,128)(2,1)}), bf16[16384,256]{1,0:T(8,128)(2,1)}) %all-gather.5.cloned.1.call-update) | async-done | bytes 8388624 | tf_op jit(solution)/shard_map/all_gather | solution.py:165
  233.5 220.3 %all-gather.7.cloned.1.call-done = bf16[16384,256]{1,0:T(8,128)(2,1)} async-done(((bf16[128,256]{1,0:T(8,128)(2,1)}), bf16[16384,256]{1,0:T(8,128)(2,1)}) %all-gather.7.cloned.1.call-update) | async-done | bytes 8388624 | tf_op jit(solution)/shard_map/all_gather | solution.py:166
  455.4 148.8 %while.29 = (s32[]{:T(128)}, f32[512]{0:T(512)S(1)}, f32[512]{0:T(512)S(1)}, f32[512,256]{1,0:T(8,128)}, f32[512]{0:T(512)S(1)}, /*index=5*/f32[512]{0:T(512)S(1...) while((s32[]{:T(128)}, f32[512]{0:T(512)S(1)}, ...), condition=%wide.region_17.18_spmd.clone, body=%wide.region_0.17_spmd.clone.sunk | while | flops 1082667776 | bytes 27890576 | solution.py:160
  455.5 2.1 dynamic-slice_bitcast_fusion.3
  460.3 3.6 conditional.7
  460.4 1.7 fusion.48
  464.5 3.5 conditional.6
  464.6 1.6 fusion.47
  468.0 2.1 dynamic-slice_bitcast_fusion.3
  472.9 3.6 conditional.7
  472.9 1.7 multiply_reduce_fusion.1
  477.2 2.1 dynamic-slice_bitcast_fusion.3
  482.0 3.6 conditional.7
  482.1 1.6 multiply_reduce_fusion.1
  486.3 2.1 dynamic-slice_bitcast_fusion.3
  491.1 3.6 conditional.7
  491.2 1.6 multiply_reduce_fusion.1
  495.4 2.1 dynamic-slice_bitcast_fusion.3
  500.2 3.6 conditional.7
  500.2 1.6 multiply_reduce_fusion.1
  504.4 2.1 dynamic-slice_bitcast_fusion.3
  509.3 3.6 conditional.7
  509.3 1.7 multiply_reduce_fusion.1
  513.6 2.1 dynamic-slice_bitcast_fusion.3
  518.4 3.6 conditional.7
  518.4 1.6 multiply_reduce_fusion.1
  522.6 2.1 dynamic-slice_bitcast_fusion.3
  527.5 3.6 conditional.7
  527.5 1.6 multiply_reduce_fusion.1
  531.7 2.1 dynamic-slice_bitcast_fusion.3
  536.5 3.6 conditional.7
  536.6 1.6 multiply_reduce_fusion.1
  540.8 2.1 dynamic-slice_bitcast_fusion.3
  545.6 3.6 conditional.7
  545.6 1.6 multiply_reduce_fusion.1
  549.9 2.1 dynamic-slice_bitcast_fusion.3
  554.7 3.6 conditional.7
  554.7 1.6 multiply_reduce_fusion.1
  558.9 2.1 dynamic-slice_bitcast_fusion.3
  563.7 3.6 conditional.7
  563.8 1.6 multiply_reduce_fusion.1
  568.0 2.1 dynamic-slice_bitcast_fusion.3
  572.8 3.6 conditional.7
  572.9 1.6 multiply_reduce_fusion.1
  577.1 2.1 dynamic-slice_bitcast_fusion.3
  581.9 3.6 conditional.7
  581.9 1.6 multiply_reduce_fusion.1
  586.1 2.1 dynamic-slice_bitcast_fusion.3
  591.0 3.6 conditional.7
  591.0 1.6 multiply_reduce_fusion.1
  595.2 2.1 dynamic-slice_bitcast_fusion.3
  600.0 3.6 conditional.7
  600.1 1.6 multiply_reduce_fusion.1
  604.3 2.2 broadcast_divide_fusion
  606.5 1.9 reshape.115
  609.4 5.7 fusion.32
  616.0 264.3 %all-gather.11.cloned.1.call-done = bf16[1024,2048]{1,0:T(8,128)(2,1)} async-done(((bf16[8,2048]{1,0:T(8,128)(2,1)}), bf16[1024,2048]{1,0:T(8,128)(2,1)}) %all-gather.11.cloned.1.call-update) | async-done | bytes 4194320 | tf_op jit(solution)/shard_map/all_gather | solution.py:189
  880.4 7.1 fusion.52
  (256 shorter events, 64.0 us)
Async XLA Ops:
  7.2 873.2 %copy-start = (bf16[2048,640]{1,0:T(8,128)(2,1)S(1)}, bf16[2048,640]{1,0:T(8,128)(2,1)}, u32[]{:S(2)}) copy-start(bf16[2048,640]{1,0:T(8,128)(2,1)} %param.25) | copy-start | bytes 7864324
  7.2 11.1 %copy-start.9 = (bf16[4,2048]{1,0:T(4,128)(2,1)S(1)}, bf16[4,2048]{1,0:T(4,128)(2,1)}, u32[]{:S(2)}) copy-start(bf16[4,2048]{1,0:T(4,128)(2,1)} %param.18) | copy-start | bytes 49156
  7.2 226.3 %all-gather.5.cloned.1.call-start = ((), (), s32[]{:S(2)}) async-start(), calls=%async_computation | async-start | bytes 8454144 | tf_op jit(solution)/shard_map/all_gather | solution.py:165
  7.9 445.8 %all-gather.7.cloned.1.call-start = ((), (), s32[]{:S(2)}) async-start(), calls=%async_computation.1 | async-start | bytes 8454144 | tf_op jit(solution)/shard_map/all_gather | solution.py:166
  8.7 600.7 %all-gather.9.cloned.1.call-start = ((), (), s32[]{:S(2)}) async-start(), calls=%async_computation.2 | async-start | bytes 8650752 | tf_op jit(solution)/shard_map/all_gather | solution.py:177
  9.4 871.0 %all-gather.11.cloned.1.call-start = ((), (), s32[]{:S(2)}) async-start(), calls=%async_computation.3 | async-start | bytes 4227072 | tf_op jit(solution)/shard_map/all_gather | solution.py:189
  10.2 11.0 %collective-permute-start.1 = (bf16[3,2048]{1,0:T(4,128)(2,1)S(1)}, bf16[3,2048]{1,0:T(4,128)(2,1)S(1)}, u32[]{:S(2)}, u32[]{:S(2)}) collective-permute-start(bf16[3,2048]{1,0:T(4,128)(2,1)S(1)} %slice.72), channel_id=1, source_target_pairs={{2,0},{4,2},{6,4},{8,6},{10,8},{12,10},{14,12},{16,14},{18,16},{20... | collective-permute-start | bytes 36872 | tf_op jit(solution)/shard_map/ppermute | solution.py:22
  22.0 3.1 collective-permute-start
  460.4 2.0 copy-start.5
  463.1 0.8 copy-start.7
  464.6 2.0 copy-start.1
  467.2 0.8 copy-start.3
  472.9 2.1 copy-start.6
  475.7 0.8 copy-start.8
  482.0 2.1 copy-start.6
  484.8 0.8 copy-start.8
  491.2 2.1 copy-start.6
  493.9 0.8 copy-start.8
  500.2 2.1 copy-start.6
  503.0 0.8 copy-start.8
  509.3 2.1 copy-start.6
  512.1 0.8 copy-start.8
  518.4 2.1 copy-start.6
  521.2 0.8 copy-start.8
  527.5 2.1 copy-start.6
  530.2 0.8 copy-start.8
  536.6 2.1 copy-start.6
  539.3 0.8 copy-start.8
  545.6 2.1 copy-start.6
  548.4 0.8 copy-start.8
  554.7 2.1 copy-start.6
  557.4 0.8 copy-start.8
  563.8 2.1 copy-start.6
  566.5 0.8 copy-start.8
  572.8 2.1 copy-start.6
  575.6 0.8 copy-start.8
  581.9 2.1 copy-start.6
  584.6 0.8 copy-start.8
  591.0 2.1 copy-start.6
  593.7 0.8 copy-start.8
  600.1 2.1 copy-start.6
  602.8 0.8 copy-start.8
  609.4 5.9 copy-start.11
  615.1 272.4 %copy-start.10 = (bf16[128,2048]{1,0:T(8,128)(2,1)}, bf16[128,2048]{1,0:T(8,128)(2,1)S(1)}, u32[]{:S(2)}) copy-start(bf16[128,2048]{1,0:T(8,128)(2,1)S(1)} %fusion.32) | copy-start | bytes 1572868
Sparse Core Ops, SparseCore 0:
  9.9 223.5 all-gather.4
  235.3 218.3 all-gather.6
  455.6 70.9 all-gather.8
  616.1 264.1 all-gather.10
where the time goes:
time: 896 us; the launch traced here: 894 us
  waiting for transfers between devices  695 us (78%)
  local copies, waits for them, and re-layouts  58.9 us (7%)
  matrix products  51.5 us (6%)
  other arithmetic  35.1 us (4%)
  loops' own time  32.7 us (4%)
  between operations  13.9 us (2%)
    all_gather x1, waiting for transfers between devices, body(): lax.all_gather(normed, ('ctx', 'sp'), axis=0, tiled=True)  264 us
    all_gather x1, waiting for transfers between devices, body(): lax.all_gather(values, ('ctx', 'sp'), axis=0, tiled=True)  220 us
    all_gather x1, waiting for transfers between devices, body(): lax.all_gather(keys, ('ctx', 'sp'), axis=0, tiled=True)  207 us
    squeeze x16, local copies, waits for them, and re-layouts, run_group(): lax.dynamic_index_in_dim(value_groups, group_id, 0, keepdims=False)  34 us
    another operation x1, loops' own time, fold_keys(): return lax.fori_loop(0, group_total, run_group, states_in)  31.5 us
    dot_general x17, matrix products, attend_block(): lax.dot_general(key_block, query_rows, (((1,), (1,)), ((), ())), preferre...  27.9 us
  transfers between devices with their start and end apart: 6, of which 4 were waited for; matrix products, arithmetic and copies ran while one was open for 13% of the time, Pallas kernels for 0%

commit v1 on v0

v1 whole, which is shorter than its diff:
```python
import functools
import math

import jax
import jax.numpy as jnp
from jax import lax
from jax.experimental import pallas as pl
from jax.experimental.pallas import tpu as pltpu
from jax.sharding import Mesh
from jax.sharding import PartitionSpec as P

NY, NZ, NX, NC = 4, 8, 2, 2
HEADS, HD = 8, 256
HALF = 64
TEAM = NX * NC
SUPER = TEAM * HALF
CHUNKS = 2 * NY * NZ
NEG = -1e30
LOG2E = math.log2(math.e)
BK = 512
BF = jnp.bfloat16
F32 = jnp.float32


def shift(x, axis, by, count):
    return lax.ppermute(x, axis, [(i, (i + by) % count) for i in range(count)])


def moved(entries, axis, delta):
    return [(tuple(o + (delta if a == axis else 0) for a, o in enumerate(off)), r0, n) for off, r0, n in entries]


AXES = {"y": (0, NY), "z": (1, NZ), "xl": (2, NX)}


def joined(pieces):
    arrays = [p[0] for p in pieces]
    entries = [e for p in pieces for e in p[1]]
    return (arrays[0] if len(arrays) == 1 else jnp.concatenate(arrays, 0)), entries


def split(x, entries):
    rows = x.shape[0]
    if len(entries) % 2 == 0:
        k = len(entries) // 2
        low, high = entries[:k], entries[k:]
    else:
        assert len(entries) == 1
        off, r0, n = entries[0]
        low, high = [(off, r0, n // 2)], [(off, r0 + n // 2, n // 2)]
    return (x[: rows // 2], low), (x[rows // 2 :], high)


def hop(piece, name, by):
    axis, count = AXES[name]
    return shift(piece[0], name, by, count), moved(piece[1], axis, -by)


def pair(piece, name="xl"):
    return [piece, hop(piece, name, 1)]


def direct(piece, name):
    count = AXES[name][1]
    return [piece] + [hop(piece, name, s) for s in range(1, count)]


def two_step(piece, name="z"):
    a, b = hop(piece, name, 1), hop(piece, name, -1)
    c, d = hop(piece, name, 2), hop(piece, name, -2)
    e, f = hop(c, name, 1), hop(d, name, -1)
    g = hop(split(*c)[0], name, 2)
    h = hop(split(*d)[1], name, -2)
    return [piece, a, b, c, d, e, f, g, h]


def ring(piece, name):
    count = AXES[name][1]
    out, fwd, bwd = [piece], piece, piece
    for _ in range(count // 2 - 1):
        fwd, bwd = hop(fwd, name, 1), hop(bwd, name, -1)
        out += [fwd, bwd]
    return out + [hop(split(*fwd)[0], name, 1), hop(split(*bwd)[1], name, -1)]


def wrapped(entry, y, z, xl):
    off = entry[0]
    return (y + off[0]) % NY, (z + off[1]) % NZ, (xl + off[2]) % NX


def attention_kernel(layout, place, *refs):
    n_in = len(layout)
    q_refs, kv_refs = refs[:TEAM], refs[TEAM : TEAM + n_in]
    keep_ref, send_ref, lse_ref = refs[TEAM + n_in : TEAM + n_in + 3]
    kvs, qs, acc, m_s, l_s, sems = refs[TEAM + n_in + 3 :]
    half = pl.program_id(0)
    y, z, xl, c = place[0], place[1], place[2], place[3]
    j = y * NZ + z
    k = xl * NC + c
    late = half == 1
    block = jnp.where(late, CHUNKS - 1 - j, j)

    @pl.when(half == 0)
    def _():
        copies = []
        for ref, (is_late, entries) in zip(kv_refs, layout):
            at = 0
            for off, r0, n in entries:
                jj = ((y + off[0] + NY) & (NY - 1)) * NZ + ((z + off[1] + NZ) & (NZ - 1))
                slot = (CHUNKS - 1 - jj) if is_late else jj
                dst = kvs.at[pl.ds(pl.multiple_of(slot * HALF + r0, 16), n)]
                copies.append(pltpu.make_async_copy(ref.at[pl.ds(at, n)], dst, sems.at[len(copies)]))
                at += n
        for cp in copies:
            cp.start()
        for cp in copies:
            cp.wait()

    for h in range(HEADS):
        for r in range(TEAM):
            rows = q_refs[r][pl.ds(pl.multiple_of(half * HALF, HALF), HALF), h * HD : (h + 1) * HD]
            qs[h, r * HALF : (r + 1) * HALF, :] = rows * BF(1.0 / math.sqrt(HD))
    acc[...] = jnp.zeros_like(acc)
    m_s[...] = jnp.full_like(m_s, NEG)
    l_s[...] = jnp.zeros_like(l_s)
    per = BK // HALF

    def step(b, masked):
        start = pl.multiple_of(b * BK, BK)
        kb = kvs[pl.ds(start, BK), :HD]
        vb = kvs[pl.ds(start, BK), HD:]
        if masked:
            idx = start + lax.broadcasted_iota(jnp.int32, (SUPER, BK), 1)
            sub_k = jnp.where(idx >= CHUNKS // 2 * HALF, TEAM - 1 - k, k)
            k_pos = (idx >> 6) * SUPER + sub_k * HALF + (idx & (HALF - 1))
            row = lax.broadcasted_iota(jnp.int32, (SUPER, BK), 0)
            member = (row >> 6) ^ k
            sub_q = jnp.where(late, TEAM - 1 - member, member)
            q_pos = block * SUPER + sub_q * HALF + (row & (HALF - 1))
            visible = k_pos <= q_pos
        for h in range(HEADS):
            s = lax.dot_general(qs[h], kb, (((1,), (1,)), ((), ())), preferred_element_type=F32)
            if masked:
                s = jnp.where(visible, s, NEG)
            m_old = m_s[h]
            mx = s[:, :128]
            for t in range(1, BK // 128):
                mx = jnp.maximum(mx, s[:, t * 128 : (t + 1) * 128])
            m_new = jnp.maximum(m_old, jnp.max(mx, axis=1, keepdims=True))
            alpha = jnp.exp2((m_old - m_new) * LOG2E)
            m_s[h] = m_new
            parts, total = [], l_s[h] * alpha
            for t in range(BK // 128):
                p = jnp.exp2((s[:, t * 128 : (t + 1) * 128] - m_new) * LOG2E)
                total = total + p
                parts.append(p.astype(BF))
            l_s[h] = total
            o = jnp.dot(jnp.concatenate(parts, 1), vb, preferred_element_type=F32)
            acc[h] = acc[h] * jnp.concatenate([alpha, alpha], 1) + o

    full = block // per

    def body(b, carry):
        step(b, False)
        return carry

    lax.fori_loop(0, full, body, 0)
    step(full, True)
    lane = lax.broadcasted_iota(jnp.int32, (SUPER, 128), 1)
    lse = jnp.zeros((SUPER, 128), F32)
    for h in range(HEADS):
        total = jnp.sum(l_s[h], axis=1, keepdims=True)
        o = acc[h] / total
        lse = jnp.where(lane == h, m_s[h] + jnp.log(total), lse)
        a, b = o[:, :128], o[:, 128:]
        cols = slice(h * 128, (h + 1) * 128)
        keep_ref[:, :, cols] = jnp.where(c == 0, a, b).astype(BF).reshape(TEAM, HALF, 128)
        send_ref[:, :, cols] = jnp.where(c == 0, b, a).astype(BF).reshape(TEAM, HALF, 128)
    lse_ref[0] = lse.T[:HEADS]


def attention(place, q_team, kv):
    tok, width = q_team[0].shape
    layout = [(is_late, entries) for _, is_late, entries in kv]
    n_copies = sum(len(e) for _, e in layout)
    return pl.pallas_call(
        functools.partial(attention_kernel, layout),
        grid_spec=pltpu.PrefetchScalarGridSpec(
            num_scalar_prefetch=1,
            grid=(2,),
            in_specs=[pl.BlockSpec((tok, width), lambda i, p: (0, 0))] * TEAM
            + [pl.BlockSpec(memory_space=pl.ANY)] * len(kv),
            out_specs=[pl.BlockSpec((TEAM, HALF, HEADS * 128), lambda i, p: (0, i, 0))] * 2
            + [pl.BlockSpec((1, HEADS, SUPER), lambda i, p: (i, 0, 0))],
            scratch_shapes=[
                pltpu.VMEM((CHUNKS * HALF, 2 * HD), BF),
                pltpu.VMEM((HEADS, SUPER, HD), BF),
                pltpu.VMEM((HEADS, SUPER, HD), F32),
                pltpu.VMEM((HEADS, SUPER, 128), F32),
                pltpu.VMEM((HEADS, SUPER, 128), F32),
                pltpu.SemaphoreType.DMA((n_copies,)),
            ],
        ),
        out_shape=[
            jax.ShapeDtypeStruct((TEAM, tok, HEADS * 128), BF),
            jax.ShapeDtypeStruct((TEAM, tok, HEADS * 128), BF),
            jax.ShapeDtypeStruct((2, HEADS, SUPER), F32),
        ],
        compiler_params=pltpu.CompilerParams(vmem_limit_bytes=40 * 2**20),
        cost_estimate=pl.CostEstimate(flops=10**10, bytes_accessed=8 * 2**20, transcendentals=10**7),
    )(place, *q_team, *[a for a, _, _ in kv])


def by_row(lse):
    return jnp.concatenate([lse, jnp.zeros((128 - lse.shape[0], lse.shape[1]), F32)], 0).T


def join_kernel(keep_ref, recv_ref, lse_ref, lse_recv_ref, mine_ref, other_ref, lse_out_ref):
    lane = lax.broadcasted_iota(jnp.int32, (HALF, 128), 1)
    for half in range(2):
        own, theirs = by_row(lse_ref[half]), by_row(lse_recv_ref[half])
        rows = slice(half * HALF, (half + 1) * HALF)
        joint = []
        for r in range(TEAM):
            a = own[r * HALF : (r + 1) * HALF]
            b = theirs[(r ^ 1) * HALF : ((r ^ 1) + 1) * HALF]
            m = jnp.maximum(a, b)
            wa, wb = jnp.exp(a - m), jnp.exp(b - m)
            total = wa + wb
            wa, wb = wa / total, wb / total
            joint.append(m + jnp.log(total))
            for h in range(HEADS):
                cols = slice(h * 128, (h + 1) * 128)
                o = keep_ref[r, rows, cols].astype(F32) * wa[:, h : h + 1]
                o = o + recv_ref[r ^ 1, rows, cols].astype(F32) * wb[:, h : h + 1]
                if r < 2:
                    mine_ref[r, rows, cols] = o.astype(BF)
                else:
                    other_ref[r - 2, rows, cols] = o.astype(BF)
        lse_out_ref[half] = jnp.concatenate(joint, 0).T[:HEADS]


def join(keep, recv, lse, lse_recv):
    tok, width = keep.shape[1:]
    return pl.pallas_call(
        join_kernel,
        out_shape=[
            jax.ShapeDtypeStruct((2, tok, width), BF),
            jax.ShapeDtypeStruct((2, tok, width), BF),
            jax.ShapeDtypeStruct(lse.shape, F32),
        ],
        compiler_params=pltpu.CompilerParams(vmem_limit_bytes=32 * 2**20),
    )(keep, recv, lse, lse_recv)


def project_kernel(layout, place, mine_ref, recv_ref, lse_ref, lse_recv_ref, g0_ref, g1_ref, *refs):
    w_refs = refs[: len(layout)]
    keep_ref, send_ref, ws, gated, sems = refs[len(layout) :]
    y, z = place[0], place[1]
    copies = []
    for ref, (base, entries) in zip(w_refs, layout):
        at = 0
        for off, r0, n in entries:
            head = (z + off[1] + NZ) & (NZ - 1)
            row = head * 128 + base + r0
            if base:
                row = row + ((y + off[0] + NY) & (NY - 1)) * 16
            dst = ws.at[pl.ds(pl.multiple_of(row, 16), n)]
            copies.append(pltpu.make_async_copy(ref.at[pl.ds(at, n)], dst, sems.at[len(copies)]))
            at += n
    for cp in copies:
        cp.start()
    tok = keep_ref.shape[0]
    for half in range(2):
        own, theirs = by_row(lse_ref[half]), by_row(lse_recv_ref[half])
        rows = slice(half * HALF, (half + 1) * HALF)
        for r in range(2):
            a = own[r * HALF : (r + 1) * HALF]
            b = theirs[(r + 2) * HALF : (r + 3) * HALF]
            m = jnp.maximum(a, b)
            wa, wb = jnp.exp(a - m), jnp.exp(b - m)
            total = wa + wb
            wa, wb = wa / total, wb / total
            g_ref = (g0_ref, g1_ref)[r]
            for h in range(HEADS):
                cols = slice(h * 128, (h + 1) * 128)
                o = mine_ref[r, rows, cols].astype(F32) * wa[:, h : h + 1]
                o = o + recv_ref[r, rows, cols].astype(F32) * wb[:, h : h + 1]
                o = jax.nn.sigmoid(g_ref[rows, cols].astype(F32)) * o
                gated[r * tok + half * HALF : r * tok + (half + 1) * HALF, cols] = o.astype(BF)
    for cp in copies:
        cp.wait()
    step = 512

    @pl.loop(0, keep_ref.shape[1] // step)
    def _(n):
        cols = pl.ds(pl.multiple_of(n * step, step), step)
        out = jnp.dot(gated[...], ws[:, cols], preferred_element_type=F32)
        keep_ref[:, cols] = out[:tok]
        send_ref[:, cols] = out[tok:].astype(BF)


def project(place, mine, recv, lse, lse_recv, g0, g1, weights):
    tok = mine.shape[1]
    width = weights[0][0].shape[1]
    layout = [(base, entries) for _, base, entries in weights]
    n_copies = sum(len(e) for _, e in layout)
    vm = pl.BlockSpec(memory_space=pltpu.VMEM)
    return pl.pallas_call(
        functools.partial(project_kernel, layout),
        in_specs=[pl.BlockSpec(memory_space=pltpu.SMEM)] + [vm] * 6 + [pl.BlockSpec(memory_space=pl.ANY)] * len(weights),
        out_specs=[vm, vm],
        out_shape=[jax.ShapeDtypeStruct((tok, width), F32), jax.ShapeDtypeStruct((tok, width), BF)],
        scratch_shapes=[
            pltpu.VMEM((HEADS * 128, width), BF),
            pltpu.VMEM((2 * tok, HEADS * 128), BF),
            pltpu.SemaphoreType.DMA((n_copies,)),
        ],
        compiler_params=pltpu.CompilerParams(vmem_limit_bytes=32 * 2**20),
    )(place, mine, recv, lse, lse_recv, g0, g1, *[a for a, _, _ in weights])


def lens_kernel(pos_ref, x0_ref, x1_ref, x2_ref, x3_ref, w_ref, out_ref):
    depth = x0_ref.shape[1]
    tile = 128
    for src, ref in enumerate((x0_ref, x1_ref, x2_ref, x3_ref)):
        part = src % 2

        @pl.loop(0, ref.shape[0] // tile)
        def _(m, src=src, ref=ref, part=part):
            x = ref[pl.ds(pl.multiple_of(m * tile, tile), tile), :]
            got = jnp.dot(x, w_ref[part * depth : (part + 1) * depth, :], preferred_element_type=F32)
            for g in range(tile // 8):
                at = pl.ds(pl.multiple_of(pos_ref[src, m * (tile // 8) + g] * 8, 8), 8)
                if part == 0:
                    out_ref[at, :] = got[g * 8 : (g + 1) * 8]
                else:
                    out_ref[at, :] = out_ref[at, :] + got[g * 8 : (g + 1) * 8]


def lens_matmul(pos, xs, weight):
    vm = pl.BlockSpec(memory_space=pltpu.VMEM)
    rows = 2 * xs[0].shape[0]
    return pl.pallas_call(
        lens_kernel,
        in_specs=[pl.BlockSpec(memory_space=pltpu.SMEM)] + [vm] * 5,
        out_specs=vm,
        out_shape=jax.ShapeDtypeStruct((rows, weight.shape[1]), F32),
        compiler_params=pltpu.CompilerParams(vmem_limit_bytes=40 * 2**20),
    )(pos, *xs, weight)


def short_conv(prefix, rows, taps):
    lag = taps.shape[0] - 1
    extended = jnp.concatenate([prefix, rows], 0).astype(F32)
    total = jnp.zeros(rows.shape, F32)
    for t in range(lag + 1):
        total = total + taps[t].astype(F32) * extended[lag - t : lag - t + rows.shape[0]]
    return total


def hidden_rows(resid, taps, me, last):
    lag = taps.shape[0] - 1
    count = NY * NZ * NX * NC
    names = ("y", "z", "xl", "c")
    low = lax.ppermute(resid[HALF - lag : HALF], names, [(i, i + 1) for i in range(count - 1)])
    high = lax.ppermute(resid[2 * HALF - lag :], names, [(i + 1, i) for i in range(count - 1)])
    high = jnp.where(me == last, resid[HALF - lag : HALF], high)
    conv = jnp.concatenate([short_conv(low, resid[:HALF], taps), short_conv(high, resid[HALF:], taps)], 0)
    return (resid.astype(F32) + jax.nn.silu(conv)).astype(BF)


def body(resid, conv_weight, queries, keys, values, gates, out_weight, norm_gain, lens_weight):
    y, z, xl, c = (lax.axis_index(a) for a in ("y", "z", "xl", "c"))
    me = ((y * NZ + z) * NX + xl) * NC + c
    k = xl * NC + c
    place = jnp.stack([y, z, xl, c]).astype(jnp.int32)
    swap = lambda x: shift(x, "c", 1, NC)
    cross = lambda x: shift(x, "xl", 1, NX)
    here = (0, 0, 0)
    tok = resid.shape[0]

    kv_own = jnp.concatenate([keys, values], 1)
    early = two_step((kv_own[:HALF], [(here, 0, HALF)]), "z")
    late = joined(direct((kv_own[HALF:], [(here, 0, HALF)]), "y"))
    late = ring(late, "z")
    early = direct(joined(early), "y")
    kv = [(a, False, e) for a, e in early] + [(a, True, e) for a, e in late]

    q1, q2 = swap(queries), cross(queries)
    q3 = swap(q2)

    pairs = gates.reshape(tok, HEADS, 2, 128)
    g_keep = jnp.where(c == 0, pairs[:, :, 0], pairs[:, :, 1]).reshape(tok, HEADS * 128)
    g_send = jnp.where(c == 0, pairs[:, :, 1], pairs[:, :, 0]).reshape(tok, HEADS * 128)
    g_other = swap(g_send)

    team = ("xl", "c")
    p1 = lax.ppermute(out_weight, team, [(1, 0), (2, 3)])
    p2 = lax.ppermute(out_weight, team, [(0, 2), (3, 1)])
    p3 = lax.ppermute(out_weight, team, [(1, 2), (2, 1)])
    pick = lambda a, b, d, e: jnp.where(k == 0, a, jnp.where(k == 1, b, jnp.where(k == 2, d, e)))
    w_low = pick(out_weight, p3, p2, p1)
    w_high = pick(p1, p2, p3, out_weight)
    n_low = w_low.shape[0]
    w_a = ring((w_low, [(here, 0, n_low)]), "z")
    quarter = lax.dynamic_slice_in_dim(w_high, y * (n_low // NY), n_low // NY, 0)
    w_b = joined(two_step((quarter, [(here, 0, n_low // NY)]), "z")) if False else joined(direct((quarter, [(here, 0, n_low // NY)]), "z"))
    w_b = direct(w_b, "y")
    weights = [(a, 0, e) for a, e in w_a] + [(a, n_low, e) for a, e in w_b]

    hidden = hidden_rows(resid, conv_weight, me, NY * NZ * NX * NC - 1)

    keep, send, lse = attention(place, [queries, q1, q2, q3], kv)
    mine, other, lse = join(keep, swap(send), lse, swap(lse))
    p_keep, p_send = project(place, mine, cross(other), lse, cross(lse), g_keep, g_other, weights)
    mixed = (hidden.astype(F32) + p_keep + swap(p_send).astype(F32)).astype(BF)

    lens_rows = tok // 16
    rows = mixed.reshape(lens_rows, 16, -1)[:, 15].astype(F32)
    normed = (rows * lax.rsqrt(jnp.mean(rows * rows, axis=-1, keepdims=True) + 1e-6) * norm_gain).astype(BF)
    depth = normed.shape[1] // 2
    r1 = joined(direct((normed[:, :depth], [(here, 0, lens_rows)]), "y"))
    r1 = joined(pair(r1))
    r1 = joined(ring(r1, "z"))
    r2 = joined(direct((normed[:, depth:], [(here, 0, lens_rows)]), "z"))
    r2 = joined(pair(r2))
    r2 = joined(direct(r2, "y"))
    pos = []
    for who in (c, 1 - c):
        for _, entries in (r1, r2):
            offs = jnp.array([e[0] for e in entries], jnp.int32)
            yy, zz, xx = (y + offs[:, 0]) % NY, (z + offs[:, 1]) % NZ, (xl + offs[:, 2]) % NX
            pos.append(((yy * NZ + zz) * NX + xx) * NC + who)
    logits = lens_matmul(jnp.stack(pos), [r1[0], r2[0], swap(r1[0]), swap(r2[0])], lens_weight)
    return mixed, logits


def solution(mesh):
    fine = Mesh(mesh.devices.reshape(NY, NZ, NX, NC, -1), ("y", "z", "xl", "c", "dp"))
    rows = P(("dp", "y", "z", "xl", "c"), None)
    return jax.shard_map(
        body,
        mesh=fine,
        in_specs=(rows, P(), rows, rows, rows, rows, P(("z", "xl", "c"), None), P(), P(None, ("y", "z", "xl", "c"))),
        out_specs=(rows, P("dp", ("y", "z", "xl", "c"))),
        check_vma=False,
    )
```

time: 896 us -> 286 us (0.32)
  waiting for transfers between devices: 695 us -> 69.9 us
  starting transfers between devices: 7.22 us -> 139 us
  matrix products: 51.5 us -> 0 us
  Pallas kernels: 0 us -> 44 us
  local copies, waits for them, and re-layouts: 58.9 us -> 25 us
  other arithmetic: 35.1 us -> 2.37 us
  loops' own time: 32.7 us -> 0 us
  between operations: 13.9 us -> 1.59 us
    all_gather x4 -> x0, waiting for transfers between devices: 692 us -> none  [the longest x1 264 us: body(): lax.all_gather(normed, ('ctx', 'sp'), axis=0, tiled=True)]
    ppermute x2 -> x79, starting transfers between devices: 7.07 us -> 139 us  [the longest x74 122 us: shift(): return lax.ppermute(x, axis, [(i, (i + by) % count) for i in range(count)])]
    ppermute x2 -> x79, waiting for transfers between devices: 1.08 us -> 69.9 us  [the longest x74 69.9 us: shift(): return lax.ppermute(x, axis, [(i, (i + by) % count) for i in range(count)])]
    dot_general x36 -> x0, matrix products: 51.5 us -> none  [the longest x17 27.9 us: attend_block(): lax.dot_general(key_block, query_rows, (((1,), (1,)), ((), ())), preferre...]
    pallas_call x0 -> x4, Pallas kernels: none -> 44 us  [the longest x1 26.1 us: attention(): pl.pallas_call(functools.partial(attention_kernel, layout), grid_spec=plt...]
    squeeze x16 -> x0, local copies, waits for them, and re-layouts: 34 us -> none  [run_group(): lax.dynamic_index_in_dim(value_groups, group_id, 0, keepdims=False)]
    another operation x33 -> x0, loops' own time: 32.7 us -> none  [the longest x1 31.5 us: fold_keys(): return lax.fori_loop(0, group_total, run_group, states_in)]
    unnamed x8 -> x78, local copies, waits for them, and re-layouts: 0.02 us -> 14.6 us
  transfers between devices with their start and end apart: 6 -> 79, of which waited for: 4 -> 20; matrix products, arithmetic and copies ran while one was open for 13% -> 9% of each run, Pallas kernels for 0% -> 12%
where the time goes in v1:
time: 286 us; the launch traced here: 282 us
  starting transfers between devices  139 us (49%)
  waiting for transfers between devices  69.9 us (24%)
  Pallas kernels  44 us (15%)
  local copies, waits for them, and re-layouts  25 us (9%)
    ppermute x74, starting transfers between devices, shift(): return lax.ppermute(x, axis, [(i, (i + by) % count) for i in range(count)])  122 us
    ppermute x74, waiting for transfers between devices, shift(): return lax.ppermute(x, axis, [(i, (i + by) % count) for i in range(count)])  69.9 us
    pallas_call x1, Pallas kernels, attention(): pl.pallas_call(functools.partial(attention_kernel, layout), grid_spec=plt...  26.1 us
    unnamed x78, local copies, waits for them, and re-layouts  14.6 us
    pallas_call x1, Pallas kernels, lens_matmul(): pl.pallas_call(lens_kernel, in_specs=[pl.BlockSpec(memory_space=pltpu.SME...  10.2 us
    pallas_call x1, Pallas kernels, project(): pl.pallas_call(functools.partial(project_kernel, layout), in_specs=[pl.Bl...  6.15 us
  transfers between devices with their start and end apart: 79, of which 20 were waited for; matrix products, arithmetic and copies ran while one was open for 9% of the time, Pallas kernels for 12%

profile of v1, /device:TPU:1, one launch (start us, length us, event | category | flops | bytes accessed | tf_op | source)
XLA Modules:
  0.0 281.6 jit_solution(11690545449037619631)
XLA Ops:
  2.4 2.5 collective-permute-start.5
  4.9 4.0 %collective-permute-start.6 = (bf16[64,512]{1,0:T(8,128)(2,1)S(1)}, bf16[64,512]{1,0:T(8,128)(2,1)S(1)}, u32[]{:S(2)}, u32[]{:S(2)}) collective-permute-start(bf16[64,512]{1,0:T(8,128)(2,1)S(1)} %get-tuple-element.36), channel_id=1, source_target_pairs={{0,56},{8,0},{16,8},{24,16},{32,24},{40,32},{48,40},{56,48},{1,57}... | collective-permute-start | bytes 196616 | tf_op jit(solution)/shard_map/ppermute | solution.py:26
  9.0 1.3 collective-permute-start.16
  10.3 2.6 collective-permute-start.17
  14.7 1.9 fusion.26
  16.7 1.4 reshape.643
  18.1 1.7 fusion.27
  19.9 3.6 %collective-permute-start.8 = (bf16[64,512]{1,0:T(8,128)(2,1)S(1)}, bf16[64,512]{1,0:T(8,128)(2,1)S(1)}, u32[]{:S(2)}, u32[]{:S(2)}) collective-permute-start(bf16[64,512]{1,0:T(8,128)(2,1)S(1)} %get-tuple-element.36), channel_id=1, source_target_pairs={{0,48},{8,56},{16,0},{24,8},{32,16},{40,24},{48,32},{56,40},{1,49}... | collective-permute-start | bytes 196616 | tf_op jit(solution)/shard_map/ppermute | solution.py:26
  23.5 5.3 %collective-permute-start.32 = (bf16[64,2048]{1,0:T(8,128)(2,1)S(1)}, bf16[64,2048]{1,0:T(8,128)(2,1)S(1)}, u32[]{:S(2)}, u32[]{:S(2)}) collective-permute-start(bf16[64,2048]{1,0:T(8,128)(2,1)S(1)} %copy-done.12), channel_id=1, source_target_pairs={{2,4},{4,2},{3,5},{5,3},{10,12},{12,10},{11,13},{13,11},{18,20},{2... | collective-permute-start | bytes 786440 | tf_op jit(solution)/shard_map/ppermute | solution.py:401
  29.0 2.6 collective-permute-start.20
  31.8 2.2 collective-permute-start.9
  34.0 4.6 %collective-permute-done.11 = bf16[32,512]{1,0:T(8,128)(2,1)S(1)} collective-permute-done((bf16[32,512]{1,0:T(8,128)(2,1)S(1)}, bf16[32,512]{1,0:T(8,128)(2,1)S(1)}, u32[]{:S(2)}, u32[]{:S(2)}) %collective-permute-start.11) | collective-permute-done | bytes 32800 | tf_op jit(solution)/shard_map/ppermute | solution.py:26
  38.9 2.3 collective-permute-done.9
  41.2 1.3 collective-permute-start.33
  42.6 3.4 %collective-permute-start.34 = (bf16[64,2048]{1,0:T(8,128)(2,1)S(1)}, bf16[64,2048]{1,0:T(8,128)(2,1)S(1)}, u32[]{:S(2)}, u32[]{:S(2)}) collective-permute-start(bf16[64,2048]{1,0:T(8,128)(2,1)S(1)} %copy-done.12), channel_id=1, source_target_pairs={{2,0},{4,6},{3,1},{5,7},{10,8},{12,14},{11,9},{13,15},{18,16},{20,... | collective-permute-start | bytes 786440 | tf_op jit(solution)/shard_map/ppermute | solution.py:399
  46.1 1.8 collective-permute-start.21
  47.9 1.2 collective-permute-start.22
  49.2 2.2 collective-permute-start.12
  51.4 3.9 %collective-permute-done.21.refs_11_ = bf16[256,512]{1,0:T(8,128)(2,1)S(1)} collective-permute-done((bf16[256,512]{1,0:T(8,128)(2,1)S(1)}, bf16[256,512]{1,0:T(8,128)(2,1)S(1)}, u32[]{:S(2)}, u32[]{:S(2)}) %collective-permute-start.21) | collective-permute-done | bytes 262176 | tf_op jit(solution)/shard_map/ppermute | solution.py:26
  57.0 1.4 collective-permute-start.24
  58.6 2.5 collective-permute-start.44
  61.1 5.7 %collective-permute-done.43 = bf16[16,2048]{1,0:T(8,128)(2,1)S(1)} collective-permute-done((bf16[16,2048]{1,0:T(8,128)(2,1)S(1)}, bf16[16,2048]{1,0:T(8,128)(2,1)S(1)}, u32[]{:S(2)}, u32[]{:S(2)}) %collective-permute-start.43) | collective-permute-done | bytes 65568 | tf_op jit(solution)/shard_map/ppermute | solution.py:26
  66.8 2.0 collective-permute-start.2
  69.8 1.9 collective-permute-start.15
  72.4 1.9 collective-permute-start.25
  74.2 20.6 %collective-permute-done.13.refs_5_ = bf16[512,512]{1,0:T(8,128)(2,1)S(1)} collective-permute-done((bf16[512,512]{1,0:T(8,128)(2,1)S(1)}, bf16[512,512]{1,0:T(8,128)(2,1)S(1)}, u32[]{:S(2)}, u32[]{:S(2)}) %collective-permute-start.13) | collective-permute-done | bytes 524320 | tf_op jit(solution)/shard_map/ppermute | solution.py:26
  94.8 2.9 %collective-permute-start.1 = (bf16[3,2048]{1,0:T(4,128)(2,1)S(1)}, bf16[3,2048]{1,0:T(4,128)(2,1)S(1)}, u32[]{:S(2)}, u32[]{:S(2)}) collective-permute-start(bf16[3,2048]{1,0:T(4,128)(2,1)S(1)} %slice.146), channel_id=1, source_target_pairs={{2,0},{4,2},{6,4},{8,6},{10,8},{12,10},{14,12},{16,14},{18,16},{20... | collective-permute-start | bytes 36872 | tf_op jit(solution)/shard_map/ppermute | solution.py:367
  98.5 3.2 %collective-permute-start.46 = (bf16[16,2048]{1,0:T(8,128)(2,1)S(1)}, bf16[16,2048]{1,0:T(8,128)(2,1)S(1)}, u32[]{:S(2)}, u32[]{:S(2)}) collective-permute-start(bf16[16,2048]{1,0:T(8,128)(2,1)S(1)} %get-tuple-element.23), channel_id=1, source_target_pairs={{0,32},{8,40},{16,48},{24,56},{32,0},{40,8},{48,16},{56,24},{1,33}... | collective-permute-start | bytes 196616 | tf_op jit(solution)/shard_map/ppermute | solution.py:26
  101.7 1.8 collective-permute-start.35
  103.5 11.3 %collective-permute-start.36 = (bf16[64,2048]{1,0:T(8,128)(2,1)S(1)}, bf16[64,2048]{1,0:T(8,128)(2,1)S(1)}, u32[]{:S(2)}, u32[]{:S(2)}) collective-permute-start(bf16[64,2048]{1,0:T(8,128)(2,1)S(1)} %select_select_fusion.refs_0_), channel_id=1, source_target_pairs={{0,56},{8,0},{16,8},{24,16},{32,24},{40,32},{48,40},{56,48},{1,57}... | collective-permute-start | bytes 786440 | tf_op jit(solution)/shard_map/ppermute | solution.py:26
  114.8 26.1 %shard_map.140 = (bf16[4,128,1024]{2,1,0:T(8,128)(2,1)S(1)}, bf16[4,128,1024]{2,1,0:T(8,128)(2,1)S(1)}, f32[2,8,256]{2,1,0:T(8,128)S(1)}) custom-call(s32[4]{0:T(128)S(1)} %pad_add_fusion.1.place, bf16[128,2048]{1,0:T(8,128)(2,1)S(1)} %copy-done.5, bf16[128,2048]{1,0:T(8,128)(2,1)S(1)} %collective-permute-done.2.refs_1_, ...), custom_call_target="tpu_custom_call" | custom-call | flops 10000000000 | bytes 8388608 | tf_op jit(solution)/shard_map/pallas_call | solution.py:186
  141.9 1.8 collective-permute-start.47
  143.7 5.6 %collective-permute-done.47 = bf16[16,2048]{1,0:T(8,128)(2,1)S(1)} collective-permute-done((bf16[16,2048]{1,0:T(8,128)(2,1)S(1)}, bf16[16,2048]{1,0:T(8,128)(2,1)S(1)}, u32[]{:S(2)}, u32[]{:S(2)}) %collective-permute-start.47) | collective-permute-done | bytes 65568 | tf_op jit(solution)/shard_map/ppermute | solution.py:26
  149.3 1.9 collective-permute-start.48
  151.2 3.0 %collective-permute-start.37 = (bf16[64,2048]{1,0:T(8,128)(2,1)S(1)}, bf16[64,2048]{1,0:T(8,128)(2,1)}, u32[]{:S(2)}, u32[]{:S(2)}) collective-permute-start(bf16[64,2048]{1,0:T(8,128)(2,1)S(1)} %collective-permute-done.35.refs_1_), channel_id=1, source_target_pairs={{0,8},{8,16},{16,24},{24,32},{32,40},{40,48},{48,56},{56,0},{1,9},... | collective-permute-start | bytes 786440 | tf_op jit(solution)/shard_map/ppermute | solution.py:26
  155.2 3.8 %collective-permute-start.49 = (bf16[16,2048]{1,0:T(8,128)(2,1)S(1)}, bf16[16,2048]{1,0:T(8,128)(2,1)S(1)}, u32[]{:S(2)}, u32[]{:S(2)}) collective-permute-start(bf16[16,2048]{1,0:T(8,128)(2,1)S(1)} %get-tuple-element.23), channel_id=1, source_target_pairs={{0,56},{8,0},{16,8},{24,16},{32,24},{40,32},{48,40},{56,48},{1,57}... | collective-permute-start | bytes 196616 | tf_op jit(solution)/shard_map/ppermute | solution.py:26
  159.1 2.3 collective-permute-start.39
  161.7 2.2 collective-permute-start.40
  163.9 3.4 %collective-permute-start.28 = (f32[2,8,256]{2,1,0:T(8,128)S(1)}, f32[2,8,256]{2,1,0:T(8,128)S(1)}, u32[]{:S(2)}, u32[]{:S(2)}) collective-permute-start(f32[2,8,256]{2,1,0:T(8,128)S(1)} %get-tuple-element.12.lse_ref), channel_id=1, source_target_pairs={{0,2},{2,0},{1,3},{3,1},{4,6},{6,4},{5,7},{7,5},{8,10},{10,8},{9,1... | collective-permute-start | bytes 49160 | tf_op jit(solution)/shard_map/ppermute | solution.py:26
  168.5 2.1 collective-permute-start.52
  171.6 1.6 shard_map.141
  175.5 3.6 %collective-permute-start = (bf16[3,2048]{1,0:T(4,128)(2,1)S(1)}, bf16[3,2048]{1,0:T(4,128)(2,1)S(1)}, u32[]{:S(2)}, u32[]{:S(2)}) collective-permute-start(bf16[3,2048]{1,0:T(4,128)(2,1)S(1)} %get-tuple-element.26), channel_id=1, source_target_pairs={{0,2},{2,4},{4,6},{6,8},{8,10},{10,12},{12,14},{14,16},{16,18},{18... | collective-permute-start | bytes 36872 | tf_op jit(solution)/shard_map/ppermute | solution.py:366
  179.2 14.8 %collective-permute-done.50.refs_10_ = bf16[128,2048]{1,0:T(8,128)(2,1)} collective-permute-done((bf16[128,2048]{1,0:T(8,128)(2,1)S(1)}, bf16[128,2048]{1,0:T(8,128)(2,1)}, u32[]{:S(2)}, u32[]{:S(2)}) %collective-permute-start.50) | collective-permute-done | bytes 524320 | tf_op jit(solution)/shard_map/ppermute | solution.py:26
  193.9 2.7 collective-permute-start.42
  196.7 2.7 collective-permute-done.41.refs_7_
  199.5 6.2 %shard_map.142 = (f32[128,2048]{1,0:T(8,128)S(1)}, bf16[128,2048]{1,0:T(8,128)(2,1)S(1)}) custom-call(s32[4]{0:T(128)S(1)} %pad_add_fusion.1.place, bf16[2,128,1024]{2,1,0:T(8,128)(2,1)S(1)} %get-tuple-element.13.mine_ref, bf16[2,128,1024]{2,1,0:T(8,128)(2,1)S(1)} %collective-permute-done.29.recv_ref, f32[2,8,256]{2,1,0:T(8,128)S(1)} %get-tuple-element.15.lse_ref, ...), custom_call_target="tpu_custom_call" | custom-call | tf_op jit(solution)/shard_map/pallas_call | solution.py:309
  205.7 2.3 collective-permute-start.53
  210.9 1.7 collective-permute-start.67
  212.6 1.2 collective-permute-start.68
  213.9 2.9 %collective-permute-start.69 = (bf16[8,1024]{1,0:T(8,128)(2,1)S(1)}, bf16[8,1024]{1,0:T(8,128)(2,1)S(1)}, u32[]{:S(2)}, u32[]{:S(2)}) collective-permute-start(bf16[8,1024]{1,0:T(8,128)(2,1)S(1)} %get-tuple-element.44), channel_id=1, source_target_pairs={{0,32},{8,40},{16,48},{24,56},{32,0},{40,8},{48,16},{56,24},{1,33}... | collective-permute-start | bytes 49160 | tf_op jit(solution)/shard_map/ppermute | solution.py:26
  216.8 4.2 %collective-permute-start.70 = (bf16[8,1024]{1,0:T(8,128)(2,1)S(1)}, bf16[8,1024]{1,0:T(8,128)(2,1)S(1)}, u32[]{:S(2)}, u32[]{:S(2)}) collective-permute-start(bf16[8,1024]{1,0:T(8,128)(2,1)S(1)} %get-tuple-element.44), channel_id=1, source_target_pairs={{0,40},{8,48},{16,56},{24,0},{32,8},{40,16},{48,24},{56,32},{1,41}... | collective-permute-start | bytes 49160 | tf_op jit(solution)/shard_map/ppermute | solution.py:26
  221.6 1.2 collective-permute-start.72
  225.4 2.0 collective-permute-start.56
  232.6 1.1 collective-permute-done.57
  234.5 2.5 collective-permute-start.59
  238.2 1.8 collective-permute-start.75
  240.0 2.1 collective-permute-start.76
  242.8 2.7 collective-permute-start.61
  246.1 1.3 collective-permute-done.60
  248.1 2.9 %collective-permute-start.63 = (bf16[64,1024]{1,0:T(8,128)(2,1)S(1)}, bf16[64,1024]{1,0:T(8,128)(2,1)S(1)}, u32[]{:S(2)}, u32[]{:S(2)}) collective-permute-start(bf16[64,1024]{1,0:T(8,128)(2,1)S(1)} %collective-permute-done.61), channel_id=1, source_target_pairs={{0,56},{8,0},{16,8},{24,16},{32,24},{40,32},{48,40},{56,48},{1,57}... | collective-permute-start | bytes 393224 | tf_op jit(solution)/shard_map/ppermute | solution.py:26
  253.9 7.7 %collective-permute-start.78 = (bf16[512,1024]{1,0:T(8,128)(2,1)}, bf16[512,1024]{1,0:T(8,128)(2,1)}, u32[]{:S(2)}, u32[]{:S(2)}) collective-permute-start(bf16[512,1024]{1,0:T(8,128)(2,1)} %constant_dynamic-update-slice_fusion.54.x1_ref), channel_id=1, source_target_pairs={{0,2},{2,0},{1,3},{3,1},{4,6},{6,4},{5,7},{7,5},{8,10},{10,8},{9,1... | collective-permute-start | bytes 3145736 | tf_op jit(solution)/shard_map/ppermute | solution.py:26
  261.7 2.7 collective-permute-start.65
  268.7 2.5 collective-permute-done.77.x2_ref
  271.2 10.2 %shard_map.143 = f32[1024,640]{1,0:T(8,128)} custom-call(s32[4,64]{1,0:T(4,128)S(1)} %pad_add_fusion.pos_ref, bf16[512,1024]{1,0:T(8,128)(2,1)} %constant_dynamic-update-slice_fusion.24.x0_ref, bf16[512,1024]{1,0:T(8,128)(2,1)} %constant_dynamic-update-slice_fusion.54.x1_ref, bf16[512,1024]{1,0:T(8,128)(2,1)} %collective-permute-done.77.x2_ref, ...), custom_call_target="tpu_custom_call" | custom-call | tf_op jit(solution)/shard_map/pallas_call | solution.py:344
  (216 shorter events, 38.4 us)
Async XLA Ops:
  2.4 26.6 %collective-permute-start.5 = (bf16[64,512]{1,0:T(8,128)(2,1)S(1)}, bf16[64,512]{1,0:T(8,128)(2,1)S(1)}, u32[]{:S(2)}, u32[]{:S(2)}) collective-permute-start(bf16[64,512]{1,0:T(8,128)(2,1)S(1)} %get-tuple-element.36), channel_id=1, source_target_pairs={{0,8},{8,16},{16,24},{24,32},{32,40},{40,48},{48,56},{56,0},{1,9},... | collective-permute-start | bytes 196616 | tf_op jit(solution)/shard_map/ppermute | solution.py:26
  4.9 26.7 %collective-permute-start.6 = (bf16[64,512]{1,0:T(8,128)(2,1)S(1)}, bf16[64,512]{1,0:T(8,128)(2,1)S(1)}, u32[]{:S(2)}, u32[]{:S(2)}) collective-permute-start(bf16[64,512]{1,0:T(8,128)(2,1)S(1)} %get-tuple-element.36), channel_id=1, source_target_pairs={{0,56},{8,0},{16,8},{24,16},{32,24},{40,32},{48,40},{56,48},{1,57}... | collective-permute-start | bytes 196616 | tf_op jit(solution)/shard_map/ppermute | solution.py:26
  9.0 10.9 %collective-permute-start.16 = (bf16[64,512]{1,0:T(8,128)(2,1)S(1)}, bf16[64,512]{1,0:T(8,128)(2,1)S(1)}, u32[]{:S(2)}, u32[]{:S(2)}) collective-permute-start(bf16[64,512]{1,0:T(8,128)(2,1)S(1)} %get-tuple-element.34), channel_id=1, source_target_pairs={{0,64},{64,128},{128,192},{192,0},{1,65},{65,129},{129,193},{193,1... | collective-permute-start | bytes 196616 | tf_op jit(solution)/shard_map/ppermute | solution.py:26
  10.3 9.7 %collective-permute-start.17 = (bf16[64,512]{1,0:T(8,128)(2,1)S(1)}, bf16[64,512]{1,0:T(8,128)(2,1)S(1)}, u32[]{:S(2)}, u32[]{:S(2)}) collective-permute-start(bf16[64,512]{1,0:T(8,128)(2,1)S(1)} %get-tuple-element.34), channel_id=1, source_target_pairs={{0,128},{64,192},{128,0},{192,64},{1,129},{65,193},{129,1},{193,65... | collective-permute-start | bytes 196616 | tf_op jit(solution)/shard_map/ppermute | solution.py:26
  12.9 10.6 %collective-permute-start.18 = (bf16[64,512]{1,0:T(8,128)(2,1)S(1)}, bf16[64,512]{1,0:T(8,128)(2,1)S(1)}, u32[]{:S(2)}, u32[]{:S(2)}) collective-permute-start(bf16[64,512]{1,0:T(8,128)(2,1)S(1)} %get-tuple-element.34), channel_id=1, source_target_pairs={{0,192},{64,0},{128,64},{192,128},{1,193},{65,1},{129,65},{193,129... | collective-permute-start | bytes 196616 | tf_op jit(solution)/shard_map/ppermute | solution.py:26
  19.9 9.0 %collective-permute-start.7 = (bf16[64,512]{1,0:T(8,128)(2,1)S(1)}, bf16[64,512]{1,0:T(8,128)(2,1)S(1)}, u32[]{:S(2)}, u32[]{:S(2)}) collective-permute-start(bf16[64,512]{1,0:T(8,128)(2,1)S(1)} %get-tuple-element.36), channel_id=1, source_target_pairs={{0,16},{8,24},{16,32},{24,40},{32,48},{40,56},{48,0},{56,8},{1,17}... | collective-permute-start | bytes 196616 | tf_op jit(solution)/shard_map/ppermute | solution.py:26
  19.9 11.9 %collective-permute-start.8 = (bf16[64,512]{1,0:T(8,128)(2,1)S(1)}, bf16[64,512]{1,0:T(8,128)(2,1)S(1)}, u32[]{:S(2)}, u32[]{:S(2)}) collective-permute-start(bf16[64,512]{1,0:T(8,128)(2,1)S(1)} %get-tuple-element.36), channel_id=1, source_target_pairs={{0,48},{8,56},{16,0},{24,8},{32,16},{40,24},{48,32},{56,40},{1,49}... | collective-permute-start | bytes 196616 | tf_op jit(solution)/shard_map/ppermute | solution.py:26
  23.5 25.6 %collective-permute-start.32 = (bf16[64,2048]{1,0:T(8,128)(2,1)S(1)}, bf16[64,2048]{1,0:T(8,128)(2,1)S(1)}, u32[]{:S(2)}, u32[]{:S(2)}) collective-permute-start(bf16[64,2048]{1,0:T(8,128)(2,1)S(1)} %copy-done.12), channel_id=1, source_target_pairs={{2,4},{4,2},{3,5},{5,3},{10,12},{12,10},{11,13},{13,11},{18,20},{2... | collective-permute-start | bytes 786440 | tf_op jit(solution)/shard_map/ppermute | solution.py:401
  28.9 17.2 %collective-permute-start.19 = (bf16[256,512]{1,0:T(8,128)(2,1)S(1)}, bf16[256,512]{1,0:T(8,128)(2,1)S(1)}, u32[]{:S(2)}, u32[]{:S(2)}) collective-permute-start(bf16[256,512]{1,0:T(8,128)(2,1)S(1)} %pad_maximum_fusion.1.refs_8_), channel_id=1, source_target_pairs={{0,8},{8,16},{16,24},{24,32},{32,40},{40,48},{48,56},{56,0},{1,9},... | collective-permute-start | bytes 786440 | tf_op jit(solution)/shard_map/ppermute | solution.py:26
  29.0 18.9 %collective-permute-start.20 = (bf16[256,512]{1,0:T(8,128)(2,1)S(1)}, bf16[256,512]{1,0:T(8,128)(2,1)S(1)}, u32[]{:S(2)}, u32[]{:S(2)}) collective-permute-start(bf16[256,512]{1,0:T(8,128)(2,1)S(1)} %pad_maximum_fusion.1.refs_8_), channel_id=1, source_target_pairs={{0,56},{8,0},{16,8},{24,16},{32,24},{40,32},{48,40},{56,48},{1,57}... | collective-permute-start | bytes 786440 | tf_op jit(solution)/shard_map/ppermute | solution.py:26
  31.7 6.9 %collective-permute-start.11 = (bf16[32,512]{1,0:T(8,128)(2,1)S(1)}, bf16[32,512]{1,0:T(8,128)(2,1)S(1)}, u32[]{:S(2)}, u32[]{:S(2)}) collective-permute-start(bf16[32,512]{1,0:T(8,128)(2,1)S(1)} %slice.188), channel_id=1, source_target_pairs={{0,16},{8,24},{16,32},{24,40},{32,48},{40,56},{48,0},{56,8},{1,17}... | collective-permute-start | bytes 98312 | tf_op jit(solution)/shard_map/ppermute | solution.py:26
  31.8 9.4 %collective-permute-start.9 = (bf16[64,512]{1,0:T(8,128)(2,1)S(1)}, bf16[64,512]{1,0:T(8,128)(2,1)S(1)}, u32[]{:S(2)}, u32[]{:S(2)}) collective-permute-start(bf16[64,512]{1,0:T(8,128)(2,1)S(1)} %collective-permute-done.7), channel_id=1, source_target_pairs={{0,8},{8,16},{16,24},{24,32},{32,40},{40,48},{48,56},{56,0},{1,9},... | collective-permute-start | bytes 196616 | tf_op jit(solution)/shard_map/ppermute | solution.py:26
  41.2 8.0 %collective-permute-start.33 = (bf16[64,2048]{1,0:T(8,128)(2,1)S(1)}, bf16[64,2048]{1,0:T(8,128)(2,1)S(1)}, u32[]{:S(2)}, u32[]{:S(2)}) collective-permute-start(bf16[64,2048]{1,0:T(8,128)(2,1)S(1)} %copy-done.12), channel_id=1, source_target_pairs={{0,4},{6,2},{1,5},{7,3},{8,12},{14,10},{9,13},{15,11},{16,20},{22,... | collective-permute-start | bytes 786440 | tf_op jit(solution)/shard_map/ppermute | solution.py:400
  42.6 15.8 %collective-permute-start.34 = (bf16[64,2048]{1,0:T(8,128)(2,1)S(1)}, bf16[64,2048]{1,0:T(8,128)(2,1)S(1)}, u32[]{:S(2)}, u32[]{:S(2)}) collective-permute-start(bf16[64,2048]{1,0:T(8,128)(2,1)S(1)} %copy-done.12), channel_id=1, source_target_pairs={{2,0},{4,6},{3,1},{5,7},{10,8},{12,14},{11,9},{13,15},{18,16},{20,... | collective-permute-start | bytes 786440 | tf_op jit(solution)/shard_map/ppermute | solution.py:399
  46.1 9.3 %collective-permute-start.21 = (bf16[256,512]{1,0:T(8,128)(2,1)S(1)}, bf16[256,512]{1,0:T(8,128)(2,1)S(1)}, u32[]{:S(2)}, u32[]{:S(2)}) collective-permute-start(bf16[256,512]{1,0:T(8,128)(2,1)S(1)} %collective-permute-done.19.refs_9_), channel_id=1, source_target_pairs={{0,8},{8,16},{16,24},{24,32},{32,40},{40,48},{48,56},{56,0},{1,9},... | collective-permute-start | bytes 786440 | tf_op jit(solution)/shard_map/ppermute | solution.py:26
  47.9 9.1 %collective-permute-start.22 = (bf16[256,512]{1,0:T(8,128)(2,1)S(1)}, bf16[256,512]{1,0:T(8,128)(2,1)S(1)}, u32[]{:S(2)}, u32[]{:S(2)}) collective-permute-start(bf16[256,512]{1,0:T(8,128)(2,1)S(1)} %collective-permute-done.20.refs_10_), channel_id=1, source_target_pairs={{0,56},{8,0},{16,8},{24,16},{32,24},{40,32},{48,40},{56,48},{1,57}... | collective-permute-start | bytes 786440 | tf_op jit(solution)/shard_map/ppermute | solution.py:26
  49.1 20.1 %collective-permute-start.3 = (bf16[128,2048]{1,0:T(8,128)(2,1)S(1)}, bf16[128,2048]{1,0:T(8,128)(2,1)S(1)}, u32[]{:S(2)}, u32[]{:S(2)}) collective-permute-start(bf16[128,2048]{1,0:T(8,128)(2,1)S(1)} %copy-done.5), channel_id=1, source_target_pairs={{0,4},{4,0},{1,5},{5,1},{2,6},{6,2},{3,7},{7,3},{8,12},{12,8},{9,1... | collective-permute-start | bytes 1572872 | tf_op jit(solution)/shard_map/ppermute | solution.py:26
  49.2 9.4 %collective-permute-start.12 = (bf16[32,512]{1,0:T(8,128)(2,1)S(1)}, bf16[32,512]{1,0:T(8,128)(2,1)S(1)}, u32[]{:S(2)}, u32[]{:S(2)}) collective-permute-start(bf16[32,512]{1,0:T(8,128)(2,1)S(1)} %slice.189), channel_id=1, source_target_pairs={{0,48},{8,56},{16,0},{24,8},{32,16},{40,24},{48,32},{56,40},{1,49}... | collective-permute-start | bytes 98312 | tf_op jit(solution)/shard_map/ppermute | solution.py:26
  55.3 14.5 %collective-permute-start.23 = (bf16[256,512]{1,0:T(8,128)(2,1)S(1)}, bf16[256,512]{1,0:T(8,128)(2,1)S(1)}, u32[]{:S(2)}, u32[]{:S(2)}) collective-permute-start(bf16[256,512]{1,0:T(8,128)(2,1)S(1)} %collective-permute-done.21.refs_11_), channel_id=1, source_target_pairs={{0,8},{8,16},{16,24},{24,32},{32,40},{40,48},{48,56},{56,0},{1,9},... | collective-permute-start | bytes 786440 | tf_op jit(solution)/shard_map/ppermute | solution.py:26
  57.0 14.6 %collective-permute-start.24 = (bf16[256,512]{1,0:T(8,128)(2,1)S(1)}, bf16[256,512]{1,0:T(8,128)(2,1)S(1)}, u32[]{:S(2)}, u32[]{:S(2)}) collective-permute-start(bf16[256,512]{1,0:T(8,128)(2,1)S(1)} %collective-permute-done.22.refs_12_), channel_id=1, source_target_pairs={{0,56},{8,0},{16,8},{24,16},{32,24},{40,32},{48,40},{56,48},{1,57}... | collective-permute-start | bytes 786440 | tf_op jit(solution)/shard_map/ppermute | solution.py:26
  58.5 8.3 %collective-permute-start.43 = (bf16[16,2048]{1,0:T(8,128)(2,1)S(1)}, bf16[16,2048]{1,0:T(8,128)(2,1)S(1)}, u32[]{:S(2)}, u32[]{:S(2)}) collective-permute-start(bf16[16,2048]{1,0:T(8,128)(2,1)S(1)} %get-tuple-element.23), channel_id=1, source_target_pairs={{0,8},{8,16},{16,24},{24,32},{32,40},{40,48},{48,56},{56,0},{1,9},... | collective-permute-start | bytes 196616 | tf_op jit(solution)/shard_map/ppermute | solution.py:26
  58.6 10.2 %collective-permute-start.44 = (bf16[16,2048]{1,0:T(8,128)(2,1)S(1)}, bf16[16,2048]{1,0:T(8,128)(2,1)S(1)}, u32[]{:S(2)}, u32[]{:S(2)}) collective-permute-start(bf16[16,2048]{1,0:T(8,128)(2,1)S(1)} %get-tuple-element.23), channel_id=1, source_target_pairs={{0,16},{8,24},{16,32},{24,40},{32,48},{40,56},{48,0},{56,8},{1,17}... | collective-permute-start | bytes 196616 | tf_op jit(solution)/shard_map/ppermute | solution.py:26
  68.8 26.0 %collective-permute-start.13 = (bf16[512,512]{1,0:T(8,128)(2,1)S(1)}, bf16[512,512]{1,0:T(8,128)(2,1)S(1)}, u32[]{:S(2)}, u32[]{:S(2)}) collective-permute-start(bf16[512,512]{1,0:T(8,128)(2,1)S(1)} %constant_dynamic-update-slice_fusion.2.refs_4_), channel_id=1, source_target_pairs={{0,64},{64,128},{128,192},{192,0},{1,65},{65,129},{129,193},{193,1... | collective-permute-start | bytes 1572872 | tf_op jit(solution)/shard_map/ppermute | solution.py:26
  69.2 25.6 %collective-permute-start.14 = (bf16[512,512]{1,0:T(8,128)(2,1)S(1)}, bf16[512,512]{1,0:T(8,128)(2,1)S(1)}, u32[]{:S(2)}, u32[]{:S(2)}) collective-permute-start(bf16[512,512]{1,0:T(8,128)(2,1)S(1)} %constant_dynamic-update-slice_fusion.2.refs_4_), channel_id=1, source_target_pairs={{0,128},{64,192},{128,0},{192,64},{1,129},{65,193},{129,1},{193,65... | collective-permute-start | bytes 1572872 | tf_op jit(solution)/shard_map/ppermute | solution.py:26
  69.8 27.9 %collective-permute-start.15 = (bf16[512,512]{1,0:T(8,128)(2,1)S(1)}, bf16[512,512]{1,0:T(8,128)(2,1)S(1)}, u32[]{:S(2)}, u32[]{:S(2)}) collective-permute-start(bf16[512,512]{1,0:T(8,128)(2,1)S(1)} %constant_dynamic-update-slice_fusion.2.refs_4_), channel_id=1, source_target_pairs={{0,192},{64,0},{128,64},{192,128},{1,193},{65,1},{129,65},{193,129... | collective-permute-start | bytes 1572872 | tf_op jit(solution)/shard_map/ppermute | solution.py:26
  71.7 31.8 %collective-permute-start.4 = (bf16[128,2048]{1,0:T(8,128)(2,1)S(1)}, bf16[128,2048]{1,0:T(8,128)(2,1)S(1)}, u32[]{:S(2)}, u32[]{:S(2)}) collective-permute-start(bf16[128,2048]{1,0:T(8,128)(2,1)S(1)} %collective-permute-done.3.refs_2_), channel_id=1, source_target_pairs={{0,2},{2,0},{1,3},{3,1},{4,6},{6,4},{5,7},{7,5},{8,10},{10,8},{9,1... | collective-permute-start | bytes 1572872 | tf_op jit(solution)/shard_map/ppermute | solution.py:26
  72.4 26.1 %collective-permute-start.25 = (bf16[128,512]{1,0:T(8,128)(2,1)S(1)}, bf16[128,512]{1,0:T(8,128)(2,1)S(1)}, u32[]{:S(2)}, u32[]{:S(2)}) collective-permute-start(bf16[128,512]{1,0:T(8,128)(2,1)S(1)} %slice.191), channel_id=1, source_target_pairs={{0,8},{8,16},{16,24},{24,32},{32,40},{40,48},{48,56},{56,0},{1,9},... | collective-permute-start | bytes 393224 | tf_op jit(solution)/shard_map/ppermute | solution.py:26
  94.8 6.9 %collective-permute-start.26 = (bf16[128,512]{1,0:T(8,128)(2,1)S(1)}, bf16[128,512]{1,0:T(8,128)(2,1)S(1)}, u32[]{:S(2)}, u32[]{:S(2)}) collective-permute-start(bf16[128,512]{1,0:T(8,128)(2,1)S(1)} %slice.192), channel_id=1, source_target_pairs={{0,56},{8,0},{16,8},{24,16},{32,24},{40,32},{48,40},{56,48},{1,57}... | collective-permute-start | bytes 393224 | tf_op jit(solution)/shard_map/ppermute | solution.py:26
  94.8 72.5 %collective-permute-start.1 = (bf16[3,2048]{1,0:T(4,128)(2,1)S(1)}, bf16[3,2048]{1,0:T(4,128)(2,1)S(1)}, u32[]{:S(2)}, u32[]{:S(2)}) collective-permute-start(bf16[3,2048]{1,0:T(4,128)(2,1)S(1)} %slice.146), channel_id=1, source_target_pairs={{2,0},{4,2},{6,4},{8,6},{10,8},{12,10},{14,12},{16,14},{18,16},{20... | collective-permute-start | bytes 36872 | tf_op jit(solution)/shard_map/ppermute | solution.py:367
  97.7 43.2 %collective-permute-start.45 = (bf16[16,2048]{1,0:T(8,128)(2,1)S(1)}, bf16[16,2048]{1,0:T(8,128)(2,1)S(1)}, u32[]{:S(2)}, u32[]{:S(2)}) collective-permute-start(bf16[16,2048]{1,0:T(8,128)(2,1)S(1)} %get-tuple-element.23), channel_id=1, source_target_pairs={{0,24},{8,32},{16,40},{24,48},{32,56},{40,0},{48,8},{56,16},{1,25}... | collective-permute-start | bytes 196616 | tf_op jit(solution)/shard_map/ppermute | solution.py:26
  98.5 43.4 %collective-permute-start.46 = (bf16[16,2048]{1,0:T(8,128)(2,1)S(1)}, bf16[16,2048]{1,0:T(8,128)(2,1)S(1)}, u32[]{:S(2)}, u32[]{:S(2)}) collective-permute-start(bf16[16,2048]{1,0:T(8,128)(2,1)S(1)} %get-tuple-element.23), channel_id=1, source_target_pairs={{0,32},{8,40},{16,48},{24,56},{32,0},{40,8},{48,16},{56,24},{1,33}... | collective-permute-start | bytes 196616 | tf_op jit(solution)/shard_map/ppermute | solution.py:26
  101.7 49.5 %collective-permute-start.35 = (bf16[64,2048]{1,0:T(8,128)(2,1)S(1)}, bf16[64,2048]{1,0:T(8,128)(2,1)S(1)}, u32[]{:S(2)}, u32[]{:S(2)}) collective-permute-start(bf16[64,2048]{1,0:T(8,128)(2,1)S(1)} %select_select_fusion.refs_0_), channel_id=1, source_target_pairs={{0,8},{8,16},{16,24},{24,32},{32,40},{40,48},{48,56},{56,0},{1,9},... | collective-permute-start | bytes 786440 | tf_op jit(solution)/shard_map/ppermute | solution.py:26
  103.5 50.7 %collective-permute-start.36 = (bf16[64,2048]{1,0:T(8,128)(2,1)S(1)}, bf16[64,2048]{1,0:T(8,128)(2,1)S(1)}, u32[]{:S(2)}, u32[]{:S(2)}) collective-permute-start(bf16[64,2048]{1,0:T(8,128)(2,1)S(1)} %select_select_fusion.refs_0_), channel_id=1, source_target_pairs={{0,56},{8,0},{16,8},{24,16},{32,24},{40,32},{48,40},{56,48},{1,57}... | collective-permute-start | bytes 786440 | tf_op jit(solution)/shard_map/ppermute | solution.py:26
  140.9 27.6 %collective-permute-start.27 = (bf16[4,128,1024]{2,1,0:T(8,128)(2,1)S(1)}, bf16[4,128,1024]{2,1,0:T(8,128)(2,1)S(1)}, u32[]{:S(2)}, u32[]{:S(2)}) collective-permute-start(bf16[4,128,1024]{2,1,0:T(8,128)(2,1)S(1)} %get-tuple-element.11), channel_id=1, source_target_pairs={{0,2},{2,0},{1,3},{3,1},{4,6},{6,4},{5,7},{7,5},{8,10},{10,8},{9,1... | collective-permute-start | bytes 3145736 | tf_op jit(solution)/shard_map/ppermute | solution.py:26
  141.9 7.4 %collective-permute-start.47 = (bf16[16,2048]{1,0:T(8,128)(2,1)S(1)}, bf16[16,2048]{1,0:T(8,128)(2,1)S(1)}, u32[]{:S(2)}, u32[]{:S(2)}) collective-permute-start(bf16[16,2048]{1,0:T(8,128)(2,1)S(1)} %get-tuple-element.23), channel_id=1, source_target_pairs={{0,40},{8,48},{16,56},{24,0},{32,8},{40,16},{48,24},{56,32},{1,41}... | collective-permute-start | bytes 196616 | tf_op jit(solution)/shard_map/ppermute | solution.py:26
  149.3 5.8 %collective-permute-start.48 = (bf16[16,2048]{1,0:T(8,128)(2,1)S(1)}, bf16[16,2048]{1,0:T(8,128)(2,1)S(1)}, u32[]{:S(2)}, u32[]{:S(2)}) collective-permute-start(bf16[16,2048]{1,0:T(8,128)(2,1)S(1)} %get-tuple-element.23), channel_id=1, source_target_pairs={{0,48},{8,56},{16,0},{24,8},{32,16},{40,24},{48,32},{56,40},{1,49}... | collective-permute-start | bytes 196616 | tf_op jit(solution)/shard_map/ppermute | solution.py:26
  151.2 7.9 %collective-permute-start.37 = (bf16[64,2048]{1,0:T(8,128)(2,1)S(1)}, bf16[64,2048]{1,0:T(8,128)(2,1)}, u32[]{:S(2)}, u32[]{:S(2)}) collective-permute-start(bf16[64,2048]{1,0:T(8,128)(2,1)S(1)} %collective-permute-done.35.refs_1_), channel_id=1, source_target_pairs={{0,8},{8,16},{16,24},{24,32},{32,40},{40,48},{48,56},{56,0},{1,9},... | collective-permute-start | bytes 786440 | tf_op jit(solution)/shard_map/ppermute | solution.py:26
  154.2 7.5 %collective-permute-start.38 = (bf16[64,2048]{1,0:T(8,128)(2,1)S(1)}, bf16[64,2048]{1,0:T(8,128)(2,1)}, u32[]{:S(2)}, u32[]{:S(2)}) collective-permute-start(bf16[64,2048]{1,0:T(8,128)(2,1)S(1)} %collective-permute-done.36.refs_2_), channel_id=1, source_target_pairs={{0,56},{8,0},{16,8},{24,16},{32,24},{40,32},{48,40},{56,48},{1,57}... | collective-permute-start | bytes 786440 | tf_op jit(solution)/shard_map/ppermute | solution.py:26
  155.2 8.8 %collective-permute-start.49 = (bf16[16,2048]{1,0:T(8,128)(2,1)S(1)}, bf16[16,2048]{1,0:T(8,128)(2,1)S(1)}, u32[]{:S(2)}, u32[]{:S(2)}) collective-permute-start(bf16[16,2048]{1,0:T(8,128)(2,1)S(1)} %get-tuple-element.23), channel_id=1, source_target_pairs={{0,56},{8,0},{16,8},{24,16},{32,24},{40,32},{48,40},{56,48},{1,57}... | collective-permute-start | bytes 196616 | tf_op jit(solution)/shard_map/ppermute | solution.py:26
  159.1 14.0 %collective-permute-start.39 = (bf16[64,2048]{1,0:T(8,128)(2,1)}, bf16[64,2048]{1,0:T(8,128)(2,1)S(1)}, u32[]{:S(2)}, u32[]{:S(2)}) collective-permute-start(bf16[64,2048]{1,0:T(8,128)(2,1)} %collective-permute-done.37.refs_3_), channel_id=1, source_target_pairs={{0,8},{8,16},{16,24},{24,32},{32,40},{40,48},{48,56},{56,0},{1,9},... | collective-permute-start | bytes 786440 | tf_op jit(solution)/shard_map/ppermute | solution.py:26
  161.7 12.1 %collective-permute-start.40 = (bf16[64,2048]{1,0:T(8,128)(2,1)}, bf16[64,2048]{1,0:T(8,128)(2,1)}, u32[]{:S(2)}, u32[]{:S(2)}) collective-permute-start(bf16[64,2048]{1,0:T(8,128)(2,1)} %collective-permute-done.38.refs_4_), channel_id=1, source_target_pairs={{0,56},{8,0},{16,8},{24,16},{32,24},{40,32},{48,40},{56,48},{1,57}... | collective-permute-start | bytes 786440 | tf_op jit(solution)/shard_map/ppermute | solution.py:26
  167.3 26.6 %collective-permute-start.50 = (bf16[128,2048]{1,0:T(8,128)(2,1)S(1)}, bf16[128,2048]{1,0:T(8,128)(2,1)}, u32[]{:S(2)}, u32[]{:S(2)}) collective-permute-start(bf16[128,2048]{1,0:T(8,128)(2,1)S(1)} %constant_dynamic-update-slice_fusion.11.refs_9_), channel_id=1, source_target_pairs={{0,64},{64,128},{128,192},{192,0},{1,65},{65,129},{129,193},{193,1... | collective-permute-start | bytes 1572872 | tf_op jit(solution)/shard_map/ppermute | solution.py:26
  168.2 25.8 %collective-permute-start.51 = (bf16[128,2048]{1,0:T(8,128)(2,1)S(1)}, bf16[128,2048]{1,0:T(8,128)(2,1)}, u32[]{:S(2)}, u32[]{:S(2)}) collective-permute-start(bf16[128,2048]{1,0:T(8,128)(2,1)S(1)} %constant_dynamic-update-slice_fusion.11.refs_9_), channel_id=1, source_target_pairs={{0,128},{64,192},{128,0},{192,64},{1,129},{65,193},{129,1},{193,65... | collective-permute-start | bytes 1572872 | tf_op jit(solution)/shard_map/ppermute | solution.py:26
  168.5 28.1 %collective-permute-start.52 = (bf16[128,2048]{1,0:T(8,128)(2,1)S(1)}, bf16[128,2048]{1,0:T(8,128)(2,1)}, u32[]{:S(2)}, u32[]{:S(2)}) collective-permute-start(bf16[128,2048]{1,0:T(8,128)(2,1)S(1)} %constant_dynamic-update-slice_fusion.11.refs_9_), channel_id=1, source_target_pairs={{0,192},{64,0},{128,64},{192,128},{1,193},{65,1},{129,65},{193,129... | collective-permute-start | bytes 1572872 | tf_op jit(solution)/shard_map/ppermute | solution.py:26
  173.8 25.7 %collective-permute-start.29 = (bf16[2,128,1024]{2,1,0:T(8,128)(2,1)S(1)}, bf16[2,128,1024]{2,1,0:T(8,128)(2,1)S(1)}, u32[]{:S(2)}, u32[]{:S(2)}) collective-permute-start(bf16[2,128,1024]{2,1,0:T(8,128)(2,1)S(1)} %get-tuple-element.14), channel_id=1, source_target_pairs={{0,4},{4,0},{1,5},{5,1},{2,6},{6,2},{3,7},{7,3},{8,12},{12,8},{9,1... | collective-permute-start | bytes 1572872 | tf_op jit(solution)/shard_map/ppermute | solution.py:26
  175.5 32.5 %collective-permute-start = (bf16[3,2048]{1,0:T(4,128)(2,1)S(1)}, bf16[3,2048]{1,0:T(4,128)(2,1)S(1)}, u32[]{:S(2)}, u32[]{:S(2)}) collective-permute-start(bf16[3,2048]{1,0:T(4,128)(2,1)S(1)} %get-tuple-element.26), channel_id=1, source_target_pairs={{0,2},{2,4},{4,6},{6,8},{8,10},{10,12},{12,14},{14,16},{16,18},{18... | collective-permute-start | bytes 36872 | tf_op jit(solution)/shard_map/ppermute | solution.py:366
  210.9 10.1 %collective-permute-start.66 = (bf16[8,1024]{1,0:T(8,128)(2,1)S(1)}, bf16[8,1024]{1,0:T(8,128)(2,1)S(1)}, u32[]{:S(2)}, u32[]{:S(2)}) collective-permute-start(bf16[8,1024]{1,0:T(8,128)(2,1)S(1)} %get-tuple-element.44), channel_id=1, source_target_pairs={{0,8},{8,16},{16,24},{24,32},{32,40},{40,48},{48,56},{56,0},{1,9},... | collective-permute-start | bytes 49160 | tf_op jit(solution)/shard_map/ppermute | solution.py:26
  210.9 10.7 %collective-permute-start.67 = (bf16[8,1024]{1,0:T(8,128)(2,1)S(1)}, bf16[8,1024]{1,0:T(8,128)(2,1)S(1)}, u32[]{:S(2)}, u32[]{:S(2)}) collective-permute-start(bf16[8,1024]{1,0:T(8,128)(2,1)S(1)} %get-tuple-element.44), channel_id=1, source_target_pairs={{0,16},{8,24},{16,32},{24,40},{32,48},{40,56},{48,0},{56,8},{1,17}... | collective-permute-start | bytes 49160 | tf_op jit(solution)/shard_map/ppermute | solution.py:26
  212.6 10.8 %collective-permute-start.68 = (bf16[8,1024]{1,0:T(8,128)(2,1)S(1)}, bf16[8,1024]{1,0:T(8,128)(2,1)S(1)}, u32[]{:S(2)}, u32[]{:S(2)}) collective-permute-start(bf16[8,1024]{1,0:T(8,128)(2,1)S(1)} %get-tuple-element.44), channel_id=1, source_target_pairs={{0,24},{8,32},{16,40},{24,48},{32,56},{40,0},{48,8},{56,16},{1,25}... | collective-permute-start | bytes 49160 | tf_op jit(solution)/shard_map/ppermute | solution.py:26
  213.9 10.2 %collective-permute-start.69 = (bf16[8,1024]{1,0:T(8,128)(2,1)S(1)}, bf16[8,1024]{1,0:T(8,128)(2,1)S(1)}, u32[]{:S(2)}, u32[]{:S(2)}) collective-permute-start(bf16[8,1024]{1,0:T(8,128)(2,1)S(1)} %get-tuple-element.44), channel_id=1, source_target_pairs={{0,32},{8,40},{16,48},{24,56},{32,0},{40,8},{48,16},{56,24},{1,33}... | collective-permute-start | bytes 49160 | tf_op jit(solution)/shard_map/ppermute | solution.py:26
  216.8 8.6 %collective-permute-start.70 = (bf16[8,1024]{1,0:T(8,128)(2,1)S(1)}, bf16[8,1024]{1,0:T(8,128)(2,1)S(1)}, u32[]{:S(2)}, u32[]{:S(2)}) collective-permute-start(bf16[8,1024]{1,0:T(8,128)(2,1)S(1)} %get-tuple-element.44), channel_id=1, source_target_pairs={{0,40},{8,48},{16,56},{24,0},{32,8},{40,16},{48,24},{56,32},{1,41}... | collective-permute-start | bytes 49160 | tf_op jit(solution)/shard_map/ppermute | solution.py:26
  221.0 7.0 %collective-permute-start.71 = (bf16[8,1024]{1,0:T(8,128)(2,1)S(1)}, bf16[8,1024]{1,0:T(8,128)(2,1)S(1)}, u32[]{:S(2)}, u32[]{:S(2)}) collective-permute-start(bf16[8,1024]{1,0:T(8,128)(2,1)S(1)} %get-tuple-element.44), channel_id=1, source_target_pairs={{0,48},{8,56},{16,0},{24,8},{32,16},{40,24},{48,32},{56,40},{1,49}... | collective-permute-start | bytes 49160 | tf_op jit(solution)/shard_map/ppermute | solution.py:26
  221.6 6.9 %collective-permute-start.72 = (bf16[8,1024]{1,0:T(8,128)(2,1)S(1)}, bf16[8,1024]{1,0:T(8,128)(2,1)S(1)}, u32[]{:S(2)}, u32[]{:S(2)}) collective-permute-start(bf16[8,1024]{1,0:T(8,128)(2,1)S(1)} %get-tuple-element.44), channel_id=1, source_target_pairs={{0,56},{8,0},{16,8},{24,16},{32,24},{40,32},{48,40},{56,48},{1,57}... | collective-permute-start | bytes 49160 | tf_op jit(solution)/shard_map/ppermute | solution.py:26
  223.5 6.7 %collective-permute-start.54 = (bf16[8,1024]{1,0:T(8,128)(2,1)S(1)}, bf16[8,1024]{1,0:T(8,128)(2,1)S(1)}, u32[]{:S(2)}, u32[]{:S(2)}) collective-permute-start(bf16[8,1024]{1,0:T(8,128)(2,1)S(1)} %get-tuple-element.45), channel_id=1, source_target_pairs={{0,64},{64,128},{128,192},{192,0},{1,65},{65,129},{129,193},{193,1... | collective-permute-start | bytes 49160 | tf_op jit(solution)/shard_map/ppermute | solution.py:26
  224.1 6.1 %collective-permute-start.55 = (bf16[8,1024]{1,0:T(8,128)(2,1)S(1)}, bf16[8,1024]{1,0:T(8,128)(2,1)S(1)}, u32[]{:S(2)}, u32[]{:S(2)}) collective-permute-start(bf16[8,1024]{1,0:T(8,128)(2,1)S(1)} %get-tuple-element.45), channel_id=1, source_target_pairs={{0,128},{64,192},{128,0},{192,64},{1,129},{65,193},{129,1},{193,65... | collective-permute-start | bytes 49160 | tf_op jit(solution)/shard_map/ppermute | solution.py:26
  229.2 7.8 %collective-permute-start.73 = (bf16[64,1024]{1,0:T(8,128)(2,1)S(1)}, bf16[64,1024]{1,0:T(8,128)(2,1)S(1)}, u32[]{:S(2)}, u32[]{:S(2)}) collective-permute-start(bf16[64,1024]{1,0:T(8,128)(2,1)S(1)} %get-tuple-element.50), channel_id=1, source_target_pairs={{0,4},{4,0},{1,5},{5,1},{2,6},{6,2},{3,7},{7,3},{8,12},{12,8},{9,1... | collective-permute-start | bytes 393224 | tf_op jit(solution)/shard_map/ppermute | solution.py:26
  234.3 7.8 %collective-permute-start.58 = (bf16[64,1024]{1,0:T(8,128)(2,1)S(1)}, bf16[64,1024]{1,0:T(8,128)(2,1)S(1)}, u32[]{:S(2)}, u32[]{:S(2)}) collective-permute-start(bf16[64,1024]{1,0:T(8,128)(2,1)S(1)} %get-tuple-element.37), channel_id=1, source_target_pairs={{0,8},{8,16},{16,24},{24,32},{32,40},{40,48},{48,56},{56,0},{1,9},... | collective-permute-start | bytes 393224 | tf_op jit(solution)/shard_map/ppermute | solution.py:26
  234.5 8.3 %collective-permute-start.59 = (bf16[64,1024]{1,0:T(8,128)(2,1)S(1)}, bf16[64,1024]{1,0:T(8,128)(2,1)S(1)}, u32[]{:S(2)}, u32[]{:S(2)}) collective-permute-start(bf16[64,1024]{1,0:T(8,128)(2,1)S(1)} %get-tuple-element.37), channel_id=1, source_target_pairs={{0,56},{8,0},{16,8},{24,16},{32,24},{40,32},{48,40},{56,48},{1,57}... | collective-permute-start | bytes 393224 | tf_op jit(solution)/shard_map/ppermute | solution.py:26
  237.7 14.0 %collective-permute-start.74 = (bf16[128,1024]{1,0:T(8,128)(2,1)S(1)}, bf16[128,1024]{1,0:T(8,128)(2,1)S(1)}, u32[]{:S(2)}, u32[]{:S(2)}) collective-permute-start(bf16[128,1024]{1,0:T(8,128)(2,1)S(1)} %get-tuple-element.32), channel_id=1, source_target_pairs={{0,64},{64,128},{128,192},{192,0},{1,65},{65,129},{129,193},{193,1... | collective-permute-start | bytes 786440 | tf_op jit(solution)/shard_map/ppermute | solution.py:26
  238.2 14.1 %collective-permute-start.75 = (bf16[128,1024]{1,0:T(8,128)(2,1)S(1)}, bf16[128,1024]{1,0:T(8,128)(2,1)S(1)}, u32[]{:S(2)}, u32[]{:S(2)}) collective-permute-start(bf16[128,1024]{1,0:T(8,128)(2,1)S(1)} %get-tuple-element.32), channel_id=1, source_target_pairs={{0,128},{64,192},{128,0},{192,64},{1,129},{65,193},{129,1},{193,65... | collective-permute-start | bytes 786440 | tf_op jit(solution)/shard_map/ppermute | solution.py:26
  240.0 13.1 %collective-permute-start.76 = (bf16[128,1024]{1,0:T(8,128)(2,1)S(1)}, bf16[128,1024]{1,0:T(8,128)(2,1)S(1)}, u32[]{:S(2)}, u32[]{:S(2)}) collective-permute-start(bf16[128,1024]{1,0:T(8,128)(2,1)S(1)} %get-tuple-element.32), channel_id=1, source_target_pairs={{0,192},{64,0},{128,64},{192,128},{1,193},{65,1},{129,65},{193,129... | collective-permute-start | bytes 786440 | tf_op jit(solution)/shard_map/ppermute | solution.py:26
  247.4 14.1 %collective-permute-start.62 = (bf16[64,1024]{1,0:T(8,128)(2,1)S(1)}, bf16[64,1024]{1,0:T(8,128)(2,1)S(1)}, u32[]{:S(2)}, u32[]{:S(2)}) collective-permute-start(bf16[64,1024]{1,0:T(8,128)(2,1)S(1)} %collective-permute-done.60), channel_id=1, source_target_pairs={{0,8},{8,16},{16,24},{24,32},{32,40},{40,48},{48,56},{56,0},{1,9},... | collective-permute-start | bytes 393224 | tf_op jit(solution)/shard_map/ppermute | solution.py:26
  248.1 13.5 %collective-permute-start.63 = (bf16[64,1024]{1,0:T(8,128)(2,1)S(1)}, bf16[64,1024]{1,0:T(8,128)(2,1)S(1)}, u32[]{:S(2)}, u32[]{:S(2)}) collective-permute-start(bf16[64,1024]{1,0:T(8,128)(2,1)S(1)} %collective-permute-done.61), channel_id=1, source_target_pairs={{0,56},{8,0},{16,8},{24,16},{32,24},{40,32},{48,40},{56,48},{1,57}... | collective-permute-start | bytes 393224 | tf_op jit(solution)/shard_map/ppermute | solution.py:26
  253.9 14.9 %collective-permute-start.78 = (bf16[512,1024]{1,0:T(8,128)(2,1)}, bf16[512,1024]{1,0:T(8,128)(2,1)}, u32[]{:S(2)}, u32[]{:S(2)}) collective-permute-start(bf16[512,1024]{1,0:T(8,128)(2,1)} %constant_dynamic-update-slice_fusion.54.x1_ref), channel_id=1, source_target_pairs={{0,2},{2,0},{1,3},{3,1},{4,6},{6,4},{5,7},{7,5},{8,10},{10,8},{9,1... | collective-permute-start | bytes 3145736 | tf_op jit(solution)/shard_map/ppermute | solution.py:26
  (36 other events, 891.4 us)

commit v2 on v0

v2 whole, which is shorter than its diff:
```python
import functools
import math

import jax
import jax.numpy as jnp
from jax import lax
from jax.experimental import pallas as pl
from jax.experimental.pallas import tpu as pltpu
from jax.sharding import Mesh
from jax.sharding import PartitionSpec as P

NY, NZ, NX, NC = 4, 8, 2, 2
HEADS, HD = 8, 256
HALF = 64
TEAM = NX * NC
SPAN = NZ * NX * NC * HALF
NEG = -1e30
BK, HB = 1024, 4
BF = jnp.bfloat16
F32 = jnp.float32


def packed(block):
    hi = block.astype(BF)
    rest = block - hi.astype(F32)
    mid = rest.astype(BF)
    low = (rest - mid.astype(F32)).astype(BF)
    pad = jnp.zeros((16 - block.shape[0], block.shape[1]), F32)
    return [jnp.concatenate([p.astype(F32), pad], 0).astype(BF) for p in (hi, mid, low)]


def attention_kernel(layout, place, *refs):
    n_kv = len(layout)
    q_refs, kv_refs, refs = refs[: NY + 1], refs[NY + 1 : NY + 1 + n_kv], refs[NY + 1 + n_kv :]
    outs, few_outs, refs = refs[: NY + 1], refs[NY + 1 : 2 * NY + 1], refs[2 * NY + 1 :]
    kvs, qs, acc, m_s, l_s, stage, ahead, sems = refs
    y, z, xl, c = place[0], place[1], place[2], place[3]
    copies = []

    def copy(src, dst):
        copies.append(pltpu.make_async_copy(src, dst, sems.at[len(copies)]))

    for ref, dy, halves in zip(q_refs, (0, 1, 3, 2, 2), ((0, 1), (0, 1), (0, 1), (0,), (1,))):
        for i, half in enumerate(halves):
            copy(ref.at[pl.ds(i * HALF, HALF)], qs.at[half * NY + ((y + dy) & (NY - 1))])
    for ref, entries in zip(kv_refs, layout):
        for at, (dz, dx, dc, r0, rows) in entries:
            s = (((z + dz) & (NZ - 1)) * NX + (xl ^ dx)) * NC + (c ^ dc)
            for half in range(2):
                low, high = max(r0, half * HALF), min(r0 + rows, (half + 1) * HALF)
                if low < high:
                    slot = (2 * NZ * NX * NC - 1 - s) if half else s
                    dst = kvs.at[pl.ds(pl.multiple_of(slot * HALF + low - half * HALF, 16), high - low)]
                    copy(ref.at[pl.ds(at + low - r0, high - low)], dst)
    for cp in copies:
        cp.start()
    m_s[...] = jnp.full_like(m_s, NEG)
    l_s[...] = jnp.zeros_like(l_s)
    acc[...] = jnp.zeros_like(acc)
    for cp in copies:
        cp.wait()

    qs[...] = qs[...] * BF(1.0 / math.sqrt(HD))
    tile = HB * HALF
    per = SPAN // BK
    me = (z * NX + xl) * NC + c
    early = me // (BK // HALF) + 1
    late = (NZ * NX * NC - 1 - me) // (BK // HALF) + 1
    n_whole = (2 * NY - 1) * per
    n_items = n_whole + early + late

    def place_of(i):
        e = i - NY * per
        f = e - (NY - 1 - y) * per
        p = i - n_whole
        g = jnp.where(e < 0, NY + i // per, jnp.where(f < 0, y + 1 + e // per, NY + f // per))
        kb = jnp.where(e < 0, i % per, jnp.where(f < 0, e % per, per + f % per))
        g = jnp.where(p < 0, g, jnp.where(p < early, y, NY + y))
        kb = jnp.where(p < 0, kb, jnp.where(p < early, p, per + p - early))
        return g, pl.multiple_of(kb * BK, BK)

    def scores(g, start, i):
        q = jnp.concatenate([qs[g, :, h * HD : (h + 1) * HD] for h in range(i * HB, (i + 1) * HB)], 0)
        return lax.dot_general(q, kvs[pl.ds(start, BK), :HD], (((1,), (1,)), ((), ())), preferred_element_type=F32)

    def fold(g, start, i, s, masked):
        rows = slice(i * tile, (i + 1) * tile)
        if masked:
            idx = start + lax.broadcasted_iota(jnp.int32, (HALF, BK), 1)
            k_pos = idx + jnp.where(idx < SPAN, y * SPAN, (2 * NY - 2 - y) * SPAN)
            row = lax.broadcasted_iota(jnp.int32, (HALF, BK), 0)
            st = (g & (NY - 1)) * (NZ * NX * NC) + me
            q_pos = jnp.where(g >= NY, 2 * NY * NZ * NX * NC - 1 - st, st) * HALF + row
            visible = k_pos <= q_pos
            s = jnp.concatenate([jnp.where(visible, s[h * HALF : (h + 1) * HALF], NEG) for h in range(HB)], 0)
        m_old = m_s[g, rows]
        mx = s[:, :128]
        for t in range(1, BK // 128):
            mx = jnp.maximum(mx, s[:, t * 128 : (t + 1) * 128])
        m_new = jnp.maximum(m_old, jnp.max(mx, axis=1, keepdims=True))
        alpha = jnp.exp(m_old - m_new)
        m_s[g, rows] = m_new
        parts, total = [], l_s[g, rows] * alpha
        for t in range(BK // 128):
            p = jnp.exp(s[:, t * 128 : (t + 1) * 128] - m_new)
            total = total + p
            parts.append(p.astype(BF))
        l_s[g, rows] = total
        v = kvs[pl.ds(start, BK), HD:]
        o = jnp.dot(jnp.concatenate(parts, 1), v, preferred_element_type=F32)
        acc[g, rows] = acc[g, rows] * jnp.concatenate([alpha, alpha], 1) + o

    def item(masked, i, carry):
        g, start = place_of(i)
        g_next, start_next = place_of(jnp.minimum(i + 1, n_items - 1))
        n = HEADS // HB
        s = ahead[...]
        for j in range(n):
            after = scores(g, start, j + 1) if j + 1 < n else scores(g_next, start_next, 0)
            fold(g, start, j, s, masked)
            s = after
        ahead[...] = s
        return carry

    ahead[...] = scores(*place_of(0), 0)
    lax.fori_loop(0, n_whole, functools.partial(item, False), 0)
    lax.fori_loop(n_whole, n_items, functools.partial(item, True), 0)

    lane = lax.broadcasted_iota(jnp.int32, (HALF, 128), 1)
    lane8 = lax.broadcasted_iota(jnp.int32, (8, 128), 1)
    pick = pl.ds(15, 4, stride=16)
    for dy in range(NY):
        lse = [jnp.zeros((HALF, 128), F32)] * 2
        few = jnp.zeros((8, 128), F32)
        for h in range(HEADS):
            rows = slice(h * HALF, (h + 1) * HALF)
            for half in range(2):
                g = half * NY + ((y + dy) & (NY - 1))
                total = jnp.maximum(jnp.sum(l_s[g, rows], axis=1, keepdims=True), 1e-30)
                value = m_s[g, rows] + jnp.log(total)
                lse[half] = jnp.where(lane == h, value, lse[half])
                o = acc[g, rows] * (1.0 / total)
                out, at = (outs[NY], 0) if dy == 2 and half else (outs[dy], half * HALF)
                out[at : at + HALF, h * HD : (h + 1) * HD] = o.astype(BF)
                stage[half * HALF : (half + 1) * HALF] = o[:, :128]
                stage[(2 + half) * HALF : (3 + half) * HALF] = o[:, 128:]
                stage[(4 + half) * HALF : (5 + half) * HALF] = value
            got = [stage[pl.ds(i * 2 * HALF + 15, 8, stride=16), :] for i in range(3)]
            few_outs[dy][:16, h * HD : (h + 1) * HD] = jnp.concatenate(
                [jnp.concatenate(got[:2], 1), jnp.zeros((8, HD), F32)], 0
            ).astype(BF)
            few = jnp.where(lane8 == h, got[2], few)
        block = jnp.concatenate(lse, 0).T[:HEADS]
        for out, blk, at in ((outs[NY], block, HALF) if dy == 2 else (outs[dy], block, 2 * HALF), (few_outs[dy], few, 16)):
            for p, v in enumerate(packed(blk)):
                out[at : at + 16, p * 128 : (p + 1) * 128] = v
            out[at : at + 16, 384:] = jnp.zeros((16, HEADS * HD - 384), BF)


def attention(place, qs, kv):
    tok, width = qs[0].shape
    layout = [e for _, e in kv]
    hbm = pl.BlockSpec(memory_space=pl.ANY)
    vm = pl.BlockSpec(memory_space=pltpu.VMEM)
    spans = [(r0, r0 + rows) for e in layout for _, (_, _, _, r0, rows) in e]
    n_copies = 2 * NY + sum(len([h for h in (0, 1) if max(a, h * HALF) < min(b, (h + 1) * HALF)]) for a, b in spans)
    return pl.pallas_call(
        functools.partial(attention_kernel, layout),
        in_specs=[pl.BlockSpec(memory_space=pltpu.SMEM)] + [hbm] * (len(qs) + len(kv)),
        out_specs=[vm] * (2 * NY + 1),
        out_shape=[jax.ShapeDtypeStruct((n, width), BF) for n in (tok + 16, tok + 16, HALF, tok + 16, HALF + 16)]
        + [jax.ShapeDtypeStruct((32, width), BF)] * NY,
        scratch_shapes=[
            pltpu.VMEM((2 * SPAN, 2 * HD), BF),
            pltpu.VMEM((2 * NY, HALF, width), BF),
            pltpu.VMEM((2 * NY, HEADS * HALF, HD), F32),
            pltpu.VMEM((2 * NY, HEADS * HALF, 128), F32),
            pltpu.VMEM((2 * NY, HEADS * HALF, 128), F32),
            pltpu.VMEM((6 * HALF, 128), F32),
            pltpu.VMEM((HB * HALF, BK), F32),
            pltpu.SemaphoreType.DMA((n_copies,)),
        ],
        compiler_params=pltpu.CompilerParams(vmem_limit_bytes=56 * 2**20),
        cost_estimate=pl.CostEstimate(flops=10**10, bytes_accessed=8 * 2**20, transcendentals=10**7),
    )(place, *qs, *[a for a, _ in kv])


def by_row(block, rows):
    if rows == 16:
        return jnp.concatenate([block, jnp.zeros((8, 128), F32)], 0)
    return jnp.concatenate([block, jnp.zeros((120, 128), F32)], 0).T


def join_kernel(rows, place, r0, r1, r2, r3, g_ref, keep_ref, send_ref):
    xl, c = place[2], place[3]
    refs = (r0, r1, r2, r3)
    blocks = []
    for r in refs:
        parts = [r[rows : rows + 16, p * 128 : (p + 1) * 128].astype(F32) for p in range(3)]
        blocks.append((parts[0] + parts[1] + parts[2])[:8])
    m = functools.reduce(jnp.maximum, blocks)
    exps = [jnp.exp(b - m) for b in blocks]
    total = exps[0] + exps[1] + exps[2] + exps[3]
    weights = [by_row(e / total, rows) for e in exps]
    low = lax.broadcasted_iota(jnp.int32, (rows, 128), 1) < 64
    for pair in range(HEADS // 2):
        quarters = []
        for h in (2 * pair, 2 * pair + 1):
            for t in range(2):
                cols = slice(h * HD + t * 128, h * HD + (t + 1) * 128)
                o = jnp.zeros((rows, 128), F32)
                for r, w in zip(refs, weights):
                    o = o + r[:rows, cols].astype(F32) * w[:, h : h + 1]
                quarters.append(jax.nn.sigmoid(g_ref[:, cols].astype(F32)) * o)
        cols = slice(pair * 128, (pair + 1) * 128)
        for t in range(2):
            a, b = quarters[t], quarters[2 + t]
            first = jnp.where(low, a, pltpu.roll(b, 64, 1))
            second = jnp.where(low, pltpu.roll(a, 64, 1), b)
            keep_ref[t ^ xl, :, cols] = jnp.where(c == 0, first, second).astype(BF)
            send_ref[t ^ xl, :, cols] = jnp.where(c == 0, second, first).astype(BF)


def join(place, parts, g):
    rows, width = g.shape
    vm = pl.BlockSpec(memory_space=pltpu.VMEM)
    half = jax.ShapeDtypeStruct((NX, rows, width // TEAM), BF)
    return pl.pallas_call(
        functools.partial(join_kernel, rows),
        in_specs=[pl.BlockSpec(memory_space=pltpu.SMEM)] + [vm] * 5,
        out_specs=[vm, vm],
        out_shape=[half, half],
        compiler_params=pltpu.CompilerParams(vmem_limit_bytes=24 * 2**20),
    )(place, *parts, g)


def project_kernel(rows, a_ref, b_ref, w0_hbm, w1_hbm, w2_hbm, keep_ref, send_ref, ws, sems):
    step = 512
    n = keep_ref.shape[1] // step
    loads = []
    for i in range(n):
        cols = slice(i * step, (i + 1) * step)
        at = 0
        for t, w in enumerate((w0_hbm, w1_hbm, w2_hbm)):
            n_rows = w.shape[0]
            loads.append(pltpu.make_async_copy(w.at[:, cols], ws.at[at : at + n_rows, cols], sems.at[i, t]))
            at += n_rows
    for load in loads:
        load.start()
    x = jnp.concatenate([jnp.concatenate([a_ref[t], b_ref[t]], 0) for t in range(NX)], 1)
    for i in range(n):
        for t in range(3):
            loads[3 * i + t].wait()
        cols = slice(i * step, (i + 1) * step)
        out = jnp.dot(x, ws[:, cols], preferred_element_type=F32)
        keep_ref[:, cols] = out[:rows]
        send_ref[:, cols] = out[rows:].astype(BF)


def project(a, b, w0, w1, w2):
    rows, width = a.shape[1], w0.shape[1]
    vm = pl.BlockSpec(memory_space=pltpu.VMEM)
    hbm = pl.BlockSpec(memory_space=pl.ANY)
    return pl.pallas_call(
        functools.partial(project_kernel, rows),
        in_specs=[vm, vm, hbm, hbm, hbm],
        out_specs=[vm, vm],
        out_shape=[jax.ShapeDtypeStruct((rows, width), F32), jax.ShapeDtypeStruct((rows, width), BF)],
        scratch_shapes=[pltpu.VMEM((NX * w0.shape[0], width), BF), pltpu.SemaphoreType.DMA((4, 3))],
        compiler_params=pltpu.CompilerParams(vmem_limit_bytes=24 * 2**20),
    )(a, b, w0, w1, w2)


def lens_kernel(who, x_ref, w_ref, *refs):
    out_ref = refs[-1]
    got = jnp.dot(x_ref[...], w_ref[...], preferred_element_type=F32)
    for i in range(out_ref.shape[0]):
        for j in range(NX):
            at = (i * NX + j) * NZ * 8
            out_ref[i, :, j, 0] = got[at : at + NZ * 8].reshape(NZ, 8, -1)


def lens(who, x, weight, before=None):
    ys = 2
    tile = ys * NX * NZ * 8
    rows, depth = x.shape
    vocab = weight.shape[1]
    extra = [] if before is None else [before]
    return pl.pallas_call(
        lens_kernel,
        grid_spec=pltpu.PrefetchScalarGridSpec(
            num_scalar_prefetch=1,
            grid=(rows // tile,),
            in_specs=[pl.BlockSpec((tile, depth), lambda i, w: (i, 0)), pl.BlockSpec((depth, vocab), lambda i, w: (0, 0))]
            + [pl.BlockSpec(memory_space=pl.ANY)] * len(extra),
            out_specs=pl.BlockSpec((ys, NZ, NX, 1, 8, vocab), lambda i, w: (i, 0, 0, w[0], 0, 0)),
        ),
        out_shape=jax.ShapeDtypeStruct((NY, NZ, NX, NC, 8, vocab), F32),
        input_output_aliases={} if before is None else {3: 0},
        compiler_params=pltpu.CompilerParams(vmem_limit_bytes=28 * 2**20),
        cost_estimate=pl.CostEstimate(flops=2 * rows * weight.size, bytes_accessed=6 * 2**20, transcendentals=0),
    )(who, x, weight, *extra)


def short_conv(prefix, rows, taps):
    lag = taps.shape[0] - 1
    extended = jnp.concatenate([prefix, rows], 0).astype(F32)
    total = jnp.zeros(rows.shape, F32)
    for t in range(lag + 1):
        total = total + taps[t].astype(F32) * extended[lag - t : lag - t + rows.shape[0]]
    return total


def hidden_rows(resid, rims, taps, me, last):
    lag = taps.shape[0] - 1
    count = NY * NZ * NX * NC
    names = ("y", "z", "xl", "c")
    low = lax.ppermute(rims[:lag], names, [(i, i + 1) for i in range(count - 1)])
    high = lax.ppermute(rims[lag:], names, [(i + 1, i) for i in range(count - 1)])
    high = jnp.where(me == last, resid[HALF - lag : HALF], high)
    conv = jnp.concatenate([short_conv(low, resid[:HALF], taps), short_conv(high, resid[HALF:], taps)], 0)
    return (resid.astype(F32) + jax.nn.silu(conv)).astype(BF)


def shift(x, axis, by):
    count = {"y": NY, "z": NZ, "xl": NX, "c": NC}[axis]
    return lax.ppermute(x, axis, [(i, (i + by) % count) for i in range(count)])


def body(resid, conv_weight, queries, keys, values, gates, out_weight, norm_gain, lens_weight):
    y, z, xl, c = (lax.axis_index(a) for a in ("y", "z", "xl", "c"))
    me = ((y * NZ + z) * NX + xl) * NC + c
    place = jnp.stack([y, z, xl, c]).astype(jnp.int32)
    tok, width = resid.shape
    few = lambda a: jnp.pad(a.reshape(8, 16, -1)[:, 15], ((0, 8), (0, 0)))

    w_own = lax.all_gather(out_weight, "z", axis=0, tiled=True)

    kv_own = jnp.concatenate([keys, values], 1)
    q_up, q_down = shift(queries, "y", -1), shift(queries, "y", 1)
    q_far = [shift(q_down[:HALF], "y", 1), shift(q_up[HALF:], "y", -1)]
    pair = jnp.concatenate([kv_own, shift(kv_own, "xl", 1)], 0)
    both = lambda dz: [(dz, 0, 0, 0, tok), (dz, 1, 0, 0, tok)]
    held = [(pair, both(0))]
    fwd = bwd = pair
    for s in range(1, NZ // 2):
        fwd, bwd = shift(fwd, "z", 1), shift(bwd, "z", -1)
        held += [(fwd, both(-s)), (bwd, both(s))]
    fwd, bwd = fwd[:tok], bwd[tok:]
    fwd, bwd, q_up, q_down, *q_far = lax.optimization_barrier((fwd, bwd, q_up, q_down, *q_far))
    held += [(shift(fwd, "z", 1), both(4)[:1]), (shift(bwd, "z", -1), both(4)[1:])]
    q_team = [queries, q_up, q_down] + q_far

    kv = []
    for group in (held[:5], held[5:]):
        entries, at = [], 0
        for piece, spans in group:
            kv.append((piece, [(i * tok, e) for i, e in enumerate(spans)]))
            for dz, dx, _, r0, n in spans:
                entries.append((at, (dz, dx, 1, r0, n)))
                at += n
        kv.append((shift(jnp.concatenate([p for p, _ in group], 0), "c", 1), entries))

    blocks = resid.reshape(8, 16, width)
    taps = conv_weight.astype(F32)
    conv_few = sum(taps[t] * blocks[:, 15 - t].astype(F32) for t in range(conv_weight.shape[0]))
    hidden_few = (blocks[:, 15].astype(F32) + jax.nn.silu(conv_few)).astype(BF)
    g_few = few(gates)
    half_w = w_own.shape[0] // 2
    w_other = [
        shift(w_own[:half_w], "xl", 1),
        lax.ppermute(w_own[half_w:], ("xl", "dp"), [(i, 3 - i) for i in range(4)]),
    ]
    place, hidden_few, g_few, _ = lax.optimization_barrier((place, hidden_few, g_few, w_own))
    got = attention(place, q_team, kv)
    main, lead = got[: NY + 1], got[NY + 1 :]
    to_team = lambda a: [a[0], shift(a[1], "y", 1), shift(a[2], "y", 2), shift(a[3], "y", -1)]
    spread = lambda a, axes, n: lax.all_to_all(jnp.broadcast_to(a[None], (n,) + a.shape), axes, 0, 0).reshape(-1, width)

    lead = to_team(lead)
    far = [shift(shift(main[2], "y", 1), "y", 1), shift(shift(main[4], "y", -1), "y", -1)]
    main = [main[0], shift(main[1], "y", 1), jnp.concatenate(far, 0), shift(main[3], "y", -1)]
    f_keep, f_send = join(place, lead, g_few)
    f_own, f_other = project(f_keep, shift(f_send, "c", 1), w_own, *w_other)
    rows = (hidden_few.astype(F32) + (f_own + shift(f_other, "c", 1).astype(F32))[:8]).astype(BF).astype(F32)
    normed = (rows * lax.rsqrt(jnp.mean(rows * rows, axis=-1, keepdims=True) + 1e-6) * norm_gain).astype(BF)
    per_z = spread(normed, "z", NZ)
    lag = conv_weight.shape[0] - 1
    rims = jnp.concatenate([resid[HALF - lag : HALF], resid[2 * HALF - lag :]], 0)
    per_z, rims, *main = lax.optimization_barrier((per_z, rims, *main))
    every = spread(per_z, ("y", "xl"), NY * NX)

    hidden = hidden_rows(resid, rims, conv_weight, me, NY * NZ * NX * NC - 1)
    keep, send = join(place, main, gates)
    p_own, p_other = project(keep, shift(send, "c", 1), w_own, *w_other)
    mixed = (hidden.astype(F32) + p_own + shift(p_other, "c", 1).astype(F32)).astype(BF)

    theirs = shift(every, "c", 1)
    who = c.astype(jnp.int32).reshape(1)
    logits = lens(who, every, lens_weight)
    logits = lens(1 - who, theirs, lens_weight, logits)
    return mixed, logits.reshape(-1, lens_weight.shape[1])


def solution(mesh):
    fine = Mesh(mesh.devices.reshape(NY, NZ, NX, NC, -1), ("y", "z", "xl", "c", "dp"))
    rows = P(("dp", "y", "z", "xl", "c"), None)
    return jax.shard_map(
        body,
        mesh=fine,
        in_specs=(rows, P(), rows, rows, rows, rows, P(("z", "xl", "c"), None), P(), P(None, ("y", "z", "xl", "c"))),
        out_specs=(rows, P("dp", ("y", "z", "xl", "c"))),
        check_vma=False,
    )
```

time: 896 us -> 208 us (0.23)
  waiting for transfers between devices: 695 us -> 51.8 us
  starting transfers between devices: 7.22 us -> 76.3 us
  matrix products: 51.5 us -> 0 us
  Pallas kernels: 0 us -> 39.5 us
  local copies, waits for them, and re-layouts: 58.9 us -> 19.4 us
  loops' own time: 32.7 us -> 0 us
  other arithmetic: 35.1 us -> 4.85 us
    all_gather x4 -> x1, waiting for transfers between devices: 692 us -> 0.01 us  [body(): w_own = lax.all_gather(out_weight, 'z', axis=0, tiled=True)]
    ppermute x2 -> x33, starting transfers between devices: 7.07 us -> 65.8 us  [the longest x30 55.8 us: shift(): return lax.ppermute(x, axis, [(i, (i + by) % count) for i in range(count)])]
    dot_general x36 -> x0, matrix products: 51.5 us -> none  [the longest x17 27.9 us: attend_block(): lax.dot_general(key_block, query_rows, (((1,), (1,)), ((), ())), preferre...]
    pallas_call x0 -> x7, Pallas kernels: none -> 39.5 us  [the longest x1 23.8 us: attention(): pl.pallas_call(functools.partial(attention_kernel, layout), in_specs=[pl....]
    squeeze x16 -> x0, local copies, waits for them, and re-layouts: 34 us -> none  [run_group(): lax.dynamic_index_in_dim(value_groups, group_id, 0, keepdims=False)]
    another operation x33 -> x0, loops' own time: 32.7 us -> none  [the longest x1 31.5 us: fold_keys(): return lax.fori_loop(0, group_total, run_group, states_in)]
    ppermute x2 -> x33, waiting for transfers between devices: 1.08 us -> 33.3 us  [the longest x30 33.3 us: shift(): return lax.ppermute(x, axis, [(i, (i + by) % count) for i in range(count)])]
    all_to_all x0 -> x2, waiting for transfers between devices: none -> 17.8 us  [body(): lax.all_to_all(jnp.broadcast_to(a[None], (n,) + a.shape), axes, 0, 0)]
  transfers between devices with their start and end apart: 6 -> 36, of which waited for: 4 -> 12; matrix products, arithmetic and copies ran while one was open for 13% -> 9% of each run, Pallas kernels for 0% -> 17%
where the time goes in v2:
time: 208 us; the launch traced here: 206 us
  starting transfers between devices  76.3 us (37%)
  waiting for transfers between devices  51.8 us (25%)
  Pallas kernels  39.5 us (19%)
  local copies, waits for them, and re-layouts  19.4 us (9%)
  between operations  14.6 us (7%)
  other arithmetic  4.85 us (2%)
    ppermute x30, starting transfers between devices, shift(): return lax.ppermute(x, axis, [(i, (i + by) % count) for i in range(count)])  55.8 us
    ppermute x30, waiting for transfers between devices, shift(): return lax.ppermute(x, axis, [(i, (i + by) % count) for i in range(count)])  33.3 us
    pallas_call x1, Pallas kernels, attention(): pl.pallas_call(functools.partial(attention_kernel, layout), in_specs=[pl....  23.8 us
    all_to_all x2, waiting for transfers between devices, body(): lax.all_to_all(jnp.broadcast_to(a[None], (n,) + a.shape), axes, 0, 0)  17.8 us
    unnamed x61, local copies, waits for them, and re-layouts  10.7 us
    all_to_all x2, starting transfers between devices, body(): lax.all_to_all(jnp.broadcast_to(a[None], (n,) + a.shape), axes, 0, 0)  10.4 us
    pallas_call x2, Pallas kernels, lens(): pl.pallas_call(lens_kernel, grid_spec=pltpu.PrefetchScalarGridSpec(num_sc...  8.08 us
    ppermute x1, starting transfers between devices, hidden_rows(): lax.ppermute(rims[lag:], names, [(i + 1, i) for i in range(count - 1)])  4.58 us
  transfers between devices with their start and end apart: 36, of which 12 were waited for; matrix products, arithmetic and copies ran while one was open for 9% of the time, Pallas kernels for 17%

profile of v2, /device:TPU:1, one launch (start us, length us, event | category | flops | bytes accessed | tf_op | source)
XLA Modules:
  0.0 206.4 jit_solution(11896791359780188658)
XLA Ops:
  7.2 0.7 all-gather.2.cloned.1.call-update
  7.9 1.5 constant_dynamic-update-slice_fusion.8
  9.4 1.5 constant_dynamic-update-slice_fusion.7
  10.9 2.0 collective-permute-start
  12.9 2.4 %collective-permute-done = bf16[128,512]{1,0:T(8,128)(2,1)S(1)} collective-permute-done((bf16[128,512]{1,0:T(8,128)(2,1)S(1)}, bf16[128,512]{1,0:T(8,128)(2,1)S(1)}, u32[]{:S(2)}, u32[]{:S(2)}) %collective-permute-start) | collective-permute-done | bytes 131104 | tf_op jit(solution)/shard_map/ppermute | solution.py:327
  15.3 2.5 %collective-permute-start.1 = (bf16[256,512]{1,0:T(8,128)(2,1)S(1)}, bf16[256,512]{1,0:T(8,128)(2,1)S(1)}, u32[]{:S(2)}, u32[]{:S(2)}) collective-permute-start(bf16[256,512]{1,0:T(8,128)(2,1)S(1)} %pad_maximum_fusion.3.refs_5_), channel_id=1, source_target_pairs={{0,8},{8,16},{16,24},{24,32},{32,40},{40,48},{48,56},{56,0},{1,9},... | collective-permute-start | bytes 786440 | tf_op jit(solution)/shard_map/ppermute | solution.py:327
  17.8 4.0 %collective-permute-start.4 = (bf16[256,512]{1,0:T(8,128)(2,1)S(1)}, bf16[256,512]{1,0:T(8,128)(2,1)S(1)}, u32[]{:S(2)}, u32[]{:S(2)}) collective-permute-start(bf16[256,512]{1,0:T(8,128)(2,1)S(1)} %pad_maximum_fusion.3.refs_5_), channel_id=1, source_target_pairs={{0,56},{8,0},{16,8},{24,16},{32,24},{40,32},{48,40},{56,48},{1,57}... | collective-permute-start | bytes 786440 | tf_op jit(solution)/shard_map/ppermute | solution.py:327
  21.8 2.7 %collective-permute-start.7 = (bf16[128,2048]{1,0:T(8,128)(2,1)}, bf16[128,2048]{1,0:T(8,128)(2,1)S(1)}, u32[]{:S(2)}, u32[]{:S(2)}) collective-permute-start(bf16[128,2048]{1,0:T(8,128)(2,1)} %refs_0_.1), channel_id=1, source_target_pairs={{0,192},{64,0},{128,64},{192,128},{1,193},{65,1},{129,65},{193,129... | collective-permute-start | bytes 1572872 | tf_op jit(solution)/shard_map/ppermute | solution.py:327
  24.6 2.2 %collective-permute-done.1.refs_6_ = bf16[256,512]{1,0:T(8,128)(2,1)S(1)} collective-permute-done((bf16[256,512]{1,0:T(8,128)(2,1)S(1)}, bf16[256,512]{1,0:T(8,128)(2,1)S(1)}, u32[]{:S(2)}, u32[]{:S(2)}) %collective-permute-start.1) | collective-permute-done | bytes 262176 | tf_op jit(solution)/shard_map/ppermute | solution.py:327
  26.8 3.5 %collective-permute-start.5 = (bf16[256,512]{1,0:T(8,128)(2,1)S(1)}, bf16[256,512]{1,0:T(8,128)(2,1)S(1)}, u32[]{:S(2)}, u32[]{:S(2)}) collective-permute-start(bf16[256,512]{1,0:T(8,128)(2,1)S(1)} %collective-permute-done.4.refs_7_), channel_id=1, source_target_pairs={{0,56},{8,0},{16,8},{24,16},{32,24},{40,32},{48,40},{56,48},{1,57}... | collective-permute-start | bytes 786440 | tf_op jit(solution)/shard_map/ppermute | solution.py:327
  30.6 0.7 constant_dynamic-update-slice_fusion.6
  31.2 0.7 constant_dynamic-update-slice_fusion.5
  32.0 5.4 %collective-permute-done.8.refs_2_ = bf16[128,2048]{1,0:T(8,128)(2,1)S(1)} collective-permute-done((bf16[128,2048]{1,0:T(8,128)(2,1)}, bf16[128,2048]{1,0:T(8,128)(2,1)S(1)}, u32[]{:S(2)}, u32[]{:S(2)}) %collective-permute-start.8) | collective-permute-done | bytes 524320 | tf_op jit(solution)/shard_map/ppermute | solution.py:327
  37.6 2.7 %collective-permute-start.10 = (bf16[64,2048]{1,0:T(8,128)(2,1)S(1)}, bf16[64,2048]{1,0:T(8,128)(2,1)S(1)}, u32[]{:S(2)}, u32[]{:S(2)}) collective-permute-start(bf16[64,2048]{1,0:T(8,128)(2,1)S(1)} %slice.154), channel_id=1, source_target_pairs={{0,192},{64,0},{128,64},{192,128},{1,193},{65,1},{129,65},{193,129... | collective-permute-start | bytes 786440 | tf_op jit(solution)/shard_map/ppermute | solution.py:327
  40.3 2.8 %collective-permute-start.6 = (bf16[256,512]{1,0:T(8,128)(2,1)S(1)}, bf16[256,512]{1,0:T(8,128)(2,1)S(1)}, u32[]{:S(2)}, u32[]{:S(2)}) collective-permute-start(bf16[256,512]{1,0:T(8,128)(2,1)S(1)} %collective-permute-done.5.refs_9_), channel_id=1, source_target_pairs={{0,56},{8,0},{16,8},{24,16},{32,24},{40,32},{48,40},{56,48},{1,57}... | collective-permute-start | bytes 786440 | tf_op jit(solution)/shard_map/ppermute | solution.py:327
  43.1 0.7 constant_dynamic-update-slice_fusion.4
  43.8 0.7 constant_dynamic-update-slice_fusion.3
  44.5 0.7 constant_dynamic-update-slice_fusion.2
  45.3 6.2 %collective-permute-start.11 = (bf16[1280,512]{1,0:T(8,128)(2,1)}, bf16[1280,512]{1,0:T(8,128)(2,1)}, u32[]{:S(2)}, u32[]{:S(2)}) collective-permute-start(bf16[1280,512]{1,0:T(8,128)(2,1)} %constant_dynamic-update-slice_fusion.2), channel_id=1, source_target_pairs={{0,2},{2,0},{1,3},{3,1},{4,6},{6,4},{5,7},{7,5},{8,10},{10,8},{9,1... | collective-permute-start | bytes 3932168 | tf_op jit(solution)/shard_map/ppermute | solution.py:327
  51.4 1.8 collective-permute-done.3.refs_11_
  53.4 2.9 %collective-permute-start.13 = (bf16[128,512]{1,0:T(8,128)(2,1)S(1)}, bf16[128,512]{1,0:T(8,128)(2,1)S(1)}, u32[]{:S(2)}, u32[]{:S(2)}) collective-permute-start(bf16[128,512]{1,0:T(8,128)(2,1)S(1)} %slice.152), channel_id=1, source_target_pairs={{0,56},{8,0},{16,8},{24,16},{32,24},{40,32},{48,40},{56,48},{1,57}... | collective-permute-start | bytes 393224 | tf_op jit(solution)/shard_map/ppermute | solution.py:327
  56.3 5.1 %collective-permute-done.12.refs_13_ = bf16[128,512]{1,0:T(8,128)(2,1)S(1)} collective-permute-done((bf16[128,512]{1,0:T(8,128)(2,1)S(1)}, bf16[128,512]{1,0:T(8,128)(2,1)S(1)}, u32[]{:S(2)}, u32[]{:S(2)}) %collective-permute-start.12) | collective-permute-done | bytes 131104 | tf_op jit(solution)/shard_map/ppermute | solution.py:327
  61.5 5.2 %collective-permute-start.14 = (bf16[768,512]{1,0:T(8,128)(2,1)S(1)}, bf16[768,512]{1,0:T(8,128)(2,1)}, u32[]{:S(2)}, u32[]{:S(2)}) collective-permute-start(bf16[768,512]{1,0:T(8,128)(2,1)S(1)} %pad_maximum_fusion.1), channel_id=1, source_target_pairs={{0,2},{2,0},{1,3},{3,1},{4,6},{6,4},{5,7},{7,5},{8,10},{10,8},{9,1... | collective-permute-start | bytes 2359304 | tf_op jit(solution)/shard_map/ppermute | solution.py:327
  66.8 1.0 slice.150
  67.9 0.6 pad_add_fusion.place
  68.5 1.8 fusion.16
  70.3 0.7 collective-permute-start.19
  71.0 2.5 %collective-permute-start.20 = (bf16[256,2048]{1,0:T(8,128)(2,1)S(1)}, bf16[256,2048]{1,0:T(8,128)(2,1)S(1)}, u32[]{:S(2)}, u32[]{:S(2)}) collective-permute-start(bf16[256,2048]{1,0:T(8,128)(2,1)S(1)} %get-tuple-element.68), channel_id=1, source_target_pairs={{0,5},{1,4},{4,1},{5,0},{2,7},{3,6},{6,3},{7,2},{8,13},{9,12},{12,... | collective-permute-start | bytes 3145736 | tf_op jit(solution)/shard_map/ppermute | solution.py:372
  73.6 23.8 %shard_map.104 = (bf16[144,2048]{1,0:T(8,128)(2,1)}, bf16[144,2048]{1,0:T(8,128)(2,1)}, bf16[64,2048]{1,0:T(8,128)(2,1)}, bf16[144,2048]{1,0:T(8,128)(2,1)}, bf1...) custom-call(s32[4]{0:T(128)} %pad_add_fusion.place, ...), custom_call_target="tpu_custom_call" | custom-call | flops 10000000000 | bytes 8388608 | tf_op jit(solution)/shard_map/pallas_call | solution.py:167
  97.4 1.7 collective-permute-start.15
  99.1 2.4 %collective-permute-start.16 = (bf16[32,2048]{1,0:T(8,128)(2,1)}, bf16[32,2048]{1,0:T(8,128)(2,1)S(1)}, u32[]{:S(2)}, u32[]{:S(2)}) collective-permute-start(bf16[32,2048]{1,0:T(8,128)(2,1)} %get-tuple-element.44), channel_id=1, source_target_pairs={{0,128},{64,192},{128,0},{192,64},{1,129},{65,193},{129,1},{193,65... | collective-permute-start | bytes 393224 | tf_op jit(solution)/shard_map/ppermute | solution.py:327
  101.5 1.6 collective-permute-start.17
  103.3 3.5 %collective-permute-done.16.r2 = bf16[32,2048]{1,0:T(8,128)(2,1)S(1)} collective-permute-done((bf16[32,2048]{1,0:T(8,128)(2,1)}, bf16[32,2048]{1,0:T(8,128)(2,1)S(1)}, u32[]{:S(2)}, u32[]{:S(2)}) %collective-permute-start.16) | collective-permute-done | bytes 131104 | tf_op jit(solution)/shard_map/ppermute | solution.py:327
  106.9 0.9 copy-done.7
  107.8 0.8 shard_map.105
  108.5 2.1 %collective-permute-start.18 = (bf16[2,16,512]{2,1,0:T(8,128)(2,1)S(1)}, bf16[2,16,512]{2,1,0:T(8,128)(2,1)S(1)}, u32[]{:S(2)}, u32[]{:S(2)}) collective-permute-start(bf16[2,16,512]{2,1,0:T(8,128)(2,1)S(1)} %get-tuple-element.48), channel_id=1, source_target_pairs={{0,2},{2,0},{1,3},{3,1},{4,6},{6,4},{5,7},{7,5},{8,10},{10,8},{9,1... | collective-permute-start | bytes 98312 | tf_op jit(solution)/shard_map/ppermute | solution.py:327
  110.7 2.2 %collective-permute-start.25 = (bf16[80,2048]{1,0:T(8,128)(2,1)}, bf16[80,2048]{1,0:T(8,128)(2,1)}, u32[]{:S(2)}, u32[]{:S(2)}) collective-permute-start(bf16[80,2048]{1,0:T(8,128)(2,1)} %get-tuple-element.54), channel_id=1, source_target_pairs={{0,192},{64,0},{128,64},{192,128},{1,193},{65,1},{129,65},{193,129... | collective-permute-start | bytes 983048 | tf_op jit(solution)/shard_map/ppermute | solution.py:327
  112.9 1.8 shard_map.106
  115.1 0.8 fusion.18
  115.9 0.6 collective-permute-start.22
  116.6 2.7 %collective-permute-start.27 = (bf16[144,2048]{1,0:T(8,128)(2,1)}, bf16[144,2048]{1,0:T(8,128)(2,1)}, u32[]{:S(2)}, u32[]{:S(2)}) collective-permute-start(bf16[144,2048]{1,0:T(8,128)(2,1)} %get-tuple-element.55), channel_id=1, source_target_pairs={{0,192},{64,0},{128,64},{192,128},{1,193},{65,1},{129,65},{193,129... | collective-permute-start | bytes 1769480 | tf_op jit(solution)/shard_map/ppermute | solution.py:327
  119.3 2.6 %collective-permute-done.23 = bf16[64,2048]{1,0:T(8,128)(2,1)} collective-permute-done((bf16[64,2048]{1,0:T(8,128)(2,1)}, bf16[64,2048]{1,0:T(8,128)(2,1)}, u32[]{:S(2)}, u32[]{:S(2)}) %collective-permute-start.23) | collective-permute-done | bytes 262176 | tf_op jit(solution)/shard_map/ppermute | solution.py:327
  121.9 2.7 %collective-permute-start.26 = (bf16[80,2048]{1,0:T(8,128)(2,1)}, bf16[80,2048]{1,0:T(8,128)(2,1)}, u32[]{:S(2)}, u32[]{:S(2)}) collective-permute-start(bf16[80,2048]{1,0:T(8,128)(2,1)} %collective-permute-done.25), channel_id=1, source_target_pairs={{0,192},{64,0},{128,64},{192,128},{1,193},{65,1},{129,65},{193,129... | collective-permute-start | bytes 983048 | tf_op jit(solution)/shard_map/ppermute | solution.py:327
  124.8 0.7 broadcast_in_dim.4
  125.5 6.0 %all-to-all-start = ((bf16[8,8,2048]{2,1,0:T(8,128)(2,1)}), bf16[8,8,2048]{2,1,0:T(8,128)(2,1)S(1)}, u32[]{:S(2)}, u32[]{:S(2)}) async-start(bf16[8,8,2048]{2,1,0:T(8,128)(2,1)} %broadcast_in_dim.4), calls=%async_computation | async-start | bytes 524288 | tf_op jit(solution)/shard_map/all_to_all | solution.py:378
  131.6 8.6 %collective-permute-done.24 = bf16[64,2048]{1,0:T(8,128)(2,1)} collective-permute-done((bf16[64,2048]{1,0:T(8,128)(2,1)}, bf16[64,2048]{1,0:T(8,128)(2,1)}, u32[]{:S(2)}, u32[]{:S(2)}) %collective-permute-start.24) | collective-permute-done | bytes 262176 | tf_op jit(solution)/shard_map/ppermute | solution.py:327
  140.2 2.0 pad_maximum_fusion.2.r2
  142.2 1.6 broadcast_in_dim.5
  143.7 4.4 %all-to-all-start.1 = ((bf16[8,64,2048]{2,1,0:T(8,128)(2,1)}), bf16[8,64,2048]{2,1,0:T(8,128)(2,1)}, u32[]{:S(2)}, u32[]{:S(2)}) async-start(bf16[8,64,2048]{2,1,0:T(8,128)(2,1)} %broadcast_in_dim.5), calls=%async_computation.1 | async-start | bytes 4194304 | tf_op jit(solution)/shard_map/all_to_all | solution.py:378
  148.1 1.8 fusion.17
  149.9 4.6 %collective-permute-start.29 = (bf16[3,2048]{1,0:T(4,128)(2,1)S(1)}, bf16[3,2048]{1,0:T(4,128)(2,1)S(1)}, u32[]{:S(2)}, u32[]{:S(2)}) collective-permute-start(bf16[3,2048]{1,0:T(4,128)(2,1)S(1)} %get-tuple-element.85), channel_id=1, source_target_pairs={{2,0},{4,2},{6,4},{8,6},{10,8},{12,10},{14,12},{16,14},{18,16},{20... | collective-permute-start | bytes 36872 | tf_op jit(solution)/shard_map/ppermute | solution.py:319
  154.5 17.8 %all-to-all-done.1 = bf16[8,64,2048]{2,1,0:T(8,128)(2,1)} async-done(((bf16[8,64,2048]{2,1,0:T(8,128)(2,1)}), bf16[8,64,2048]{2,1,0:T(8,128)(2,1)}, u32[]{:S(2)}, u32[]{:S(2)}) %all-to-all-start.1) | async-done | bytes 2097184 | tf_op jit(solution)/shard_map/all_to_all | solution.py:378
  172.3 3.8 %collective-permute-start.32 = (bf16[512,2048]{1,0:T(8,128)(2,1)}, bf16[512,2048]{1,0:T(8,128)(2,1)}, u32[]{:S(2)}, u32[]{:S(2)}) collective-permute-start(bf16[512,2048]{1,0:T(8,128)(2,1)} %bitcast.21.x_ref), channel_id=1, source_target_pairs={{0,2},{2,0},{1,3},{3,1},{4,6},{6,4},{5,7},{7,5},{8,10},{10,8},{9,1... | collective-permute-start | bytes 6291464 | tf_op jit(solution)/shard_map/ppermute | solution.py:327
  176.2 1.1 copy-done.4
  177.2 1.0 copy-done.5
  178.3 1.1 copy-done.6
  179.4 2.7 %shard_map.107 = (bf16[2,128,512]{2,1,0:T(8,128)(2,1)S(1)}, bf16[2,128,512]{2,1,0:T(8,128)(2,1)S(1)}) custom-call(s32[4]{0:T(128)S(1)} %copy-done.8, bf16[144,2048]{1,0:T(8,128)(2,1)S(1)} %copy-done.6, bf16[144,2048]{1,0:T(8,128)(2,1)} %collective-permute-done.22.r1, bf16[144,2048]{1,0:T(8,128)(2,1)S(1)} %copy-done.4, ...), custom_call_target="tpu_custom_call" | custom-call | tf_op jit(solution)/shard_map/pallas_call | solution.py:228
  182.1 2.9 %collective-permute-start.28 = (bf16[3,2048]{1,0:T(4,128)(2,1)S(1)}, bf16[3,2048]{1,0:T(4,128)(2,1)S(1)}, u32[]{:S(2)}, u32[]{:S(2)}) collective-permute-start(bf16[3,2048]{1,0:T(4,128)(2,1)S(1)} %get-tuple-element.84), channel_id=1, source_target_pairs={{0,2},{2,4},{4,6},{6,8},{8,10},{10,12},{12,14},{14,16},{16,18},{18... | collective-permute-start | bytes 36872 | tf_op jit(solution)/shard_map/ppermute | solution.py:318
  185.2 2.4 %shard_map.108 = (f32[128,2048]{1,0:T(8,128)S(1)}, bf16[128,2048]{1,0:T(8,128)(2,1)S(1)}) custom-call(bf16[2,128,512]{2,1,0:T(8,128)(2,1)S(1)} %get-tuple-element.61.a_ref, bf16[2,128,512]{2,1,0:T(8,128)(2,1)S(1)} %collective-permute-done.30.b_ref, bf16[512,2048]{1,0:T(8,128)(2,1)S(1)} %copy-done, bf16[256,2048]{1,0:T(8,128)(2,1)S(1)} %collective-permute-done.19.w1_hbm, ...), custom_call_target="tpu_custom_call" | custom-call | tf_op jit(solution)/shard_map/pallas_call | solution.py:264
  188.2 1.4 collective-permute-done.31
  189.6 1.2 add_convert_fusion
  190.8 0.7 copy-done.1
  191.5 4.0 %shard_map.109.refs_0_ = f32[4,8,2,2,8,640]{5,4,3,2,1,0:T(8,128)} custom-call(s32[1]{0:T(128)} %bitcast.4.who, bf16[512,2048]{1,0:T(8,128)(2,1)} %bitcast.21.x_ref, bf16[2048,640]{1,0:T(8,128)(2,1)S(1)} %copy-done.1), custom_call_target="tpu_custom_call" | custom-call | flops 1342177280 | bytes 6291456 | tf_op jit(solution)/shard_map/pallas_call | solution.py:289
  195.5 4.0 %shard_map.110 = f32[4,8,2,2,8,640]{5,4,3,2,1,0:T(8,128)} custom-call(s32[1]{0:T(128)S(6)} %sub.3.who, bf16[512,2048]{1,0:T(8,128)(2,1)} %collective-permute-done.32.x_ref, bf16[2048,640]{1,0:T(8,128)(2,1)S(1)} %copy-done.1, f32[4,8,2,2,8,640]{5,4,3,2,1,0:T(8,128)} %shard_map.109.refs_0_), custom_call_target="tpu_custom_call", output_to_operand_aliasing={{}: (3, {})} | custom-call | flops 1342177280 | bytes 6291456 | tf_op jit(solution)/shard_map/pallas_call | solution.py:289
  (107 shorter events, 2.7 us)
Async XLA Ops:
  7.2 23.2 %copy-start.9 = (bf16[128,2048]{1,0:T(8,128)(2,1)S(1)}, bf16[128,2048]{1,0:T(8,128)(2,1)}, u32[]{:S(2)}) copy-start(bf16[128,2048]{1,0:T(8,128)(2,1)} %param.9) | copy-start | bytes 1572868
  7.2 61.3 %all-gather.2.cloned.1.call-start = ((), (), s32[]{:S(2)}) async-start(), calls=%async_computation.2 | async-start | bytes 2359296 | tf_op jit(solution)/shard_map/all_gather | solution.py:337
  10.9 4.4 %collective-permute-start = (bf16[128,512]{1,0:T(8,128)(2,1)S(1)}, bf16[128,512]{1,0:T(8,128)(2,1)S(1)}, u32[]{:S(2)}, u32[]{:S(2)}) collective-permute-start(bf16[128,512]{1,0:T(8,128)(2,1)S(1)} %get-tuple-element.79), channel_id=1, source_target_pairs={{0,4},{4,0},{1,5},{5,1},{2,6},{6,2},{3,7},{7,3},{8,12},{12,8},{9,1... | collective-permute-start | bytes 393224 | tf_op jit(solution)/shard_map/ppermute | solution.py:327
  15.3 28.5 %copy-start.14 = (bf16[256,512]{1,0:T(8,128)(2,1)}, bf16[256,512]{1,0:T(8,128)(2,1)S(1)}, u32[]{:S(2)}) copy-start(bf16[256,512]{1,0:T(8,128)(2,1)S(1)} %pad_maximum_fusion.3.refs_5_) | copy-start | bytes 786436
  15.3 11.5 %collective-permute-start.1 = (bf16[256,512]{1,0:T(8,128)(2,1)S(1)}, bf16[256,512]{1,0:T(8,128)(2,1)S(1)}, u32[]{:S(2)}, u32[]{:S(2)}) collective-permute-start(bf16[256,512]{1,0:T(8,128)(2,1)S(1)} %pad_maximum_fusion.3.refs_5_), channel_id=1, source_target_pairs={{0,8},{8,16},{16,24},{24,32},{32,40},{40,48},{48,56},{56,0},{1,9},... | collective-permute-start | bytes 786440 | tf_op jit(solution)/shard_map/ppermute | solution.py:327
  17.8 9.0 %collective-permute-start.4 = (bf16[256,512]{1,0:T(8,128)(2,1)S(1)}, bf16[256,512]{1,0:T(8,128)(2,1)S(1)}, u32[]{:S(2)}, u32[]{:S(2)}) collective-permute-start(bf16[256,512]{1,0:T(8,128)(2,1)S(1)} %pad_maximum_fusion.3.refs_5_), channel_id=1, source_target_pairs={{0,56},{8,0},{16,8},{24,16},{32,24},{40,32},{48,40},{56,48},{1,57}... | collective-permute-start | bytes 786440 | tf_op jit(solution)/shard_map/ppermute | solution.py:327
  21.8 15.7 %collective-permute-start.7 = (bf16[128,2048]{1,0:T(8,128)(2,1)}, bf16[128,2048]{1,0:T(8,128)(2,1)S(1)}, u32[]{:S(2)}, u32[]{:S(2)}) collective-permute-start(bf16[128,2048]{1,0:T(8,128)(2,1)} %refs_0_.1), channel_id=1, source_target_pairs={{0,192},{64,0},{128,64},{192,128},{1,193},{65,1},{129,65},{193,129... | collective-permute-start | bytes 1572872 | tf_op jit(solution)/shard_map/ppermute | solution.py:327
  24.6 12.8 %collective-permute-start.8 = (bf16[128,2048]{1,0:T(8,128)(2,1)}, bf16[128,2048]{1,0:T(8,128)(2,1)S(1)}, u32[]{:S(2)}, u32[]{:S(2)}) collective-permute-start(bf16[128,2048]{1,0:T(8,128)(2,1)} %refs_0_.1), channel_id=1, source_target_pairs={{0,64},{64,128},{128,192},{192,0},{1,65},{65,129},{129,193},{193,1... | collective-permute-start | bytes 1572872 | tf_op jit(solution)/shard_map/ppermute | solution.py:327
  26.8 17.0 %copy-start.15 = (bf16[256,512]{1,0:T(8,128)(2,1)}, bf16[256,512]{1,0:T(8,128)(2,1)S(1)}, u32[]{:S(2)}) copy-start(bf16[256,512]{1,0:T(8,128)(2,1)S(1)} %collective-permute-done.1.refs_6_) | copy-start | bytes 786436
  26.8 13.5 %collective-permute-start.2 = (bf16[256,512]{1,0:T(8,128)(2,1)S(1)}, bf16[256,512]{1,0:T(8,128)(2,1)S(1)}, u32[]{:S(2)}, u32[]{:S(2)}) collective-permute-start(bf16[256,512]{1,0:T(8,128)(2,1)S(1)} %collective-permute-done.1.refs_6_), channel_id=1, source_target_pairs={{0,8},{8,16},{16,24},{24,32},{32,40},{40,48},{48,56},{56,0},{1,9},... | collective-permute-start | bytes 786440 | tf_op jit(solution)/shard_map/ppermute | solution.py:327
  26.8 17.0 %copy-start.16 = (bf16[256,512]{1,0:T(8,128)(2,1)}, bf16[256,512]{1,0:T(8,128)(2,1)S(1)}, u32[]{:S(2)}) copy-start(bf16[256,512]{1,0:T(8,128)(2,1)S(1)} %collective-permute-done.4.refs_7_) | copy-start | bytes 786436
  26.8 13.5 %collective-permute-start.5 = (bf16[256,512]{1,0:T(8,128)(2,1)S(1)}, bf16[256,512]{1,0:T(8,128)(2,1)S(1)}, u32[]{:S(2)}, u32[]{:S(2)}) collective-permute-start(bf16[256,512]{1,0:T(8,128)(2,1)S(1)} %collective-permute-done.4.refs_7_), channel_id=1, source_target_pairs={{0,56},{8,0},{16,8},{24,16},{32,24},{40,32},{48,40},{56,48},{1,57}... | collective-permute-start | bytes 786440 | tf_op jit(solution)/shard_map/ppermute | solution.py:327
  37.4 7.9 %copy-start.23 = (bf16[128,2048]{1,0:T(8,128)(2,1)}, bf16[128,2048]{1,0:T(8,128)(2,1)S(1)}, u32[]{:S(2)}) copy-start(bf16[128,2048]{1,0:T(8,128)(2,1)S(1)} %collective-permute-done.8.refs_2_) | copy-start | bytes 1572868
  37.4 18.9 %copy-start.19 = (bf16[4,2048]{1,0:T(4,128)(2,1)S(1)}, bf16[4,2048]{1,0:T(4,128)(2,1)}, u32[]{:S(2)}) copy-start(bf16[4,2048]{1,0:T(4,128)(2,1)} %param.10) | copy-start | bytes 49156
  37.4 15.9 %collective-permute-start.9 = (bf16[64,2048]{1,0:T(8,128)(2,1)S(1)}, bf16[64,2048]{1,0:T(8,128)(2,1)S(1)}, u32[]{:S(2)}, u32[]{:S(2)}) collective-permute-start(bf16[64,2048]{1,0:T(8,128)(2,1)S(1)} %slice.153), channel_id=1, source_target_pairs={{0,64},{64,128},{128,192},{192,0},{1,65},{65,129},{129,193},{193,1... | collective-permute-start | bytes 786440 | tf_op jit(solution)/shard_map/ppermute | solution.py:327
  37.5 15.8 %copy-start.22 = (bf16[128,2048]{1,0:T(8,128)(2,1)}, bf16[128,2048]{1,0:T(8,128)(2,1)S(1)}, u32[]{:S(2)}) copy-start(bf16[128,2048]{1,0:T(8,128)(2,1)S(1)} %collective-permute-done.7.refs_1_) | copy-start | bytes 1572868
  37.6 15.8 %collective-permute-start.10 = (bf16[64,2048]{1,0:T(8,128)(2,1)S(1)}, bf16[64,2048]{1,0:T(8,128)(2,1)S(1)}, u32[]{:S(2)}, u32[]{:S(2)}) collective-permute-start(bf16[64,2048]{1,0:T(8,128)(2,1)S(1)} %slice.154), channel_id=1, source_target_pairs={{0,192},{64,0},{128,64},{192,128},{1,193},{65,1},{129,65},{193,129... | collective-permute-start | bytes 786440 | tf_op jit(solution)/shard_map/ppermute | solution.py:327
  40.3 21.2 %copy-start.17 = (bf16[256,512]{1,0:T(8,128)(2,1)}, bf16[256,512]{1,0:T(8,128)(2,1)S(1)}, u32[]{:S(2)}) copy-start(bf16[256,512]{1,0:T(8,128)(2,1)S(1)} %collective-permute-done.2.refs_8_) | copy-start | bytes 786436
  40.3 12.9 %collective-permute-start.3 = (bf16[256,512]{1,0:T(8,128)(2,1)S(1)}, bf16[256,512]{1,0:T(8,128)(2,1)S(1)}, u32[]{:S(2)}, u32[]{:S(2)}) collective-permute-start(bf16[256,512]{1,0:T(8,128)(2,1)S(1)} %collective-permute-done.2.refs_8_), channel_id=1, source_target_pairs={{0,8},{8,16},{16,24},{24,32},{32,40},{40,48},{48,56},{56,0},{1,9},... | collective-permute-start | bytes 786440 | tf_op jit(solution)/shard_map/ppermute | solution.py:327
  40.3 21.2 %copy-start.18 = (bf16[256,512]{1,0:T(8,128)(2,1)}, bf16[256,512]{1,0:T(8,128)(2,1)S(1)}, u32[]{:S(2)}) copy-start(bf16[256,512]{1,0:T(8,128)(2,1)S(1)} %collective-permute-done.5.refs_9_) | copy-start | bytes 786436
  40.3 12.9 %collective-permute-start.6 = (bf16[256,512]{1,0:T(8,128)(2,1)S(1)}, bf16[256,512]{1,0:T(8,128)(2,1)S(1)}, u32[]{:S(2)}, u32[]{:S(2)}) collective-permute-start(bf16[256,512]{1,0:T(8,128)(2,1)S(1)} %collective-permute-done.5.refs_9_), channel_id=1, source_target_pairs={{0,56},{8,0},{16,8},{24,16},{32,24},{40,32},{48,40},{56,48},{1,57}... | collective-permute-start | bytes 786440 | tf_op jit(solution)/shard_map/ppermute | solution.py:327
  45.3 28.3 %collective-permute-start.11 = (bf16[1280,512]{1,0:T(8,128)(2,1)}, bf16[1280,512]{1,0:T(8,128)(2,1)}, u32[]{:S(2)}, u32[]{:S(2)}) collective-permute-start(bf16[1280,512]{1,0:T(8,128)(2,1)} %constant_dynamic-update-slice_fusion.2), channel_id=1, source_target_pairs={{0,2},{2,0},{1,3},{3,1},{4,6},{6,4},{5,7},{7,5},{8,10},{10,8},{9,1... | collective-permute-start | bytes 3932168 | tf_op jit(solution)/shard_map/ppermute | solution.py:327
  53.2 14.6 %copy-start.12 = (bf16[256,512]{1,0:T(8,128)(2,1)}, bf16[256,512]{1,0:T(8,128)(2,1)S(1)}, u32[]{:S(2)}) copy-start(bf16[256,512]{1,0:T(8,128)(2,1)S(1)} %collective-permute-done.3.refs_11_) | copy-start | bytes 786436
  53.3 17.0 %copy-start.13 = (bf16[256,512]{1,0:T(8,128)(2,1)}, bf16[256,512]{1,0:T(8,128)(2,1)S(1)}, u32[]{:S(2)}) copy-start(bf16[256,512]{1,0:T(8,128)(2,1)S(1)} %collective-permute-done.6.refs_12_) | copy-start | bytes 786436
  53.3 8.1 %copy-start.25 = (bf16[64,2048]{1,0:T(8,128)(2,1)}, bf16[64,2048]{1,0:T(8,128)(2,1)S(1)}, u32[]{:S(2)}) copy-start(bf16[64,2048]{1,0:T(8,128)(2,1)S(1)} %collective-permute-done.9.refs_3_) | copy-start | bytes 786436
  53.3 8.1 %copy-start.26 = (bf16[64,2048]{1,0:T(8,128)(2,1)}, bf16[64,2048]{1,0:T(8,128)(2,1)S(1)}, u32[]{:S(2)}) copy-start(bf16[64,2048]{1,0:T(8,128)(2,1)S(1)} %collective-permute-done.10.refs_4_) | copy-start | bytes 786436
  53.4 8.1 %collective-permute-start.12 = (bf16[128,512]{1,0:T(8,128)(2,1)S(1)}, bf16[128,512]{1,0:T(8,128)(2,1)S(1)}, u32[]{:S(2)}, u32[]{:S(2)}) collective-permute-start(bf16[128,512]{1,0:T(8,128)(2,1)S(1)} %slice.151), channel_id=1, source_target_pairs={{0,8},{8,16},{16,24},{24,32},{32,40},{40,48},{48,56},{56,0},{1,9},... | collective-permute-start | bytes 393224 | tf_op jit(solution)/shard_map/ppermute | solution.py:327
  53.4 8.0 %collective-permute-start.13 = (bf16[128,512]{1,0:T(8,128)(2,1)S(1)}, bf16[128,512]{1,0:T(8,128)(2,1)S(1)}, u32[]{:S(2)}, u32[]{:S(2)}) collective-permute-start(bf16[128,512]{1,0:T(8,128)(2,1)S(1)} %slice.152), channel_id=1, source_target_pairs={{0,56},{8,0},{16,8},{24,16},{32,24},{40,32},{48,40},{56,48},{1,57}... | collective-permute-start | bytes 393224 | tf_op jit(solution)/shard_map/ppermute | solution.py:327
  61.4 5.4 %copy-start.20 = (bf16[128,512]{1,0:T(8,128)(2,1)}, bf16[128,512]{1,0:T(8,128)(2,1)S(1)}, u32[]{:S(2)}) copy-start(bf16[128,512]{1,0:T(8,128)(2,1)S(1)} %collective-permute-done.12.refs_13_) | copy-start | bytes 393220
  61.4 8.9 %copy-start.21 = (bf16[128,512]{1,0:T(8,128)(2,1)}, bf16[128,512]{1,0:T(8,128)(2,1)S(1)}, u32[]{:S(2)}) copy-start(bf16[128,512]{1,0:T(8,128)(2,1)S(1)} %collective-permute-done.13.refs_14_) | copy-start | bytes 393220
  61.5 12.0 %collective-permute-start.14 = (bf16[768,512]{1,0:T(8,128)(2,1)S(1)}, bf16[768,512]{1,0:T(8,128)(2,1)}, u32[]{:S(2)}, u32[]{:S(2)}) collective-permute-start(bf16[768,512]{1,0:T(8,128)(2,1)S(1)} %pad_maximum_fusion.1), channel_id=1, source_target_pairs={{0,2},{2,0},{1,3},{3,1},{4,6},{6,4},{5,7},{7,5},{8,10},{10,8},{9,1... | collective-permute-start | bytes 2359304 | tf_op jit(solution)/shard_map/ppermute | solution.py:327
  70.3 42.5 %collective-permute-start.19 = (bf16[256,2048]{1,0:T(8,128)(2,1)S(1)}, bf16[256,2048]{1,0:T(8,128)(2,1)S(1)}, u32[]{:S(2)}, u32[]{:S(2)}) collective-permute-start(bf16[256,2048]{1,0:T(8,128)(2,1)S(1)} %get-tuple-element.69), channel_id=1, source_target_pairs={{0,4},{4,0},{1,5},{5,1},{2,6},{6,2},{3,7},{7,3},{8,12},{12,8},{9,1... | collective-permute-start | bytes 3145736 | tf_op jit(solution)/shard_map/ppermute | solution.py:327
  71.0 35.9 %copy-start.8 = (s32[4]{0:T(128)S(1)}, s32[4]{0:T(128)}, u32[]{:S(2)}) copy-start(s32[4]{0:T(128)} %pad_add_fusion.place) | copy-start | bytes 52
  71.0 41.8 %collective-permute-start.20 = (bf16[256,2048]{1,0:T(8,128)(2,1)S(1)}, bf16[256,2048]{1,0:T(8,128)(2,1)S(1)}, u32[]{:S(2)}, u32[]{:S(2)}) collective-permute-start(bf16[256,2048]{1,0:T(8,128)(2,1)S(1)} %get-tuple-element.68), channel_id=1, source_target_pairs={{0,5},{1,4},{4,1},{5,0},{2,7},{3,6},{6,3},{7,2},{8,13},{9,12},{12,... | collective-permute-start | bytes 3145736 | tf_op jit(solution)/shard_map/ppermute | solution.py:372
  73.6 39.3 %copy-start = (bf16[512,2048]{1,0:T(8,128)(2,1)S(1)}, bf16[512,2048]{1,0:T(8,128)(2,1)}, u32[]{:S(2)}) copy-start(bf16[512,2048]{1,0:T(8,128)(2,1)} %all-gather.2.cloned.1.call-done.w0_hbm) | copy-start | bytes 6291460
  97.4 6.0 %collective-permute-start.15 = (bf16[32,2048]{1,0:T(8,128)(2,1)}, bf16[32,2048]{1,0:T(8,128)(2,1)S(1)}, u32[]{:S(2)}, u32[]{:S(2)}) collective-permute-start(bf16[32,2048]{1,0:T(8,128)(2,1)} %get-tuple-element.43), channel_id=1, source_target_pairs={{0,64},{64,128},{128,192},{192,0},{1,65},{65,129},{129,193},{193,1... | collective-permute-start | bytes 393224 | tf_op jit(solution)/shard_map/ppermute | solution.py:327
  99.1 7.7 %collective-permute-start.16 = (bf16[32,2048]{1,0:T(8,128)(2,1)}, bf16[32,2048]{1,0:T(8,128)(2,1)S(1)}, u32[]{:S(2)}, u32[]{:S(2)}) collective-permute-start(bf16[32,2048]{1,0:T(8,128)(2,1)} %get-tuple-element.44), channel_id=1, source_target_pairs={{0,128},{64,192},{128,0},{192,64},{1,129},{65,193},{129,1},{193,65... | collective-permute-start | bytes 393224 | tf_op jit(solution)/shard_map/ppermute | solution.py:327
  101.5 5.4 %collective-permute-start.17 = (bf16[32,2048]{1,0:T(8,128)(2,1)}, bf16[32,2048]{1,0:T(8,128)(2,1)S(1)}, u32[]{:S(2)}, u32[]{:S(2)}) collective-permute-start(bf16[32,2048]{1,0:T(8,128)(2,1)} %get-tuple-element.45), channel_id=1, source_target_pairs={{0,192},{64,0},{128,64},{192,128},{1,193},{65,1},{129,65},{193,129... | collective-permute-start | bytes 393224 | tf_op jit(solution)/shard_map/ppermute | solution.py:327
  106.9 0.9 copy-start.7
  108.5 4.3 %collective-permute-start.18 = (bf16[2,16,512]{2,1,0:T(8,128)(2,1)S(1)}, bf16[2,16,512]{2,1,0:T(8,128)(2,1)S(1)}, u32[]{:S(2)}, u32[]{:S(2)}) collective-permute-start(bf16[2,16,512]{2,1,0:T(8,128)(2,1)S(1)} %get-tuple-element.48), channel_id=1, source_target_pairs={{0,2},{2,0},{1,3},{3,1},{4,6},{6,4},{5,7},{7,5},{8,10},{10,8},{9,1... | collective-permute-start | bytes 98312 | tf_op jit(solution)/shard_map/ppermute | solution.py:327
  110.7 11.2 %collective-permute-start.25 = (bf16[80,2048]{1,0:T(8,128)(2,1)}, bf16[80,2048]{1,0:T(8,128)(2,1)}, u32[]{:S(2)}, u32[]{:S(2)}) collective-permute-start(bf16[80,2048]{1,0:T(8,128)(2,1)} %get-tuple-element.54), channel_id=1, source_target_pairs={{0,192},{64,0},{128,64},{192,128},{1,193},{65,1},{129,65},{193,129... | collective-permute-start | bytes 983048 | tf_op jit(solution)/shard_map/ppermute | solution.py:327
  112.8 9.1 %collective-permute-start.23 = (bf16[64,2048]{1,0:T(8,128)(2,1)}, bf16[64,2048]{1,0:T(8,128)(2,1)}, u32[]{:S(2)}, u32[]{:S(2)}) collective-permute-start(bf16[64,2048]{1,0:T(8,128)(2,1)} %get-tuple-element.53), channel_id=1, source_target_pairs={{0,64},{64,128},{128,192},{192,0},{1,65},{65,129},{129,193},{193,1... | collective-permute-start | bytes 786440 | tf_op jit(solution)/shard_map/ppermute | solution.py:327
  112.9 1.8 copy-start.2
  112.9 11.9 %copy-start.24 = (f32[2048]{0:T(1024)S(1)}, f32[2048]{0:T(1024)}, u32[]{:S(2)}) copy-start(f32[2048]{0:T(1024)} %param.16) | copy-start | bytes 24580
  114.7 9.9 %collective-permute-start.21 = (bf16[16,2048]{1,0:T(8,128)(2,1)S(1)}, bf16[16,2048]{1,0:T(8,128)(2,1)S(1)}, u32[]{:S(2)}, u32[]{:S(2)}) collective-permute-start(bf16[16,2048]{1,0:T(8,128)(2,1)S(1)} %get-tuple-element.50), channel_id=1, source_target_pairs={{0,2},{2,0},{1,3},{3,1},{4,6},{6,4},{5,7},{7,5},{8,10},{10,8},{9,1... | collective-permute-start | bytes 196616 | tf_op jit(solution)/shard_map/ppermute | solution.py:327
  115.9 26.2 %collective-permute-start.22 = (bf16[144,2048]{1,0:T(8,128)(2,1)}, bf16[144,2048]{1,0:T(8,128)(2,1)}, u32[]{:S(2)}, u32[]{:S(2)}) collective-permute-start(bf16[144,2048]{1,0:T(8,128)(2,1)} %get-tuple-element.52), channel_id=1, source_target_pairs={{0,64},{64,128},{128,192},{192,0},{1,65},{65,129},{129,193},{193,1... | collective-permute-start | bytes 1769480 | tf_op jit(solution)/shard_map/ppermute | solution.py:327
  116.6 25.6 %collective-permute-start.27 = (bf16[144,2048]{1,0:T(8,128)(2,1)}, bf16[144,2048]{1,0:T(8,128)(2,1)}, u32[]{:S(2)}, u32[]{:S(2)}) collective-permute-start(bf16[144,2048]{1,0:T(8,128)(2,1)} %get-tuple-element.55), channel_id=1, source_target_pairs={{0,192},{64,0},{128,64},{192,128},{1,193},{65,1},{129,65},{193,129... | collective-permute-start | bytes 1769480 | tf_op jit(solution)/shard_map/ppermute | solution.py:327
  121.9 18.3 %collective-permute-start.24 = (bf16[64,2048]{1,0:T(8,128)(2,1)}, bf16[64,2048]{1,0:T(8,128)(2,1)}, u32[]{:S(2)}, u32[]{:S(2)}) collective-permute-start(bf16[64,2048]{1,0:T(8,128)(2,1)} %collective-permute-done.23), channel_id=1, source_target_pairs={{0,64},{64,128},{128,192},{192,0},{1,65},{65,129},{129,193},{193,1... | collective-permute-start | bytes 786440 | tf_op jit(solution)/shard_map/ppermute | solution.py:327
  121.9 18.3 %collective-permute-start.26 = (bf16[80,2048]{1,0:T(8,128)(2,1)}, bf16[80,2048]{1,0:T(8,128)(2,1)}, u32[]{:S(2)}, u32[]{:S(2)}) collective-permute-start(bf16[80,2048]{1,0:T(8,128)(2,1)} %collective-permute-done.25), channel_id=1, source_target_pairs={{0,192},{64,0},{128,64},{192,128},{1,193},{65,1},{129,65},{193,129... | collective-permute-start | bytes 983048 | tf_op jit(solution)/shard_map/ppermute | solution.py:327
  125.5 16.6 %all-to-all-start = ((bf16[8,8,2048]{2,1,0:T(8,128)(2,1)}), bf16[8,8,2048]{2,1,0:T(8,128)(2,1)S(1)}, u32[]{:S(2)}, u32[]{:S(2)}) async-start(bf16[8,8,2048]{2,1,0:T(8,128)(2,1)} %broadcast_in_dim.4), calls=%async_computation | async-start | bytes 524288 | tf_op jit(solution)/shard_map/all_to_all | solution.py:378
  143.7 28.6 %all-to-all-start.1 = ((bf16[8,64,2048]{2,1,0:T(8,128)(2,1)}), bf16[8,64,2048]{2,1,0:T(8,128)(2,1)}, u32[]{:S(2)}, u32[]{:S(2)}) async-start(bf16[8,64,2048]{2,1,0:T(8,128)(2,1)} %broadcast_in_dim.5), calls=%async_computation.1 | async-start | bytes 4194304 | tf_op jit(solution)/shard_map/all_to_all | solution.py:378
  149.9 35.1 %collective-permute-start.29 = (bf16[3,2048]{1,0:T(4,128)(2,1)S(1)}, bf16[3,2048]{1,0:T(4,128)(2,1)S(1)}, u32[]{:S(2)}, u32[]{:S(2)}) collective-permute-start(bf16[3,2048]{1,0:T(4,128)(2,1)S(1)} %get-tuple-element.85), channel_id=1, source_target_pairs={{2,0},{4,2},{6,4},{8,6},{10,8},{12,10},{14,12},{16,14},{18,16},{20... | collective-permute-start | bytes 36872 | tf_op jit(solution)/shard_map/ppermute | solution.py:319
  172.3 23.2 %collective-permute-start.32 = (bf16[512,2048]{1,0:T(8,128)(2,1)}, bf16[512,2048]{1,0:T(8,128)(2,1)}, u32[]{:S(2)}, u32[]{:S(2)}) collective-permute-start(bf16[512,2048]{1,0:T(8,128)(2,1)} %bitcast.21.x_ref), channel_id=1, source_target_pairs={{0,2},{2,0},{1,3},{3,1},{4,6},{6,4},{5,7},{7,5},{8,10},{10,8},{9,1... | collective-permute-start | bytes 6291464 | tf_op jit(solution)/shard_map/ppermute | solution.py:327
  176.2 1.1 copy-start.4
  177.2 1.0 copy-start.5
  178.3 1.1 copy-start.6
  179.4 5.7 %copy-start.10 = (bf16[128,2048]{1,0:T(8,128)(2,1)S(1)}, bf16[128,2048]{1,0:T(8,128)(2,1)}, u32[]{:S(2)}) copy-start(bf16[128,2048]{1,0:T(8,128)(2,1)} %param.9) | copy-start | bytes 1572868
  179.4 5.7 %copy-start.11 = (bf16[64,2048]{1,0:T(8,128)(2,1)S(1)}, bf16[64,2048]{1,0:T(8,128)(2,1)}, u32[]{:S(2)}) copy-start(bf16[64,2048]{1,0:T(8,128)(2,1)} %get-tuple-element.71) | copy-start | bytes 786436
  179.4 5.8 %copy-start.3 = (bf16[256,2048]{1,0:T(8,128)(2,1)S(1)}, bf16[256,2048]{1,0:T(8,128)(2,1)}, u32[]{:S(2)}) copy-start(bf16[256,2048]{1,0:T(8,128)(2,1)} %copy-done.2) | copy-start | bytes 3145732
  182.0 3.1 %collective-permute-start.30 = (bf16[2,128,512]{2,1,0:T(8,128)(2,1)S(1)}, bf16[2,128,512]{2,1,0:T(8,128)(2,1)S(1)}, u32[]{:S(2)}, u32[]{:S(2)}) collective-permute-start(bf16[2,128,512]{2,1,0:T(8,128)(2,1)S(1)} %get-tuple-element.62), channel_id=1, source_target_pairs={{0,2},{2,0},{1,3},{3,1},{4,6},{6,4},{5,7},{7,5},{8,10},{10,8},{9,1... | collective-permute-start | bytes 786440 | tf_op jit(solution)/shard_map/ppermute | solution.py:327
  182.1 5.5 %collective-permute-start.28 = (bf16[3,2048]{1,0:T(4,128)(2,1)S(1)}, bf16[3,2048]{1,0:T(4,128)(2,1)S(1)}, u32[]{:S(2)}, u32[]{:S(2)}) collective-permute-start(bf16[3,2048]{1,0:T(4,128)(2,1)S(1)} %get-tuple-element.84), channel_id=1, source_target_pairs={{0,2},{2,4},{4,6},{6,8},{8,10},{10,12},{12,14},{14,16},{16,18},{18... | collective-permute-start | bytes 36872 | tf_op jit(solution)/shard_map/ppermute | solution.py:318
  187.6 2.0 collective-permute-start.31
  189.6 1.9 copy-start.1
Sparse Core Ops, SparseCore 0:
  9.8 51.5 all-gather.1

commit v3 on v2

--- a/solution.py
+++ b/solution.py
@@ -15,7 +15,7 @@
 TEAM = NX * NC
 SPAN = NZ * NX * NC * HALF
 NEG = -1e30
-BK, HB = 1024, 4
+BK, HB = 1024, 8
 BF = jnp.bfloat16
 F32 = jnp.float32
 
@@ -336,7 +336,7 @@
 
     w_own = lax.all_gather(out_weight, "z", axis=0, tiled=True)
 
-    kv_own = jnp.concatenate([keys, values], 1)
+    kv_own = lax.optimization_barrier(jnp.concatenate([keys, values], 1))
     q_up, q_down = shift(queries, "y", -1), shift(queries, "y", 1)
     q_far = [shift(q_down[:HALF], "y", 1), shift(q_up[HALF:], "y", -1)]
     pair = jnp.concatenate([kv_own, shift(kv_own, "xl", 1)], 0)
@@ -345,14 +345,22 @@
     fwd = bwd = pair
     for s in range(1, NZ // 2):
         fwd, bwd = shift(fwd, "z", 1), shift(bwd, "z", -1)
-        held += [(fwd, both(-s)), (bwd, both(s))]
-    fwd, bwd = fwd[:tok], bwd[tok:]
-    fwd, bwd, q_up, q_down, *q_far = lax.optimization_barrier((fwd, bwd, q_up, q_down, *q_far))
-    held += [(shift(fwd, "z", 1), both(4)[:1]), (shift(bwd, "z", -1), both(4)[1:])]
+        if s < NZ // 2 - 1:
+            held += [(fwd, both(-s)), (bwd, both(s))]
+    taps = conv_weight.astype(F32)
+    blocks = resid.reshape(8, 16, width)
+    conv_few = sum(taps[t] * blocks[:, 15 - t].astype(F32) for t in range(conv_weight.shape[0]))
+    hidden_few = (blocks[:, 15].astype(F32) + jax.nn.silu(conv_few)).astype(BF)
+    g_few = few(gates)
+    fwd, bwd, q_up, q_down, hidden_few, g_few, place, *q_far = lax.optimization_barrier(
+        (fwd, bwd, q_up, q_down, hidden_few, g_few, place, *q_far)
+    )
+    held += [(fwd, both(1 - NZ // 2)), (bwd, both(NZ // 2 - 1))]
+    held += [(shift(fwd[:tok], "z", 1), both(4)[:1]), (shift(bwd[tok:], "z", -1), both(4)[1:])]
     q_team = [queries, q_up, q_down] + q_far
 
     kv = []
-    for group in (held[:5], held[5:]):
+    for group in (held[:7], held[7:]):
         entries, at = [], 0
         for piece, spans in group:
             kv.append((piece, [(i * tok, e) for i, e in enumerate(spans)]))
@@ -361,39 +369,41 @@
                 at += n
         kv.append((shift(jnp.concatenate([p for p, _ in group], 0), "c", 1), entries))
 
-    blocks = resid.reshape(8, 16, width)
-    taps = conv_weight.astype(F32)
-    conv_few = sum(taps[t] * blocks[:, 15 - t].astype(F32) for t in range(conv_weight.shape[0]))
-    hidden_few = (blocks[:, 15].astype(F32) + jax.nn.silu(conv_few)).astype(BF)
-    g_few = few(gates)
     half_w = w_own.shape[0] // 2
     w_other = [
         shift(w_own[:half_w], "xl", 1),
         lax.ppermute(w_own[half_w:], ("xl", "dp"), [(i, 3 - i) for i in range(4)]),
     ]
-    place, hidden_few, g_few, _ = lax.optimization_barrier((place, hidden_few, g_few, w_own))
+    place, _ = lax.optimization_barrier((place, w_own))
     got = attention(place, q_team, kv)
     main, lead = got[: NY + 1], got[NY + 1 :]
     to_team = lambda a: [a[0], shift(a[1], "y", 1), shift(a[2], "y", 2), shift(a[3], "y", -1)]
     spread = lambda a, axes, n: lax.all_to_all(jnp.broadcast_to(a[None], (n,) + a.shape), axes, 0, 0).reshape(-1, width)
 
     lead = to_team(lead)
-    far = [shift(shift(main[2], "y", 1), "y", 1), shift(shift(main[4], "y", -1), "y", -1)]
-    main = [main[0], shift(main[1], "y", 1), jnp.concatenate(far, 0), shift(main[3], "y", -1)]
     f_keep, f_send = join(place, lead, g_few)
     f_own, f_other = project(f_keep, shift(f_send, "c", 1), w_own, *w_other)
-    rows = (hidden_few.astype(F32) + (f_own + shift(f_other, "c", 1).astype(F32))[:8]).astype(BF).astype(F32)
+    far = [shift(main[2], "y", 1), shift(main[4], "y", -1)]
+    f_other = shift(f_other, "c", 1)
+    lag = conv_weight.shape[0] - 1
+    rims = jnp.concatenate([resid[HALF - lag : HALF], resid[2 * HALF - lag :]], 0)
+    f_other, rims, *far = lax.optimization_barrier((f_other, rims, *far))
+    far = [shift(far[0], "y", 1), shift(far[1], "y", -1)]
+    near = [shift(main[1], "y", 1), shift(main[3], "y", -1)]
+    rows = (hidden_few.astype(F32) + (f_own + f_other.astype(F32))[:8]).astype(BF).astype(F32)
     normed = (rows * lax.rsqrt(jnp.mean(rows * rows, axis=-1, keepdims=True) + 1e-6) * norm_gain).astype(BF)
     per_z = spread(normed, "z", NZ)
-    lag = conv_weight.shape[0] - 1
-    rims = jnp.concatenate([resid[HALF - lag : HALF], resid[2 * HALF - lag :]], 0)
-    per_z, rims, *main = lax.optimization_barrier((per_z, rims, *main))
-    every = spread(per_z, ("y", "xl"), NY * NX)
+    per_z, *near = lax.optimization_barrier((per_z, *near))
+    copies = jnp.broadcast_to(per_z[None], (NY * NX,) + per_z.shape)
+    _, *far = lax.optimization_barrier((copies, *far))
+    main = [main[0], near[0], jnp.concatenate(far, 0), near[1]]
+    every = lax.all_to_all(copies, ("y", "xl"), 0, 0).reshape(-1, width)
 
     hidden = hidden_rows(resid, rims, conv_weight, me, NY * NZ * NX * NC - 1)
     keep, send = join(place, main, gates)
     p_own, p_other = project(keep, shift(send, "c", 1), w_own, *w_other)
     mixed = (hidden.astype(F32) + p_own + shift(p_other, "c", 1).astype(F32)).astype(BF)
+    every, mixed = lax.optimization_barrier((every, mixed))
 
     theirs = shift(every, "c", 1)
     who = c.astype(jnp.int32).reshape(1)

time: 208 us -> 182 us (0.88)
  waiting for transfers between devices: 51.8 us -> 39.3 us
  starting transfers between devices: 76.3 us -> 67 us
  Pallas kernels: 39.5 us -> 36.8 us
    all_to_all x2 -> x1, waiting for transfers between devices: 17.8 us -> 1.67 us  [body(): lax.all_to_all(jnp.broadcast_to(a[None], (n,) + a.shape), axes, 0, 0)]
    all_to_all x0 -> x1, waiting for transfers between devices: none -> 10.6 us  [body(): every = lax.all_to_all(copies, ('y', 'xl'), 0, 0).reshape(-1, width)]
    ppermute x30, starting transfers between devices: 55.8 us -> 46.6 us  [shift(): return lax.ppermute(x, axis, [(i, (i + by) % count) for i in range(count)])]
    ppermute x30, waiting for transfers between devices: 33.3 us -> 27 us  [shift(): return lax.ppermute(x, axis, [(i, (i + by) % count) for i in range(count)])]
    all_to_all x0 -> x1, starting transfers between devices: none -> 5.1 us  [body(): every = lax.all_to_all(copies, ('y', 'xl'), 0, 0).reshape(-1, width)]
    all_to_all x2 -> x1, starting transfers between devices: 10.4 us -> 6.76 us  [body(): lax.all_to_all(jnp.broadcast_to(a[None], (n,) + a.shape), axes, 0, 0)]
    unnamed x61 -> x68, local copies, waits for them, and re-layouts: 10.7 us -> 9.37 us
  transfers between devices with their start and end apart: 36 -> 36, of which waited for: 12 -> 15; matrix products, arithmetic and copies ran while one was open for 9% -> 11% of each run, Pallas kernels for 17% -> 19%
where the time goes in v3:
time: 182 us; the launch traced here: 181 us
  starting transfers between devices  67 us (37%)
  waiting for transfers between devices  39.3 us (22%)
  Pallas kernels  36.8 us (20%)
  local copies, waits for them, and re-layouts  18.7 us (10%)
  between operations  14.5 us (8%)
  other arithmetic  4.83 us (3%)
    ppermute x30, starting transfers between devices, shift(): return lax.ppermute(x, axis, [(i, (i + by) % count) for i in range(count)])  46.6 us
    ppermute x30, waiting for transfers between devices, shift(): return lax.ppermute(x, axis, [(i, (i + by) % count) for i in range(count)])  27 us
    pallas_call x1, Pallas kernels, attention(): pl.pallas_call(functools.partial(attention_kernel, layout), in_specs=[pl....  22.4 us
    all_to_all x1, waiting for transfers between devices, body(): every = lax.all_to_all(copies, ('y', 'xl'), 0, 0).reshape(-1, width)  10.6 us
    unnamed x68, local copies, waits for them, and re-layouts  9.37 us
    pallas_call x2, Pallas kernels, lens(): pl.pallas_call(lens_kernel, grid_spec=pltpu.PrefetchScalarGridSpec(num_sc...  6.85 us
    all_to_all x1, starting transfers between devices, body(): lax.all_to_all(jnp.broadcast_to(a[None], (n,) + a.shape), axes, 0, 0)  6.76 us
    all_to_all x1, starting transfers between devices, body(): every = lax.all_to_all(copies, ('y', 'xl'), 0, 0).reshape(-1, width)  5.1 us
  transfers between devices with their start and end apart: 36, of which 15 were waited for; matrix products, arithmetic and copies ran while one was open for 11% of the time, Pallas kernels for 19%

profile of v3, /device:TPU:1, one launch (start us, length us, event | category | flops | bytes accessed | tf_op | source)
XLA Modules:
  0.0 181.1 jit_solution(15361493427133249977)
XLA Ops:
  7.2 3.6 %collective-permute-start.7 = (bf16[128,2048]{1,0:T(8,128)(2,1)}, bf16[128,2048]{1,0:T(8,128)(2,1)S(1)}, u32[]{:S(2)}, u32[]{:S(2)}) collective-permute-start(bf16[128,2048]{1,0:T(8,128)(2,1)} %refs_0_.1), channel_id=1, source_target_pairs={{0,192},{64,0},{128,64},{192,128},{1,193},{65,1},{129,65},{193,129... | collective-permute-start | bytes 1572872 | tf_op jit(solution)/shard_map/ppermute | solution.py:327
  10.9 0.9 pad_maximum_fusion.4
  11.7 1.3 collective-permute-start
  13.1 1.6 fusion.19
  14.7 0.9 fusion.21
  16.0 1.7 collective-permute-start.1
  17.7 4.0 %collective-permute-start.4 = (bf16[256,512]{1,0:T(8,128)(2,1)S(1)}, bf16[256,512]{1,0:T(8,128)(2,1)S(1)}, u32[]{:S(2)}, u32[]{:S(2)}) collective-permute-start(bf16[256,512]{1,0:T(8,128)(2,1)S(1)} %pad_maximum_fusion.2.refs_5_), channel_id=1, source_target_pairs={{0,56},{8,0},{16,8},{24,16},{32,24},{40,32},{48,40},{56,48},{1,57}... | collective-permute-start | bytes 786440 | tf_op jit(solution)/shard_map/ppermute | solution.py:327
  21.8 0.7 constant_dynamic-update-slice_fusion.7
  22.5 3.9 %collective-permute-done.1.refs_6_ = bf16[256,512]{1,0:T(8,128)(2,1)S(1)} collective-permute-done((bf16[256,512]{1,0:T(8,128)(2,1)S(1)}, bf16[256,512]{1,0:T(8,128)(2,1)S(1)}, u32[]{:S(2)}, u32[]{:S(2)}) %collective-permute-start.1) | collective-permute-done | bytes 262176 | tf_op jit(solution)/shard_map/ppermute | solution.py:327
  26.5 2.7 %collective-permute-start.5 = (bf16[256,512]{1,0:T(8,128)(2,1)S(1)}, bf16[256,512]{1,0:T(8,128)(2,1)S(1)}, u32[]{:S(2)}, u32[]{:S(2)}) collective-permute-start(bf16[256,512]{1,0:T(8,128)(2,1)S(1)} %collective-permute-done.4.refs_7_), channel_id=1, source_target_pairs={{0,56},{8,0},{16,8},{24,16},{32,24},{40,32},{48,40},{56,48},{1,57}... | collective-permute-start | bytes 786440 | tf_op jit(solution)/shard_map/ppermute | solution.py:327
  29.7 1.0 slice.150
  30.7 0.7 constant_dynamic-update-slice_fusion.6
  31.4 0.7 constant_dynamic-update-slice_fusion.5
  32.2 2.5 %collective-permute-start.10 = (bf16[64,2048]{1,0:T(8,128)(2,1)S(1)}, bf16[64,2048]{1,0:T(8,128)(2,1)S(1)}, u32[]{:S(2)}, u32[]{:S(2)}) collective-permute-start(bf16[64,2048]{1,0:T(8,128)(2,1)S(1)} %slice.152), channel_id=1, source_target_pairs={{0,192},{64,0},{128,64},{192,128},{1,193},{65,1},{129,65},{193,129... | collective-permute-start | bytes 786440 | tf_op jit(solution)/shard_map/ppermute | solution.py:327
  34.8 2.5 %collective-permute-done.2.refs_8_ = bf16[256,512]{1,0:T(8,128)(2,1)S(1)} collective-permute-done((bf16[256,512]{1,0:T(8,128)(2,1)S(1)}, bf16[256,512]{1,0:T(8,128)(2,1)S(1)}, u32[]{:S(2)}, u32[]{:S(2)}) %collective-permute-start.2) | collective-permute-done | bytes 262176 | tf_op jit(solution)/shard_map/ppermute | solution.py:327
  37.3 0.7 collective-permute-done.5.refs_9_
  38.0 2.0 %collective-permute-start.6 = (bf16[256,512]{1,0:T(8,128)(2,1)S(1)}, bf16[256,512]{1,0:T(8,128)(2,1)S(1)}, u32[]{:S(2)}, u32[]{:S(2)}) collective-permute-start(bf16[256,512]{1,0:T(8,128)(2,1)S(1)} %collective-permute-done.5.refs_9_), channel_id=1, source_target_pairs={{0,56},{8,0},{16,8},{24,16},{32,24},{40,32},{48,40},{56,48},{1,57}... | collective-permute-start | bytes 786440 | tf_op jit(solution)/shard_map/ppermute | solution.py:327
  39.9 0.7 constant_dynamic-update-slice_fusion.4
  40.7 0.7 constant_dynamic-update-slice_fusion.3
  41.4 0.7 constant_dynamic-update-slice_fusion.2
  42.1 8.7 %collective-permute-done.3.refs_10_ = bf16[256,512]{1,0:T(8,128)(2,1)S(1)} collective-permute-done((bf16[256,512]{1,0:T(8,128)(2,1)S(1)}, bf16[256,512]{1,0:T(8,128)(2,1)S(1)}, u32[]{:S(2)}, u32[]{:S(2)}) %collective-permute-start.3) | collective-permute-done | bytes 262176 | tf_op jit(solution)/shard_map/ppermute | solution.py:327
  50.8 0.8 constant_dynamic-update-slice_fusion.1
  51.6 0.7 constant_dynamic-update-slice_fusion
  52.3 6.4 %collective-permute-start.11 = (bf16[1792,512]{1,0:T(8,128)(2,1)}, bf16[1792,512]{1,0:T(8,128)(2,1)}, u32[]{:S(2)}, u32[]{:S(2)}) collective-permute-start(bf16[1792,512]{1,0:T(8,128)(2,1)} %constant_dynamic-update-slice_fusion), channel_id=1, source_target_pairs={{0,2},{2,0},{1,3},{3,1},{4,6},{6,4},{5,7},{7,5},{8,10},{10,8},{9,1... | collective-permute-start | bytes 5505032 | tf_op jit(solution)/shard_map/ppermute | solution.py:327
  58.8 2.7 %collective-permute-start.13 = (bf16[128,512]{1,0:T(8,128)(2,1)S(1)}, bf16[128,512]{1,0:T(8,128)(2,1)S(1)}, u32[]{:S(2)}, u32[]{:S(2)}) collective-permute-start(bf16[128,512]{1,0:T(8,128)(2,1)S(1)} %slice.120), channel_id=1, source_target_pairs={{0,56},{8,0},{16,8},{24,16},{32,24},{40,32},{48,40},{56,48},{1,57}... | collective-permute-start | bytes 393224 | tf_op jit(solution)/shard_map/ppermute | solution.py:327
  61.5 3.7 %collective-permute-done.12.refs_13_ = bf16[128,512]{1,0:T(8,128)(2,1)S(1)} collective-permute-done((bf16[128,512]{1,0:T(8,128)(2,1)S(1)}, bf16[128,512]{1,0:T(8,128)(2,1)S(1)}, u32[]{:S(2)}, u32[]{:S(2)}) %collective-permute-start.12) | collective-permute-done | bytes 131104 | tf_op jit(solution)/shard_map/ppermute | solution.py:327
  65.4 1.1 collective-permute-start.14
  66.4 1.8 fusion.16
  68.3 1.3 collective-permute-start.19
  69.5 1.8 %collective-permute-start.20 = (bf16[256,2048]{1,0:T(8,128)(2,1)S(1)}, bf16[256,2048]{1,0:T(8,128)(2,1)S(1)}, u32[]{:S(2)}, u32[]{:S(2)}) collective-permute-start(bf16[256,2048]{1,0:T(8,128)(2,1)S(1)} %get-tuple-element.80), channel_id=1, source_target_pairs={{0,5},{1,4},{4,1},{5,0},{2,7},{3,6},{6,3},{7,2},{8,13},{9,12},{12,... | collective-permute-start | bytes 3145736 | tf_op jit(solution)/shard_map/ppermute | solution.py:375
  71.4 0.7 copy-done.29
  72.1 22.4 %shard_map.104 = (bf16[144,2048]{1,0:T(8,128)(2,1)}, bf16[144,2048]{1,0:T(8,128)(2,1)}, bf16[64,2048]{1,0:T(8,128)(2,1)}, bf16[144,2048]{1,0:T(8,128)(2,1)}, bf1...) custom-call(s32[4]{0:T(128)} %pad_add_fusion.place, ...), custom_call_target="tpu_custom_call" | custom-call | flops 10000000000 | bytes 8388608 | tf_op jit(solution)/shard_map/pallas_call | solution.py:167
  94.6 3.6 %collective-permute-start.16 = (bf16[32,2048]{1,0:T(8,128)(2,1)}, bf16[32,2048]{1,0:T(8,128)(2,1)S(1)}, u32[]{:S(2)}, u32[]{:S(2)}) collective-permute-start(bf16[32,2048]{1,0:T(8,128)(2,1)} %get-tuple-element.51), channel_id=1, source_target_pairs={{0,128},{64,192},{128,0},{192,64},{1,129},{65,193},{129,1},{193,65... | collective-permute-start | bytes 393224 | tf_op jit(solution)/shard_map/ppermute | solution.py:327
  98.2 0.9 fusion.17
  99.1 1.3 collective-permute-done.15.r1
  100.4 1.2 collective-permute-start.23
  101.6 2.5 %collective-permute-done.16.r2 = bf16[32,2048]{1,0:T(8,128)(2,1)S(1)} collective-permute-done((bf16[32,2048]{1,0:T(8,128)(2,1)}, bf16[32,2048]{1,0:T(8,128)(2,1)S(1)}, u32[]{:S(2)}, u32[]{:S(2)}) %collective-permute-start.16) | collective-permute-done | bytes 131104 | tf_op jit(solution)/shard_map/ppermute | solution.py:327
  104.2 0.9 copy-done.6
  105.1 0.8 shard_map.105
  105.9 2.2 %collective-permute-start.18 = (bf16[2,16,512]{2,1,0:T(8,128)(2,1)S(1)}, bf16[2,16,512]{2,1,0:T(8,128)(2,1)S(1)}, u32[]{:S(2)}, u32[]{:S(2)}) collective-permute-start(bf16[2,16,512]{2,1,0:T(8,128)(2,1)S(1)} %get-tuple-element.55), channel_id=1, source_target_pairs={{0,2},{2,0},{1,3},{3,1},{4,6},{6,4},{5,7},{7,5},{8,10},{10,8},{9,1... | collective-permute-start | bytes 98312 | tf_op jit(solution)/shard_map/ppermute | solution.py:327
  108.1 0.8 collective-permute-done.18.b_ref
  109.0 1.8 shard_map.106
  111.6 2.6 %collective-permute-start.25 = (bf16[144,2048]{1,0:T(8,128)(2,1)}, bf16[144,2048]{1,0:T(8,128)(2,1)}, u32[]{:S(2)}, u32[]{:S(2)}) collective-permute-start(bf16[144,2048]{1,0:T(8,128)(2,1)} %get-tuple-element.62), channel_id=1, source_target_pairs={{0,192},{64,0},{128,64},{192,128},{1,193},{65,1},{129,65},{193,129... | collective-permute-start | bytes 1769480 | tf_op jit(solution)/shard_map/ppermute | solution.py:327
  115.0 0.7 broadcast_in_dim.4
  115.7 6.8 %all-to-all-start = ((bf16[8,8,2048]{2,1,0:T(8,128)(2,1)}), bf16[8,8,2048]{2,1,0:T(8,128)(2,1)S(1)}, u32[]{:S(2)}, u32[]{:S(2)}) async-start(bf16[8,8,2048]{2,1,0:T(8,128)(2,1)} %broadcast_in_dim.4), calls=%async_computation | async-start | bytes 524288 | tf_op jit(solution)/shard_map/all_to_all | solution.py:381
  122.6 1.3 collective-permute-start.29
  124.1 3.5 %collective-permute-start.27 = (bf16[3,2048]{1,0:T(4,128)(2,1)S(1)}, bf16[3,2048]{1,0:T(4,128)(2,1)S(1)}, u32[]{:S(2)}, u32[]{:S(2)}) collective-permute-start(bf16[3,2048]{1,0:T(4,128)(2,1)S(1)} %get-tuple-element.93), channel_id=1, source_target_pairs={{2,0},{4,2},{6,4},{8,6},{10,8},{12,10},{14,12},{16,14},{18,16},{20... | collective-permute-start | bytes 36872 | tf_op jit(solution)/shard_map/ppermute | solution.py:319
  127.8 3.2 %collective-permute-start.26 = (bf16[3,2048]{1,0:T(4,128)(2,1)S(1)}, bf16[3,2048]{1,0:T(4,128)(2,1)S(1)}, u32[]{:S(2)}, u32[]{:S(2)}) collective-permute-start(bf16[3,2048]{1,0:T(4,128)(2,1)S(1)} %get-tuple-element.92), channel_id=1, source_target_pairs={{0,2},{2,4},{4,6},{6,8},{8,10},{10,12},{12,14},{14,16},{16,18},{18... | collective-permute-start | bytes 36872 | tf_op jit(solution)/shard_map/ppermute | solution.py:318
  131.0 1.7 all-to-all-done
  132.7 1.6 broadcast_in_dim.5
  134.3 5.1 %all-to-all-start.1 = ((bf16[8,64,2048]{2,1,0:T(8,128)(2,1)}), bf16[8,64,2048]{2,1,0:T(8,128)(2,1)}, u32[]{:S(2)}, u32[]{:S(2)}) async-start(bf16[8,64,2048]{2,1,0:T(8,128)(2,1)} %broadcast_in_dim.5), calls=%async_computation.1 | async-start | bytes 4194304 | tf_op jit(solution)/shard_map/all_to_all | solution.py:400
  139.4 1.2 pad_maximum_fusion.1.r2
  140.6 1.0 copy-done.4
  141.7 1.1 copy-done.5
  142.7 2.6 %shard_map.107 = (bf16[2,128,512]{2,1,0:T(8,128)(2,1)S(1)}, bf16[2,128,512]{2,1,0:T(8,128)(2,1)S(1)}) custom-call(s32[4]{0:T(128)S(1)} %copy-done.7, bf16[144,2048]{1,0:T(8,128)(2,1)S(1)} %copy-done.5, bf16[144,2048]{1,0:T(8,128)(2,1)} %collective-permute-done.24.r1, bf16[144,2048]{1,0:T(8,128)(2,1)S(1)} %pad_maximum_fusion.1.r2, ...), custom_call_target="tpu_custom_call" | custom-call | tf_op jit(solution)/shard_map/pallas_call | solution.py:228
  145.3 2.0 %collective-permute-start.30 = (bf16[2,128,512]{2,1,0:T(8,128)(2,1)S(1)}, bf16[2,128,512]{2,1,0:T(8,128)(2,1)S(1)}, u32[]{:S(2)}, u32[]{:S(2)}) collective-permute-start(bf16[2,128,512]{2,1,0:T(8,128)(2,1)S(1)} %get-tuple-element.73), channel_id=1, source_target_pairs={{0,2},{2,0},{1,3},{3,1},{4,6},{6,4},{5,7},{7,5},{8,10},{10,8},{9,1... | collective-permute-start | bytes 786440 | tf_op jit(solution)/shard_map/ppermute | solution.py:327
  147.4 1.0 collective-permute-done.30.b_ref
  148.5 2.4 %shard_map.108 = (f32[128,2048]{1,0:T(8,128)S(1)}, bf16[128,2048]{1,0:T(8,128)(2,1)S(1)}) custom-call(bf16[2,128,512]{2,1,0:T(8,128)(2,1)S(1)} %get-tuple-element.72.a_ref, bf16[2,128,512]{2,1,0:T(8,128)(2,1)S(1)} %collective-permute-done.30.b_ref, bf16[512,2048]{1,0:T(8,128)(2,1)S(1)} %copy-done, bf16[256,2048]{1,0:T(8,128)(2,1)S(1)} %collective-permute-done.19.w1_hbm, ...), custom_call_target="tpu_custom_call" | custom-call | tf_op jit(solution)/shard_map/pallas_call | solution.py:264
  151.9 1.0 collective-permute-done.31
  152.9 1.2 add_convert_fusion
  154.1 10.6 %all-to-all-done.1 = bf16[8,64,2048]{2,1,0:T(8,128)(2,1)} async-done(((bf16[8,64,2048]{2,1,0:T(8,128)(2,1)}), bf16[8,64,2048]{2,1,0:T(8,128)(2,1)}, u32[]{:S(2)}, u32[]{:S(2)}) %all-to-all-start.1) | async-done | bytes 2097184 | tf_op jit(solution)/shard_map/all_to_all | solution.py:400
  164.7 2.7 %collective-permute-start.32 = (bf16[512,2048]{1,0:T(8,128)(2,1)}, bf16[512,2048]{1,0:T(8,128)(2,1)S(1)}, u32[]{:S(2)}, u32[]{:S(2)}) collective-permute-start(bf16[512,2048]{1,0:T(8,128)(2,1)} %bitcast.17.x_ref), channel_id=1, source_target_pairs={{0,2},{2,0},{1,3},{3,1},{4,6},{6,4},{5,7},{7,5},{8,10},{10,8},{9,1... | collective-permute-start | bytes 6291464 | tf_op jit(solution)/shard_map/ppermute | solution.py:327
  167.4 4.0 %shard_map.109.refs_0_ = f32[4,8,2,2,8,640]{5,4,3,2,1,0:T(8,128)} custom-call(s32[1]{0:T(128)} %bitcast.15.who, bf16[512,2048]{1,0:T(8,128)(2,1)} %bitcast.17.x_ref, bf16[2048,640]{1,0:T(8,128)(2,1)S(1)} %copy-done.1), custom_call_target="tpu_custom_call" | custom-call | flops 1342177280 | bytes 6291456 | tf_op jit(solution)/shard_map/pallas_call | solution.py:289
  171.5 2.8 %shard_map.110 = f32[4,8,2,2,8,640]{5,4,3,2,1,0:T(8,128)} custom-call(s32[1]{0:T(128)S(6)} %sub.3.who, bf16[512,2048]{1,0:T(8,128)(2,1)S(1)} %collective-permute-done.32.x_ref, bf16[2048,640]{1,0:T(8,128)(2,1)S(1)} %copy-done.1, f32[4,8,2,2,8,640]{5,4,3,2,1,0:T(8,128)} %shard_map.109.refs_0_), custom_call_target="tpu_custom_call", output_to_operand_aliasing={{}: (3, {})} | custom-call | flops 1342177280 | bytes 6291456 | tf_op jit(solution)/shard_map/pallas_call | solution.py:289
  (115 shorter events, 5.1 us)
Async XLA Ops:
  7.2 59.3 %all-gather.2.cloned.1.call-start = ((), (), s32[]{:S(2)}) async-start(), calls=%async_computation.2 | async-start | bytes 2359296 | tf_op jit(solution)/shard_map/all_gather | solution.py:337
  7.2 24.9 %collective-permute-start.7 = (bf16[128,2048]{1,0:T(8,128)(2,1)}, bf16[128,2048]{1,0:T(8,128)(2,1)S(1)}, u32[]{:S(2)}, u32[]{:S(2)}) collective-permute-start(bf16[128,2048]{1,0:T(8,128)(2,1)} %refs_0_.1), channel_id=1, source_target_pairs={{0,192},{64,0},{128,64},{192,128},{1,193},{65,1},{129,65},{193,129... | collective-permute-start | bytes 1572872 | tf_op jit(solution)/shard_map/ppermute | solution.py:327
  10.9 23.8 %collective-permute-start.8 = (bf16[128,2048]{1,0:T(8,128)(2,1)}, bf16[128,2048]{1,0:T(8,128)(2,1)S(1)}, u32[]{:S(2)}, u32[]{:S(2)}) collective-permute-start(bf16[128,2048]{1,0:T(8,128)(2,1)} %refs_0_.1), channel_id=1, source_target_pairs={{0,64},{64,128},{128,192},{192,0},{1,65},{65,129},{129,193},{193,1... | collective-permute-start | bytes 1572872 | tf_op jit(solution)/shard_map/ppermute | solution.py:327
  11.7 4.2 %collective-permute-start = (bf16[128,512]{1,0:T(8,128)(2,1)S(1)}, bf16[128,512]{1,0:T(8,128)(2,1)S(1)}, u32[]{:S(2)}, u32[]{:S(2)}) collective-permute-start(bf16[128,512]{1,0:T(8,128)(2,1)S(1)} %pad_maximum_fusion.4), channel_id=1, source_target_pairs={{0,4},{4,0},{1,5},{5,1},{2,6},{6,2},{3,7},{7,3},{8,12},{12,8},{9,1... | collective-permute-start | bytes 393224 | tf_op jit(solution)/shard_map/ppermute | solution.py:327
  16.0 25.4 %copy-start.14 = (bf16[256,512]{1,0:T(8,128)(2,1)}, bf16[256,512]{1,0:T(8,128)(2,1)S(1)}, u32[]{:S(2)}) copy-start(bf16[256,512]{1,0:T(8,128)(2,1)S(1)} %pad_maximum_fusion.2.refs_5_) | copy-start | bytes 786436
  16.0 10.5 %collective-permute-start.1 = (bf16[256,512]{1,0:T(8,128)(2,1)S(1)}, bf16[256,512]{1,0:T(8,128)(2,1)S(1)}, u32[]{:S(2)}, u32[]{:S(2)}) collective-permute-start(bf16[256,512]{1,0:T(8,128)(2,1)S(1)} %pad_maximum_fusion.2.refs_5_), channel_id=1, source_target_pairs={{0,8},{8,16},{16,24},{24,32},{32,40},{40,48},{48,56},{56,0},{1,9},... | collective-permute-start | bytes 786440 | tf_op jit(solution)/shard_map/ppermute | solution.py:327
  17.7 8.8 %collective-permute-start.4 = (bf16[256,512]{1,0:T(8,128)(2,1)S(1)}, bf16[256,512]{1,0:T(8,128)(2,1)S(1)}, u32[]{:S(2)}, u32[]{:S(2)}) collective-permute-start(bf16[256,512]{1,0:T(8,128)(2,1)S(1)} %pad_maximum_fusion.2.refs_5_), channel_id=1, source_target_pairs={{0,56},{8,0},{16,8},{24,16},{32,24},{40,32},{48,40},{56,48},{1,57}... | collective-permute-start | bytes 786440 | tf_op jit(solution)/shard_map/ppermute | solution.py:327
  26.4 15.7 %copy-start.15 = (bf16[256,512]{1,0:T(8,128)(2,1)}, bf16[256,512]{1,0:T(8,128)(2,1)S(1)}, u32[]{:S(2)}) copy-start(bf16[256,512]{1,0:T(8,128)(2,1)S(1)} %collective-permute-done.1.refs_6_) | copy-start | bytes 786436
  26.4 10.8 %collective-permute-start.2 = (bf16[256,512]{1,0:T(8,128)(2,1)S(1)}, bf16[256,512]{1,0:T(8,128)(2,1)S(1)}, u32[]{:S(2)}, u32[]{:S(2)}) collective-permute-start(bf16[256,512]{1,0:T(8,128)(2,1)S(1)} %collective-permute-done.1.refs_6_), channel_id=1, source_target_pairs={{0,8},{8,16},{16,24},{24,32},{32,40},{40,48},{48,56},{56,0},{1,9},... | collective-permute-start | bytes 786440 | tf_op jit(solution)/shard_map/ppermute | solution.py:327
  26.4 15.7 %copy-start.16 = (bf16[256,512]{1,0:T(8,128)(2,1)}, bf16[256,512]{1,0:T(8,128)(2,1)S(1)}, u32[]{:S(2)}) copy-start(bf16[256,512]{1,0:T(8,128)(2,1)S(1)} %collective-permute-done.4.refs_7_) | copy-start | bytes 786436
  26.5 11.5 %collective-permute-start.5 = (bf16[256,512]{1,0:T(8,128)(2,1)S(1)}, bf16[256,512]{1,0:T(8,128)(2,1)S(1)}, u32[]{:S(2)}, u32[]{:S(2)}) collective-permute-start(bf16[256,512]{1,0:T(8,128)(2,1)S(1)} %collective-permute-done.4.refs_7_), channel_id=1, source_target_pairs={{0,56},{8,0},{16,8},{24,16},{32,24},{40,32},{48,40},{56,48},{1,57}... | collective-permute-start | bytes 786440 | tf_op jit(solution)/shard_map/ppermute | solution.py:327
  32.1 2.5 %copy-start.20 = (bf16[128,2048]{1,0:T(8,128)(2,1)}, bf16[128,2048]{1,0:T(8,128)(2,1)S(1)}, u32[]{:S(2)}) copy-start(bf16[128,2048]{1,0:T(8,128)(2,1)S(1)} %collective-permute-done.7.refs_1_) | copy-start | bytes 1572868
  32.2 10.0 %collective-permute-start.10 = (bf16[64,2048]{1,0:T(8,128)(2,1)S(1)}, bf16[64,2048]{1,0:T(8,128)(2,1)S(1)}, u32[]{:S(2)}, u32[]{:S(2)}) collective-permute-start(bf16[64,2048]{1,0:T(8,128)(2,1)S(1)} %slice.152), channel_id=1, source_target_pairs={{0,192},{64,0},{128,64},{192,128},{1,193},{65,1},{129,65},{193,129... | collective-permute-start | bytes 786440 | tf_op jit(solution)/shard_map/ppermute | solution.py:327
  34.6 24.1 %copy-start.21 = (bf16[128,2048]{1,0:T(8,128)(2,1)}, bf16[128,2048]{1,0:T(8,128)(2,1)S(1)}, u32[]{:S(2)}) copy-start(bf16[128,2048]{1,0:T(8,128)(2,1)S(1)} %collective-permute-done.8.refs_2_) | copy-start | bytes 1572868
  34.7 7.5 %collective-permute-start.9 = (bf16[64,2048]{1,0:T(8,128)(2,1)S(1)}, bf16[64,2048]{1,0:T(8,128)(2,1)S(1)}, u32[]{:S(2)}, u32[]{:S(2)}) collective-permute-start(bf16[64,2048]{1,0:T(8,128)(2,1)S(1)} %slice.151), channel_id=1, source_target_pairs={{0,64},{64,128},{128,192},{192,0},{1,65},{65,129},{129,193},{193,1... | collective-permute-start | bytes 786440 | tf_op jit(solution)/shard_map/ppermute | solution.py:327
  37.3 28.1 %copy-start.17 = (bf16[256,512]{1,0:T(8,128)(2,1)}, bf16[256,512]{1,0:T(8,128)(2,1)S(1)}, u32[]{:S(2)}) copy-start(bf16[256,512]{1,0:T(8,128)(2,1)S(1)} %collective-permute-done.2.refs_8_) | copy-start | bytes 786436
  37.3 13.6 %collective-permute-start.3 = (bf16[256,512]{1,0:T(8,128)(2,1)S(1)}, bf16[256,512]{1,0:T(8,128)(2,1)S(1)}, u32[]{:S(2)}, u32[]{:S(2)}) collective-permute-start(bf16[256,512]{1,0:T(8,128)(2,1)S(1)} %collective-permute-done.2.refs_8_), channel_id=1, source_target_pairs={{0,8},{8,16},{16,24},{24,32},{32,40},{40,48},{48,56},{56,0},{1,9},... | collective-permute-start | bytes 786440 | tf_op jit(solution)/shard_map/ppermute | solution.py:327
  38.0 27.4 %copy-start.18 = (bf16[256,512]{1,0:T(8,128)(2,1)}, bf16[256,512]{1,0:T(8,128)(2,1)S(1)}, u32[]{:S(2)}) copy-start(bf16[256,512]{1,0:T(8,128)(2,1)S(1)} %collective-permute-done.5.refs_9_) | copy-start | bytes 786436
  38.0 12.9 %collective-permute-start.6 = (bf16[256,512]{1,0:T(8,128)(2,1)S(1)}, bf16[256,512]{1,0:T(8,128)(2,1)S(1)}, u32[]{:S(2)}, u32[]{:S(2)}) collective-permute-start(bf16[256,512]{1,0:T(8,128)(2,1)S(1)} %collective-permute-done.5.refs_9_), channel_id=1, source_target_pairs={{0,56},{8,0},{16,8},{24,16},{32,24},{40,32},{48,40},{56,48},{1,57}... | collective-permute-start | bytes 786440 | tf_op jit(solution)/shard_map/ppermute | solution.py:327
  42.1 26.1 %copy-start.27 = (bf16[64,2048]{1,0:T(8,128)(2,1)}, bf16[64,2048]{1,0:T(8,128)(2,1)S(1)}, u32[]{:S(2)}) copy-start(bf16[64,2048]{1,0:T(8,128)(2,1)S(1)} %collective-permute-done.10.refs_4_) | copy-start | bytes 786436
  42.1 23.0 %copy-start.28 = (bf16[64,2048]{1,0:T(8,128)(2,1)}, bf16[64,2048]{1,0:T(8,128)(2,1)S(1)}, u32[]{:S(2)}) copy-start(bf16[64,2048]{1,0:T(8,128)(2,1)S(1)} %collective-permute-done.9.refs_3_) | copy-start | bytes 786436
  50.8 17.4 %copy-start.12 = (bf16[256,512]{1,0:T(8,128)(2,1)}, bf16[256,512]{1,0:T(8,128)(2,1)S(1)}, u32[]{:S(2)}) copy-start(bf16[256,512]{1,0:T(8,128)(2,1)S(1)} %collective-permute-done.3.refs_10_) | copy-start | bytes 786436
  50.8 7.9 %copy-start.13 = (bf16[256,512]{1,0:T(8,128)(2,1)}, bf16[256,512]{1,0:T(8,128)(2,1)S(1)}, u32[]{:S(2)}) copy-start(bf16[256,512]{1,0:T(8,128)(2,1)S(1)} %collective-permute-done.6.refs_11_) | copy-start | bytes 786436
  52.3 19.8 %collective-permute-start.11 = (bf16[1792,512]{1,0:T(8,128)(2,1)}, bf16[1792,512]{1,0:T(8,128)(2,1)}, u32[]{:S(2)}, u32[]{:S(2)}) collective-permute-start(bf16[1792,512]{1,0:T(8,128)(2,1)} %constant_dynamic-update-slice_fusion), channel_id=1, source_target_pairs={{0,2},{2,0},{1,3},{3,1},{4,6},{6,4},{5,7},{7,5},{8,10},{10,8},{9,1... | collective-permute-start | bytes 5505032 | tf_op jit(solution)/shard_map/ppermute | solution.py:327
  58.7 6.4 %collective-permute-start.12 = (bf16[128,512]{1,0:T(8,128)(2,1)S(1)}, bf16[128,512]{1,0:T(8,128)(2,1)S(1)}, u32[]{:S(2)}, u32[]{:S(2)}) collective-permute-start(bf16[128,512]{1,0:T(8,128)(2,1)S(1)} %slice.119), channel_id=1, source_target_pairs={{0,8},{8,16},{16,24},{24,32},{32,40},{40,48},{48,56},{56,0},{1,9},... | collective-permute-start | bytes 393224 | tf_op jit(solution)/shard_map/ppermute | solution.py:327
  58.8 6.5 %collective-permute-start.13 = (bf16[128,512]{1,0:T(8,128)(2,1)S(1)}, bf16[128,512]{1,0:T(8,128)(2,1)S(1)}, u32[]{:S(2)}, u32[]{:S(2)}) collective-permute-start(bf16[128,512]{1,0:T(8,128)(2,1)S(1)} %slice.120), channel_id=1, source_target_pairs={{0,56},{8,0},{16,8},{24,16},{32,24},{40,32},{48,40},{56,48},{1,57}... | collective-permute-start | bytes 393224 | tf_op jit(solution)/shard_map/ppermute | solution.py:327
  65.2 3.1 %copy-start.22 = (bf16[128,512]{1,0:T(8,128)(2,1)}, bf16[128,512]{1,0:T(8,128)(2,1)S(1)}, u32[]{:S(2)}) copy-start(bf16[128,512]{1,0:T(8,128)(2,1)S(1)} %collective-permute-done.12.refs_13_) | copy-start | bytes 393220
  65.3 2.9 %copy-start.23 = (bf16[128,512]{1,0:T(8,128)(2,1)}, bf16[128,512]{1,0:T(8,128)(2,1)S(1)}, u32[]{:S(2)}) copy-start(bf16[128,512]{1,0:T(8,128)(2,1)S(1)} %collective-permute-done.13.refs_14_) | copy-start | bytes 393220
  65.4 6.0 %collective-permute-start.14 = (bf16[256,512]{1,0:T(8,128)(2,1)S(1)}, bf16[256,512]{1,0:T(8,128)(2,1)S(1)}, u32[]{:S(2)}, u32[]{:S(2)}) collective-permute-start(bf16[256,512]{1,0:T(8,128)(2,1)S(1)} %pad_maximum_fusion.3), channel_id=1, source_target_pairs={{0,2},{2,0},{1,3},{3,1},{4,6},{6,4},{5,7},{7,5},{8,10},{10,8},{9,1... | collective-permute-start | bytes 786440 | tf_op jit(solution)/shard_map/ppermute | solution.py:327
  68.3 40.7 %collective-permute-start.19 = (bf16[256,2048]{1,0:T(8,128)(2,1)S(1)}, bf16[256,2048]{1,0:T(8,128)(2,1)S(1)}, u32[]{:S(2)}, u32[]{:S(2)}) collective-permute-start(bf16[256,2048]{1,0:T(8,128)(2,1)S(1)} %get-tuple-element.81), channel_id=1, source_target_pairs={{0,4},{4,0},{1,5},{5,1},{2,6},{6,2},{3,7},{7,3},{8,12},{12,8},{9,1... | collective-permute-start | bytes 3145736 | tf_op jit(solution)/shard_map/ppermute | solution.py:327
  69.5 28.6 %copy-start.8 = (bf16[128,2048]{1,0:T(8,128)(2,1)S(1)}, bf16[128,2048]{1,0:T(8,128)(2,1)}, u32[]{:S(2)}) copy-start(bf16[128,2048]{1,0:T(8,128)(2,1)} %param.9) | copy-start | bytes 1572868
  69.5 34.6 %copy-start.7 = (s32[4]{0:T(128)S(1)}, s32[4]{0:T(128)}, u32[]{:S(2)}) copy-start(s32[4]{0:T(128)} %pad_add_fusion.place) | copy-start | bytes 52
  69.5 39.4 %collective-permute-start.20 = (bf16[256,2048]{1,0:T(8,128)(2,1)S(1)}, bf16[256,2048]{1,0:T(8,128)(2,1)S(1)}, u32[]{:S(2)}, u32[]{:S(2)}) collective-permute-start(bf16[256,2048]{1,0:T(8,128)(2,1)S(1)} %get-tuple-element.80), channel_id=1, source_target_pairs={{0,5},{1,4},{4,1},{5,0},{2,7},{3,6},{6,3},{7,2},{8,13},{9,12},{12,... | collective-permute-start | bytes 3145736 | tf_op jit(solution)/shard_map/ppermute | solution.py:375
  72.1 36.8 %copy-start = (bf16[512,2048]{1,0:T(8,128)(2,1)S(1)}, bf16[512,2048]{1,0:T(8,128)(2,1)}, u32[]{:S(2)}) copy-start(bf16[512,2048]{1,0:T(8,128)(2,1)} %all-gather.2.cloned.1.call-done.w0_hbm) | copy-start | bytes 6291460
  94.5 5.9 %collective-permute-start.15 = (bf16[32,2048]{1,0:T(8,128)(2,1)}, bf16[32,2048]{1,0:T(8,128)(2,1)S(1)}, u32[]{:S(2)}, u32[]{:S(2)}) collective-permute-start(bf16[32,2048]{1,0:T(8,128)(2,1)} %get-tuple-element.50), channel_id=1, source_target_pairs={{0,64},{64,128},{128,192},{192,0},{1,65},{65,129},{129,193},{193,1... | collective-permute-start | bytes 393224 | tf_op jit(solution)/shard_map/ppermute | solution.py:327
  94.6 9.6 %collective-permute-start.16 = (bf16[32,2048]{1,0:T(8,128)(2,1)}, bf16[32,2048]{1,0:T(8,128)(2,1)S(1)}, u32[]{:S(2)}, u32[]{:S(2)}) collective-permute-start(bf16[32,2048]{1,0:T(8,128)(2,1)} %get-tuple-element.51), channel_id=1, source_target_pairs={{0,128},{64,192},{128,0},{192,64},{1,129},{65,193},{129,1},{193,65... | collective-permute-start | bytes 393224 | tf_op jit(solution)/shard_map/ppermute | solution.py:327
  98.2 6.0 %collective-permute-start.17 = (bf16[32,2048]{1,0:T(8,128)(2,1)}, bf16[32,2048]{1,0:T(8,128)(2,1)S(1)}, u32[]{:S(2)}, u32[]{:S(2)}) collective-permute-start(bf16[32,2048]{1,0:T(8,128)(2,1)} %get-tuple-element.52), channel_id=1, source_target_pairs={{0,192},{64,0},{128,64},{192,128},{1,193},{65,1},{129,65},{193,129... | collective-permute-start | bytes 393224 | tf_op jit(solution)/shard_map/ppermute | solution.py:327
  100.4 13.8 %collective-permute-start.23 = (bf16[80,2048]{1,0:T(8,128)(2,1)}, bf16[80,2048]{1,0:T(8,128)(2,1)S(1)}, u32[]{:S(2)}, u32[]{:S(2)}) collective-permute-start(bf16[80,2048]{1,0:T(8,128)(2,1)} %get-tuple-element.59), channel_id=1, source_target_pairs={{0,192},{64,0},{128,64},{192,128},{1,193},{65,1},{129,65},{193,129... | collective-permute-start | bytes 983048 | tf_op jit(solution)/shard_map/ppermute | solution.py:327
  104.2 10.0 %collective-permute-start.22 = (bf16[64,2048]{1,0:T(8,128)(2,1)}, bf16[64,2048]{1,0:T(8,128)(2,1)S(1)}, u32[]{:S(2)}, u32[]{:S(2)}) collective-permute-start(bf16[64,2048]{1,0:T(8,128)(2,1)} %get-tuple-element.58), channel_id=1, source_target_pairs={{0,64},{64,128},{128,192},{192,0},{1,65},{65,129},{129,193},{193,1... | collective-permute-start | bytes 786440 | tf_op jit(solution)/shard_map/ppermute | solution.py:327
  104.2 0.9 copy-start.6
  105.9 3.1 %collective-permute-start.18 = (bf16[2,16,512]{2,1,0:T(8,128)(2,1)S(1)}, bf16[2,16,512]{2,1,0:T(8,128)(2,1)S(1)}, u32[]{:S(2)}, u32[]{:S(2)}) collective-permute-start(bf16[2,16,512]{2,1,0:T(8,128)(2,1)S(1)} %get-tuple-element.55), channel_id=1, source_target_pairs={{0,2},{2,0},{1,3},{3,1},{4,6},{6,4},{5,7},{7,5},{8,10},{10,8},{9,1... | collective-permute-start | bytes 98312 | tf_op jit(solution)/shard_map/ppermute | solution.py:327
  108.9 1.8 %copy-start.2 = (bf16[256,2048]{1,0:T(8,128)(2,1)}, bf16[256,2048]{1,0:T(8,128)(2,1)S(1)}, u32[]{:S(2)}) copy-start(bf16[256,2048]{1,0:T(8,128)(2,1)S(1)} %collective-permute-done.20.w2_hbm) | copy-start | bytes 3145732
  108.9 5.4 %copy-start.24 = (f32[2048]{0:T(1024)S(1)}, f32[2048]{0:T(1024)}, u32[]{:S(2)}) copy-start(f32[2048]{0:T(1024)} %param.16) | copy-start | bytes 24580
  108.9 13.6 %copy-start.19 = (bf16[4,2048]{1,0:T(4,128)(2,1)S(1)}, bf16[4,2048]{1,0:T(4,128)(2,1)}, u32[]{:S(2)}) copy-start(bf16[4,2048]{1,0:T(4,128)(2,1)} %param.10) | copy-start | bytes 49156
  110.8 3.5 %collective-permute-start.21 = (bf16[16,2048]{1,0:T(8,128)(2,1)S(1)}, bf16[16,2048]{1,0:T(8,128)(2,1)S(1)}, u32[]{:S(2)}, u32[]{:S(2)}) collective-permute-start(bf16[16,2048]{1,0:T(8,128)(2,1)S(1)} %get-tuple-element.57), channel_id=1, source_target_pairs={{0,2},{2,0},{1,3},{3,1},{4,6},{6,4},{5,7},{7,5},{8,10},{10,8},{9,1... | collective-permute-start | bytes 196616 | tf_op jit(solution)/shard_map/ppermute | solution.py:327
  111.2 16.6 %collective-permute-start.24 = (bf16[144,2048]{1,0:T(8,128)(2,1)}, bf16[144,2048]{1,0:T(8,128)(2,1)}, u32[]{:S(2)}, u32[]{:S(2)}) collective-permute-start(bf16[144,2048]{1,0:T(8,128)(2,1)} %get-tuple-element.61), channel_id=1, source_target_pairs={{0,64},{64,128},{128,192},{192,0},{1,65},{65,129},{129,193},{193,1... | collective-permute-start | bytes 1769480 | tf_op jit(solution)/shard_map/ppermute | solution.py:327
  111.6 19.4 %collective-permute-start.25 = (bf16[144,2048]{1,0:T(8,128)(2,1)}, bf16[144,2048]{1,0:T(8,128)(2,1)}, u32[]{:S(2)}, u32[]{:S(2)}) collective-permute-start(bf16[144,2048]{1,0:T(8,128)(2,1)} %get-tuple-element.62), channel_id=1, source_target_pairs={{0,192},{64,0},{128,64},{192,128},{1,193},{65,1},{129,65},{193,129... | collective-permute-start | bytes 1769480 | tf_op jit(solution)/shard_map/ppermute | solution.py:327
  114.2 0.8 copy-start.25
  115.7 17.0 %all-to-all-start = ((bf16[8,8,2048]{2,1,0:T(8,128)(2,1)}), bf16[8,8,2048]{2,1,0:T(8,128)(2,1)S(1)}, u32[]{:S(2)}, u32[]{:S(2)}) async-start(bf16[8,8,2048]{2,1,0:T(8,128)(2,1)} %broadcast_in_dim.4), calls=%async_computation | async-start | bytes 524288 | tf_op jit(solution)/shard_map/all_to_all | solution.py:381
  122.6 16.9 %collective-permute-start.29 = (bf16[80,2048]{1,0:T(8,128)(2,1)}, bf16[80,2048]{1,0:T(8,128)(2,1)}, u32[]{:S(2)}, u32[]{:S(2)}) collective-permute-start(bf16[80,2048]{1,0:T(8,128)(2,1)} %copy-done.25), channel_id=1, source_target_pairs={{0,192},{64,0},{128,64},{192,128},{1,193},{65,1},{129,65},{193,129... | collective-permute-start | bytes 983048 | tf_op jit(solution)/shard_map/ppermute | solution.py:327
  123.8 15.6 %collective-permute-start.28 = (bf16[64,2048]{1,0:T(8,128)(2,1)}, bf16[64,2048]{1,0:T(8,128)(2,1)}, u32[]{:S(2)}, u32[]{:S(2)}) collective-permute-start(bf16[64,2048]{1,0:T(8,128)(2,1)} %copy-done.26), channel_id=1, source_target_pairs={{0,64},{64,128},{128,192},{192,0},{1,65},{65,129},{129,193},{193,1... | collective-permute-start | bytes 786440 | tf_op jit(solution)/shard_map/ppermute | solution.py:327
  124.1 23.2 %collective-permute-start.27 = (bf16[3,2048]{1,0:T(4,128)(2,1)S(1)}, bf16[3,2048]{1,0:T(4,128)(2,1)S(1)}, u32[]{:S(2)}, u32[]{:S(2)}) collective-permute-start(bf16[3,2048]{1,0:T(4,128)(2,1)S(1)} %get-tuple-element.93), channel_id=1, source_target_pairs={{2,0},{4,2},{6,4},{8,6},{10,8},{12,10},{14,12},{16,14},{18,16},{20... | collective-permute-start | bytes 36872 | tf_op jit(solution)/shard_map/ppermute | solution.py:319
  127.8 23.5 %collective-permute-start.26 = (bf16[3,2048]{1,0:T(4,128)(2,1)S(1)}, bf16[3,2048]{1,0:T(4,128)(2,1)S(1)}, u32[]{:S(2)}, u32[]{:S(2)}) collective-permute-start(bf16[3,2048]{1,0:T(4,128)(2,1)S(1)} %get-tuple-element.92), channel_id=1, source_target_pairs={{0,2},{2,4},{4,6},{6,8},{8,10},{10,12},{12,14},{14,16},{16,18},{18... | collective-permute-start | bytes 36872 | tf_op jit(solution)/shard_map/ppermute | solution.py:318
  134.3 30.4 %all-to-all-start.1 = ((bf16[8,64,2048]{2,1,0:T(8,128)(2,1)}), bf16[8,64,2048]{2,1,0:T(8,128)(2,1)}, u32[]{:S(2)}, u32[]{:S(2)}) async-start(bf16[8,64,2048]{2,1,0:T(8,128)(2,1)} %broadcast_in_dim.5), calls=%async_computation.1 | async-start | bytes 4194304 | tf_op jit(solution)/shard_map/all_to_all | solution.py:400
  139.4 7.9 %copy-start.9 = (bf16[128,2048]{1,0:T(8,128)(2,1)S(1)}, bf16[128,2048]{1,0:T(8,128)(2,1)}, u32[]{:S(2)}) copy-start(bf16[128,2048]{1,0:T(8,128)(2,1)} %param.9) | copy-start | bytes 1572868
  139.4 8.0 %copy-start.11 = (bf16[64,2048]{1,0:T(8,128)(2,1)S(1)}, bf16[64,2048]{1,0:T(8,128)(2,1)}, u32[]{:S(2)}) copy-start(bf16[64,2048]{1,0:T(8,128)(2,1)} %get-tuple-element.83) | copy-start | bytes 786436
  140.6 1.0 copy-start.4
  141.6 1.1 copy-start.5
  142.7 5.8 %copy-start.3 = (bf16[256,2048]{1,0:T(8,128)(2,1)S(1)}, bf16[256,2048]{1,0:T(8,128)(2,1)}, u32[]{:S(2)}) copy-start(bf16[256,2048]{1,0:T(8,128)(2,1)} %copy-done.2) | copy-start | bytes 3145732
  145.3 3.1 %collective-permute-start.30 = (bf16[2,128,512]{2,1,0:T(8,128)(2,1)S(1)}, bf16[2,128,512]{2,1,0:T(8,128)(2,1)S(1)}, u32[]{:S(2)}, u32[]{:S(2)}) collective-permute-start(bf16[2,128,512]{2,1,0:T(8,128)(2,1)S(1)} %get-tuple-element.73), channel_id=1, source_target_pairs={{0,2},{2,0},{1,3},{3,1},{4,6},{6,4},{5,7},{7,5},{8,10},{10,8},{9,1... | collective-permute-start | bytes 786440 | tf_op jit(solution)/shard_map/ppermute | solution.py:327
  148.5 2.9 %copy-start.10 = (bf16[64,2048]{1,0:T(8,128)(2,1)S(1)}, bf16[64,2048]{1,0:T(8,128)(2,1)}, u32[]{:S(2)}) copy-start(bf16[64,2048]{1,0:T(8,128)(2,1)} %get-tuple-element.82) | copy-start | bytes 786436
  150.9 2.0 %collective-permute-start.31 = (bf16[128,2048]{1,0:T(8,128)(2,1)S(1)}, bf16[128,2048]{1,0:T(8,128)(2,1)S(1)}, u32[]{:S(2)}, u32[]{:S(2)}) collective-permute-start(bf16[128,2048]{1,0:T(8,128)(2,1)S(1)} %get-tuple-element.75), channel_id=1, source_target_pairs={{0,2},{2,0},{1,3},{3,1},{4,6},{6,4},{5,7},{7,5},{8,10},{10,8},{9,1... | collective-permute-start | bytes 1572872 | tf_op jit(solution)/shard_map/ppermute | solution.py:327
  152.9 14.5 %copy-start.1 = (bf16[2048,640]{1,0:T(8,128)(2,1)S(1)}, bf16[2048,640]{1,0:T(8,128)(2,1)}, u32[]{:S(2)}) copy-start(bf16[2048,640]{1,0:T(8,128)(2,1)} %w_ref.3) | copy-start | bytes 7864324
  164.7 6.8 %collective-permute-start.32 = (bf16[512,2048]{1,0:T(8,128)(2,1)}, bf16[512,2048]{1,0:T(8,128)(2,1)S(1)}, u32[]{:S(2)}, u32[]{:S(2)}) collective-permute-start(bf16[512,2048]{1,0:T(8,128)(2,1)} %bitcast.17.x_ref), channel_id=1, source_target_pairs={{0,2},{2,0},{1,3},{3,1},{4,6},{6,4},{5,7},{7,5},{8,10},{10,8},{9,1... | collective-permute-start | bytes 6291464 | tf_op jit(solution)/shard_map/ppermute | solution.py:327
  (2 other events, 1.4 us)
Sparse Core Ops, SparseCore 0:
  13.2 49.0 all-gather.1

commit v4 on v3

--- a/solution.py
+++ b/solution.py
@@ -15,6 +15,8 @@
 TEAM = NX * NC
 SPAN = NZ * NX * NC * HALF
 NEG = -1e30
+ORDER = (0, -1, 1, -2, 2, -3, 3, 4)
+SWAP = 5
 BK, HB = 1024, 8
 BF = jnp.bfloat16
 F32 = jnp.float32
@@ -234,41 +236,44 @@
     )(place, *parts, g)
 
 
-def project_kernel(rows, a_ref, b_ref, w0_hbm, w1_hbm, w2_hbm, keep_ref, send_ref, ws, sems):
-    step = 512
-    n = keep_ref.shape[1] // step
+def project_kernel(rows, parts, place, a_ref, b_ref, *refs):
+    w_refs, (keep_ref, send_ref, ws, sems) = refs[: len(parts)], refs[len(parts) :]
+    z, dp = place[1], place[4]
     loads = []
-    for i in range(n):
-        cols = slice(i * step, (i + 1) * step)
-        at = 0
-        for t, w in enumerate((w0_hbm, w1_hbm, w2_hbm)):
-            n_rows = w.shape[0]
-            loads.append(pltpu.make_async_copy(w.at[:, cols], ws.at[at : at + n_rows, cols], sems.at[i, t]))
-            at += n_rows
+    for w, (part, flip, first) in zip(w_refs, parts):
+        for i in range(w.shape[0]):
+            head = (z + ORDER[first + i] + NZ) & (NZ - 1)
+            row = part * HEADS * HALF + head * HALF + (dp ^ flip) * 32
+            dst = ws.at[:, pl.ds(pl.multiple_of(row, 32), 32)]
+            loads.append(pltpu.make_async_copy(w.at[i], dst, sems.at[len(loads)]))
     for load in loads:
         load.start()
     x = jnp.concatenate([jnp.concatenate([a_ref[t], b_ref[t]], 0) for t in range(NX)], 1)
-    for i in range(n):
-        for t in range(3):
-            loads[3 * i + t].wait()
+    for load in loads:
+        load.wait()
+    step = ws.shape[2]
+    for i in range(ws.shape[0]):
         cols = slice(i * step, (i + 1) * step)
-        out = jnp.dot(x, ws[:, cols], preferred_element_type=F32)
+        out = jnp.dot(x, ws[i], preferred_element_type=F32)
         keep_ref[:, cols] = out[:rows]
         send_ref[:, cols] = out[rows:].astype(BF)
 
 
-def project(a, b, w0, w1, w2):
-    rows, width = a.shape[1], w0.shape[1]
+def project(place, a, b, weights):
+    rows = a.shape[1]
+    _, groups, _, step = weights[0][0].shape
+    width = groups * step
     vm = pl.BlockSpec(memory_space=pltpu.VMEM)
     hbm = pl.BlockSpec(memory_space=pl.ANY)
+    n = sum(w.shape[0] for w, _ in weights)
     return pl.pallas_call(
-        functools.partial(project_kernel, rows),
-        in_specs=[vm, vm, hbm, hbm, hbm],
+        functools.partial(project_kernel, rows, [p for _, p in weights]),
+        in_specs=[pl.BlockSpec(memory_space=pltpu.SMEM), vm, vm] + [hbm] * len(weights),
         out_specs=[vm, vm],
         out_shape=[jax.ShapeDtypeStruct((rows, width), F32), jax.ShapeDtypeStruct((rows, width), BF)],
-        scratch_shapes=[pltpu.VMEM((NX * w0.shape[0], width), BF), pltpu.SemaphoreType.DMA((4, 3))],
+        scratch_shapes=[pltpu.VMEM((groups, NX * HEADS * HALF, step), BF), pltpu.SemaphoreType.DMA((n,))],
         compiler_params=pltpu.CompilerParams(vmem_limit_bytes=24 * 2**20),
-    )(a, b, w0, w1, w2)
+    )(place, a, b, *[w for w, _ in weights])
 
 
 def lens_kernel(who, x_ref, w_ref, *refs):
@@ -330,23 +335,26 @@
 def body(resid, conv_weight, queries, keys, values, gates, out_weight, norm_gain, lens_weight):
     y, z, xl, c = (lax.axis_index(a) for a in ("y", "z", "xl", "c"))
     me = ((y * NZ + z) * NX + xl) * NC + c
-    place = jnp.stack([y, z, xl, c]).astype(jnp.int32)
+    dp = lax.axis_index("dp")
+    place = jnp.stack([y, z, xl, c, dp]).astype(jnp.int32)
     tok, width = resid.shape
     few = lambda a: jnp.pad(a.reshape(8, 16, -1)[:, 15], ((0, 8), (0, 0)))
 
-    w_own = lax.all_gather(out_weight, "z", axis=0, tiled=True)
+    w_half = jnp.where(dp == 0, out_weight[:32], out_weight[32:])
+    w_block = jnp.concatenate([w_half[:, i * 512 : (i + 1) * 512] for i in range(width // 512)], 0)
 
     kv_own = lax.optimization_barrier(jnp.concatenate([keys, values], 1))
     q_up, q_down = shift(queries, "y", -1), shift(queries, "y", 1)
     q_far = [shift(q_down[:HALF], "y", 1), shift(q_up[HALF:], "y", -1)]
-    pair = jnp.concatenate([kv_own, shift(kv_own, "xl", 1)], 0)
-    both = lambda dz: [(dz, 0, 0, 0, tok), (dz, 1, 0, 0, tok)]
-    held = [(pair, both(0))]
-    fwd = bwd = pair
+    load = jnp.concatenate([kv_own, shift(kv_own, "xl", 1), w_block], 0)
+    n_kv, half = 2 * tok, load.shape[0] // 2
+    both = lambda dz: [(0, (dz, 0, 0, 0, tok)), (tok, (dz, 1, 0, 0, tok))]
+    held = [(load, n_kv, both(0))]
+    fwd = bwd = load
     for s in range(1, NZ // 2):
         fwd, bwd = shift(fwd, "z", 1), shift(bwd, "z", -1)
         if s < NZ // 2 - 1:
-            held += [(fwd, both(-s)), (bwd, both(s))]
+            held += [(fwd, n_kv, both(-s)), (bwd, n_kv, both(s))]
     taps = conv_weight.astype(F32)
     blocks = resid.reshape(8, 16, width)
     conv_few = sum(taps[t] * blocks[:, 15 - t].astype(F32) for t in range(conv_weight.shape[0]))
@@ -355,34 +363,38 @@
     fwd, bwd, q_up, q_down, hidden_few, g_few, place, *q_far = lax.optimization_barrier(
         (fwd, bwd, q_up, q_down, hidden_few, g_few, place, *q_far)
     )
-    held += [(fwd, both(1 - NZ // 2)), (bwd, both(NZ // 2 - 1))]
-    held += [(shift(fwd[:tok], "z", 1), both(4)[:1]), (shift(bwd[tok:], "z", -1), both(4)[1:])]
+    held += [(fwd, n_kv, both(1 - NZ // 2)), (bwd, n_kv, both(NZ // 2 - 1))]
+    far_low, far_high = shift(fwd[:half], "z", 1), shift(bwd[half:], "z", -1)
+    cut = half - tok
+    held.append((far_low, half, [(0, (4, 0, 0, 0, tok)), (tok, (4, 1, 0, 0, cut))]))
+    held.append((far_high, tok - cut, [(0, (4, 1, 0, cut, tok - cut))]))
     q_team = [queries, q_up, q_down] + q_far
 
     kv = []
-    for group in (held[:7], held[7:]):
-        entries, at = [], 0
-        for piece, spans in group:
-            kv.append((piece, [(i * tok, e) for i, e in enumerate(spans)]))
-            for dz, dx, _, r0, n in spans:
-                entries.append((at, (dz, dx, 1, r0, n)))
-                at += n
-        kv.append((shift(jnp.concatenate([p for p, _ in group], 0), "c", 1), entries))
-
-    half_w = w_own.shape[0] // 2
-    w_other = [
-        shift(w_own[:half_w], "xl", 1),
-        lax.ppermute(w_own[half_w:], ("xl", "dp"), [(i, 3 - i) for i in range(4)]),
-    ]
+    for group in (held[:SWAP], held[SWAP:]):
+        entries, base = [], 0
+        for piece, n, spans in group:
+            kv.append((piece, spans))
+            entries += [(base + at, (dz, dx, 1, r0, rows)) for at, (dz, dx, _, r0, rows) in spans]
+            base += n
+        kv.append((shift(jnp.concatenate([p[:n] for p, n, _ in group], 0), "c", 1), entries))
+
+    shape = (NZ, width // 512, 32, 512)
+    w_own = jnp.concatenate([p[n_kv:] for p, _, _ in held[:-2]] + [far_high[tok - cut :]], 0).reshape(shape)
+    across = lambda a: lax.ppermute(a, ("xl", "dp"), [(i, 3 - i) for i in range(4)])
+    w_x, w_d = shift(w_own, "xl", 1), across(w_own)
     place, _ = lax.optimization_barrier((place, w_own))
     got = attention(place, q_team, kv)
     main, lead = got[: NY + 1], got[NY + 1 :]
     to_team = lambda a: [a[0], shift(a[1], "y", 1), shift(a[2], "y", 2), shift(a[3], "y", -1)]
     spread = lambda a, axes, n: lax.all_to_all(jnp.broadcast_to(a[None], (n,) + a.shape), axes, 0, 0).reshape(-1, width)
 
+    w_far = [across(w_x[: NZ // 2]), shift(w_d[NZ // 2 :], "xl", 1)]
+    weights = [(w_own, (0, 0, 0)), (w_x, (1, 0, 0)), (w_d, (1, 1, 0))]
+    weights += [(w_far[0], (0, 1, 0)), (w_far[1], (0, 1, NZ // 2))]
     lead = to_team(lead)
     f_keep, f_send = join(place, lead, g_few)
-    f_own, f_other = project(f_keep, shift(f_send, "c", 1), w_own, *w_other)
+    f_own, f_other = project(place, f_keep, shift(f_send, "c", 1), weights)
     far = [shift(main[2], "y", 1), shift(main[4], "y", -1)]
     f_other = shift(f_other, "c", 1)
     lag = conv_weight.shape[0] - 1
@@ -401,7 +413,7 @@
 
     hidden = hidden_rows(resid, rims, conv_weight, me, NY * NZ * NX * NC - 1)
     keep, send = join(place, main, gates)
-    p_own, p_other = project(keep, shift(send, "c", 1), w_own, *w_other)
+    p_own, p_other = project(place, keep, shift(send, "c", 1), weights)
     mixed = (hidden.astype(F32) + p_own + shift(p_other, "c", 1).astype(F32)).astype(BF)
     every, mixed = lax.optimization_barrier((every, mixed))
 

time: 182 us -> 169 us (0.929)
  between operations: 14.5 us -> 1.39 us
  local copies, waits for them, and re-layouts: 18.7 us -> 10.1 us
  waiting for transfers between devices: 39.3 us -> 43.7 us
  Pallas kernels: 36.8 us -> 39.9 us
    unnamed x68 -> x80, local copies, waits for them, and re-layouts: 9.37 us -> 2.44 us
    ppermute x30 -> x31, starting transfers between devices: 46.6 us -> 51 us  [shift(): return lax.ppermute(x, axis, [(i, (i + by) % count) for i in range(count)])]
    ppermute x30 -> x31, waiting for transfers between devices: 27 us -> 30.4 us  [shift(): return lax.ppermute(x, axis, [(i, (i + by) % count) for i in range(count)])]
    ppermute x1 -> x2, waiting for transfers between devices: 0.01 us -> 3.12 us  [body(): lax.ppermute(a, ('xl', 'dp'), [(i, 3 - i) for i in range(4)])]
    pallas_call x2, Pallas kernels: 4.17 us -> 7.22 us  [project(): pl.pallas_call(functools.partial(project_kernel, rows, [p for _, p in wei...]
    all_to_all x1, starting transfers between devices: 6.76 us -> 4.81 us  [body(): lax.all_to_all(jnp.broadcast_to(a[None], (n,) + a.shape), axes, 0, 0)]
  transfers between devices with their start and end apart: 36 -> 37, of which waited for: 15 -> 14; matrix products, arithmetic and copies ran while one was open for 11% -> 8% of each run, Pallas kernels for 19% -> 22%
where the time goes in v4:
time: 169 us
  starting transfers between devices  68.4 us (40%)
  waiting for transfers between devices  43.7 us (26%)
  Pallas kernels  39.9 us (24%)
  local copies, waits for them, and re-layouts  10.1 us (6%)
  other arithmetic  5.28 us (3%)
    ppermute x31, starting transfers between devices, shift(): return lax.ppermute(x, axis, [(i, (i + by) % count) for i in range(count)])  51 us
    ppermute x31, waiting for transfers between devices, shift(): return lax.ppermute(x, axis, [(i, (i + by) % count) for i in range(count)])  30.4 us
    pallas_call x1, Pallas kernels, attention(): pl.pallas_call(functools.partial(attention_kernel, layout), in_specs=[pl....  22.3 us
    all_to_all x1, waiting for transfers between devices, body(): every = lax.all_to_all(copies, ('y', 'xl'), 0, 0).reshape(-1, width)  9.75 us
    pallas_call x2, Pallas kernels, project(): pl.pallas_call(functools.partial(project_kernel, rows, [p for _, p in wei...  7.22 us
    pallas_call x2, Pallas kernels, lens(): pl.pallas_call(lens_kernel, grid_spec=pltpu.PrefetchScalarGridSpec(num_sc...  6.88 us
    all_to_all x1, starting transfers between devices, body(): lax.all_to_all(jnp.broadcast_to(a[None], (n,) + a.shape), axes, 0, 0)  4.81 us
    all_to_all x1, starting transfers between devices, body(): every = lax.all_to_all(copies, ('y', 'xl'), 0, 0).reshape(-1, width)  4.34 us
  transfers between devices with their start and end apart: 37, of which 14 were waited for; matrix products, arithmetic and copies ran while one was open for 8% of the time, Pallas kernels for 22%

profile of v4, /device:TPU:1, one launch (start us, length us, event | category | flops | bytes accessed | tf_op | source)
XLA Modules:
  0.0 168.7 jit_solution(1935309802694932241)
XLA Ops:
  0.6 3.6 %collective-permute-start.7 = (bf16[128,2048]{1,0:T(8,128)(2,1)}, bf16[128,2048]{1,0:T(8,128)(2,1)S(1)}, u32[]{:S(2)}, u32[]{:S(2)}) collective-permute-start(bf16[128,2048]{1,0:T(8,128)(2,1)} %refs_0_.1), channel_id=1, source_target_pairs={{0,192},{64,0},{128,64},{192,128},{1,193},{65,1},{129,65},{193,129... | collective-permute-start | bytes 1572872 | tf_op jit(solution)/shard_map/ppermute | solution.py:332
  4.3 0.9 pad_maximum_fusion.3
  5.2 1.3 collective-permute-start
  6.5 1.6 fusion.18
  8.1 1.0 slice_select_fusion
  9.1 0.9 fusion.20
  10.0 1.0 slice.236
  11.1 0.7 stack.23.place
  11.9 1.7 %collective-permute-start.1 = (bf16[384,512]{1,0:T(8,128)(2,1)S(1)}, bf16[384,512]{1,0:T(8,128)(2,1)S(1)}, u32[]{:S(2)}, u32[]{:S(2)}) collective-permute-start(bf16[384,512]{1,0:T(8,128)(2,1)S(1)} %get-tuple-element.93.refs_5_), channel_id=1, source_target_pairs={{0,8},{8,16},{16,24},{24,32},{32,40},{40,48},{48,56},{56,0},{1,9},... | collective-permute-start | bytes 1179656 | tf_op jit(solution)/shard_map/ppermute | solution.py:332
  13.6 4.0 %collective-permute-start.4 = (bf16[384,512]{1,0:T(8,128)(2,1)S(1)}, bf16[384,512]{1,0:T(8,128)(2,1)S(1)}, u32[]{:S(2)}, u32[]{:S(2)}) collective-permute-start(bf16[384,512]{1,0:T(8,128)(2,1)S(1)} %get-tuple-element.93.refs_5_), channel_id=1, source_target_pairs={{0,56},{8,0},{16,8},{24,16},{32,24},{40,32},{48,40},{56,48},{1,57}... | collective-permute-start | bytes 1179656 | tf_op jit(solution)/shard_map/ppermute | solution.py:332
  17.8 2.8 %collective-permute-start.10 = (bf16[64,2048]{1,0:T(8,128)(2,1)S(1)}, bf16[64,2048]{1,0:T(8,128)(2,1)S(1)}, u32[]{:S(2)}, u32[]{:S(2)}) collective-permute-start(bf16[64,2048]{1,0:T(8,128)(2,1)S(1)} %slice.238), channel_id=1, source_target_pairs={{0,192},{64,0},{128,64},{192,128},{1,193},{65,1},{129,65},{193,129... | collective-permute-start | bytes 786440 | tf_op jit(solution)/shard_map/ppermute | solution.py:332
  20.6 5.1 %collective-permute-done.1.refs_6_ = bf16[384,512]{1,0:T(8,128)(2,1)S(1)} collective-permute-done((bf16[384,512]{1,0:T(8,128)(2,1)S(1)}, bf16[384,512]{1,0:T(8,128)(2,1)S(1)}, u32[]{:S(2)}, u32[]{:S(2)}) %collective-permute-start.1) | collective-permute-done | bytes 393248 | tf_op jit(solution)/shard_map/ppermute | solution.py:332
  25.8 2.7 %collective-permute-start.5 = (bf16[384,512]{1,0:T(8,128)(2,1)S(1)}, bf16[384,512]{1,0:T(8,128)(2,1)S(1)}, u32[]{:S(2)}, u32[]{:S(2)}) collective-permute-start(bf16[384,512]{1,0:T(8,128)(2,1)S(1)} %collective-permute-done.4.refs_7_), channel_id=1, source_target_pairs={{0,56},{8,0},{16,8},{24,16},{32,24},{40,32},{48,40},{56,48},{1,57}... | collective-permute-start | bytes 1179656 | tf_op jit(solution)/shard_map/ppermute | solution.py:332
  28.5 7.2 %collective-permute-done.2.refs_8_ = bf16[384,512]{1,0:T(8,128)(2,1)S(1)} collective-permute-done((bf16[384,512]{1,0:T(8,128)(2,1)S(1)}, bf16[384,512]{1,0:T(8,128)(2,1)S(1)}, u32[]{:S(2)}, u32[]{:S(2)}) %collective-permute-start.2) | collective-permute-done | bytes 393248 | tf_op jit(solution)/shard_map/ppermute | solution.py:332
  35.7 2.7 %collective-permute-start.6 = (bf16[384,512]{1,0:T(8,128)(2,1)S(1)}, bf16[384,512]{1,0:T(8,128)(2,1)S(1)}, u32[]{:S(2)}, u32[]{:S(2)}) collective-permute-start(bf16[384,512]{1,0:T(8,128)(2,1)S(1)} %collective-permute-done.5.refs_9_), channel_id=1, source_target_pairs={{0,56},{8,0},{16,8},{24,16},{32,24},{40,32},{48,40},{56,48},{1,57}... | collective-permute-start | bytes 1179656 | tf_op jit(solution)/shard_map/ppermute | solution.py:332
  38.5 3.4 %collective-permute-start.12 = (bf16[1280,512]{1,0:T(8,128)(2,1)S(1)}, bf16[1280,512]{1,0:T(8,128)(2,1)S(1)}, u32[]{:S(2)}, u32[]{:S(2)}) collective-permute-start(bf16[1280,512]{1,0:T(8,128)(2,1)S(1)} %slice_dynamic-update-slice_fusion), channel_id=1, source_target_pairs={{0,2},{2,0},{1,3},{3,1},{4,6},{6,4},{5,7},{7,5},{8,10},{10,8},{9,1... | collective-permute-start | bytes 3932168 | tf_op jit(solution)/shard_map/ppermute | solution.py:332
  41.9 2.8 %collective-permute-done.3.refs_11_ = bf16[384,512]{1,0:T(8,128)(2,1)S(1)} collective-permute-done((bf16[384,512]{1,0:T(8,128)(2,1)S(1)}, bf16[384,512]{1,0:T(8,128)(2,1)S(1)}, u32[]{:S(2)}, u32[]{:S(2)}) %collective-permute-start.3) | collective-permute-done | bytes 393248 | tf_op jit(solution)/shard_map/ppermute | solution.py:332
  44.8 2.5 %collective-permute-start.11 = (bf16[192,512]{1,0:T(8,128)(2,1)S(1)}, bf16[192,512]{1,0:T(8,128)(2,1)S(1)}, u32[]{:S(2)}, u32[]{:S(2)}) collective-permute-start(bf16[192,512]{1,0:T(8,128)(2,1)S(1)} %slice.193), channel_id=1, source_target_pairs={{0,56},{8,0},{16,8},{24,16},{32,24},{40,32},{48,40},{56,48},{1,57}... | collective-permute-start | bytes 589832 | tf_op jit(solution)/shard_map/ppermute | solution.py:332
  47.4 2.4 %collective-permute-done.11.refs_14_ = bf16[192,512]{1,0:T(8,128)(2,1)S(1)} collective-permute-done((bf16[192,512]{1,0:T(8,128)(2,1)S(1)}, bf16[192,512]{1,0:T(8,128)(2,1)S(1)}, u32[]{:S(2)}, u32[]{:S(2)}) %collective-permute-start.11) | collective-permute-done | bytes 196640 | tf_op jit(solution)/shard_map/ppermute | solution.py:332
  49.9 3.2 %collective-permute-done.13.refs_13_ = bf16[192,512]{1,0:T(8,128)(2,1)S(1)} collective-permute-done((bf16[192,512]{1,0:T(8,128)(2,1)S(1)}, bf16[192,512]{1,0:T(8,128)(2,1)S(1)}, u32[]{:S(2)}, u32[]{:S(2)}) %collective-permute-start.13) | collective-permute-done | bytes 196640 | tf_op jit(solution)/shard_map/ppermute | solution.py:332
  53.1 5.5 %collective-permute-start.14 = (bf16[768,512]{1,0:T(8,128)(2,1)S(1)}, bf16[768,512]{1,0:T(8,128)(2,1)S(1)}, u32[]{:S(2)}, u32[]{:S(2)}) collective-permute-start(bf16[768,512]{1,0:T(8,128)(2,1)S(1)} %pad_maximum_fusion.1), channel_id=1, source_target_pairs={{0,2},{2,0},{1,3},{3,1},{4,6},{6,4},{5,7},{7,5},{8,10},{10,8},{9,1... | collective-permute-start | bytes 2359304 | tf_op jit(solution)/shard_map/ppermute | solution.py:332
  58.7 0.5 collective-permute-start.19
  59.2 2.5 %collective-permute-start.20 = (bf16[8,4,32,512]{3,2,1,0:T(8,128)(2,1)S(1)}, bf16[8,4,32,512]{3,2,1,0:T(8,128)(2,1)S(1)}, u32[]{:S(2)}, u32[]{:S(2)}) collective-permute-start(bf16[8,4,32,512]{3,2,1,0:T(8,128)(2,1)S(1)} %bitcast.43), channel_id=1, source_target_pairs={{0,5},{1,4},{4,1},{5,0},{2,7},{3,6},{6,3},{7,2},{8,13},{9,12},{12,... | collective-permute-start | bytes 3145736 | tf_op jit(solution)/shard_map/ppermute | solution.py:384
  61.7 1.0 copy-done.26
  62.8 0.9 copy-done.27
  63.7 22.3 %shard_map.104 = (bf16[144,2048]{1,0:T(8,128)(2,1)}, bf16[144,2048]{1,0:T(8,128)(2,1)}, bf16[64,2048]{1,0:T(8,128)(2,1)}, bf16[144,2048]{1,0:T(8,128)(2,1)}, bf1...) custom-call(s32[5]{0:T(128)} %stack.23.place, ...), custom_call_target="tpu_custom_call" | custom-call | flops 10000000000 | bytes 8388608 | tf_op jit(solution)/shard_map/pallas_call | solution.py:169
  86.1 3.3 %collective-permute-start.16 = (bf16[32,2048]{1,0:T(8,128)(2,1)}, bf16[32,2048]{1,0:T(8,128)(2,1)S(1)}, u32[]{:S(2)}, u32[]{:S(2)}) collective-permute-start(bf16[32,2048]{1,0:T(8,128)(2,1)} %get-tuple-element.51), channel_id=1, source_target_pairs={{0,128},{64,192},{128,0},{192,64},{1,129},{65,193},{129,1},{193,65... | collective-permute-start | bytes 393224 | tf_op jit(solution)/shard_map/ppermute | solution.py:332
  89.4 0.3 collective-permute-start.21
  89.9 0.9 fusion.16
  90.7 1.2 collective-permute-done.15.r1
  91.9 0.9 collective-permute-start.25
  92.8 2.5 %collective-permute-done.16.r2 = bf16[32,2048]{1,0:T(8,128)(2,1)S(1)} collective-permute-done((bf16[32,2048]{1,0:T(8,128)(2,1)}, bf16[32,2048]{1,0:T(8,128)(2,1)S(1)}, u32[]{:S(2)}, u32[]{:S(2)}) %collective-permute-start.16) | collective-permute-done | bytes 131104 | tf_op jit(solution)/shard_map/ppermute | solution.py:332
  95.4 0.8 shard_map.105
  96.1 2.8 %collective-permute-start.18 = (bf16[2,16,512]{2,1,0:T(8,128)(2,1)S(1)}, bf16[2,16,512]{2,1,0:T(8,128)(2,1)S(1)}, u32[]{:S(2)}, u32[]{:S(2)}) collective-permute-start(bf16[2,16,512]{2,1,0:T(8,128)(2,1)S(1)} %get-tuple-element.55), channel_id=1, source_target_pairs={{0,2},{2,0},{1,3},{3,1},{4,6},{6,4},{5,7},{7,5},{8,10},{10,8},{9,1... | collective-permute-start | bytes 98312 | tf_op jit(solution)/shard_map/ppermute | solution.py:332
  99.0 0.8 collective-permute-done.18.b_ref
  99.8 3.1 %collective-permute-done.21.refs_3_ = bf16[4,4,32,512]{3,2,1,0:T(8,128)(2,1)S(1)} collective-permute-done((bf16[4,4,32,512]{3,2,1,0:T(8,128)(2,1)S(1)}, bf16[4,4,32,512]{3,2,1,0:T(8,128)(2,1)S(1)}, u32[]{:S(2)}, u32[]{:S(2)}) %collective-permute-start.21) | collective-permute-done | bytes 524320 | tf_op jit(solution)/shard_map/ppermute | solution.py:384
  103.0 3.4 %shard_map.106 = (f32[16,2048]{1,0:T(8,128)S(1)}, bf16[16,2048]{1,0:T(8,128)(2,1)S(1)}) custom-call(s32[5]{0:T(128)S(1)} %copy-done.8, bf16[2,16,512]{2,1,0:T(8,128)(2,1)S(1)} %get-tuple-element.54.a_ref, bf16[2,16,512]{2,1,0:T(8,128)(2,1)S(1)} %collective-permute-done.18.b_ref, bf16[8,4,32,512]{3,2,1,0:T(8,128)(2,1)S(1)} %bitcast.44, ...), custom_call_target="tpu_custom_call" | custom-call | tf_op jit(solution)/shard_map/pallas_call | solution.py:269
  106.4 2.4 %collective-permute-start.23 = (bf16[16,2048]{1,0:T(8,128)(2,1)S(1)}, bf16[16,2048]{1,0:T(8,128)(2,1)S(1)}, u32[]{:S(2)}, u32[]{:S(2)}) collective-permute-start(bf16[16,2048]{1,0:T(8,128)(2,1)S(1)} %get-tuple-element.57), channel_id=1, source_target_pairs={{0,2},{2,0},{1,3},{3,1},{4,6},{6,4},{5,7},{7,5},{8,10},{10,8},{9,1... | collective-permute-start | bytes 196616 | tf_op jit(solution)/shard_map/ppermute | solution.py:332
  108.8 1.5 collective-permute-start.26
  110.4 1.2 collective-permute-start.27
  111.6 0.1 fusion.6
  111.8 0.7 broadcast_in_dim.4
  112.5 4.8 %all-to-all-start = ((bf16[8,8,2048]{2,1,0:T(8,128)(2,1)}), bf16[8,8,2048]{2,1,0:T(8,128)(2,1)S(1)}, u32[]{:S(2)}, u32[]{:S(2)}) async-start(bf16[8,8,2048]{2,1,0:T(8,128)(2,1)} %broadcast_in_dim.4), calls=%async_computation | async-start | bytes 524288 | tf_op jit(solution)/shard_map/all_to_all | solution.py:390
  117.5 1.5 collective-permute-start.30
  119.0 3.3 %collective-permute-start.29 = (bf16[3,2048]{1,0:T(4,128)(2,1)S(1)}, bf16[3,2048]{1,0:T(4,128)(2,1)S(1)}, u32[]{:S(2)}, u32[]{:S(2)}) collective-permute-start(bf16[3,2048]{1,0:T(4,128)(2,1)S(1)} %get-tuple-element.103), channel_id=1, source_target_pairs={{2,0},{4,2},{6,4},{8,6},{10,8},{12,10},{14,12},{16,14},{18,16},{20... | collective-permute-start | bytes 36872 | tf_op jit(solution)/shard_map/ppermute | solution.py:324
  122.3 3.1 %collective-permute-done.26.r1 = bf16[144,2048]{1,0:T(8,128)(2,1)} collective-permute-done((bf16[144,2048]{1,0:T(8,128)(2,1)}, bf16[144,2048]{1,0:T(8,128)(2,1)}, u32[]{:S(2)}, u32[]{:S(2)}) %collective-permute-start.26) | collective-permute-done | bytes 589856 | tf_op jit(solution)/shard_map/ppermute | solution.py:332
  125.4 2.1 %collective-permute-start.28 = (bf16[3,2048]{1,0:T(4,128)(2,1)S(1)}, bf16[3,2048]{1,0:T(4,128)(2,1)S(1)}, u32[]{:S(2)}, u32[]{:S(2)}) collective-permute-start(bf16[3,2048]{1,0:T(4,128)(2,1)S(1)} %get-tuple-element.102), channel_id=1, source_target_pairs={{0,2},{2,4},{4,6},{6,8},{8,10},{10,12},{12,14},{14,16},{16,18},{18... | collective-permute-start | bytes 36872 | tf_op jit(solution)/shard_map/ppermute | solution.py:323
  127.5 0.4 all-to-all-done
  127.9 1.6 broadcast_in_dim.5
  129.5 4.3 %all-to-all-start.1 = ((bf16[8,64,2048]{2,1,0:T(8,128)(2,1)}), bf16[8,64,2048]{2,1,0:T(8,128)(2,1)}, u32[]{:S(2)}, u32[]{:S(2)}) async-start(bf16[8,64,2048]{2,1,0:T(8,128)(2,1)} %broadcast_in_dim.5), calls=%async_computation.1 | async-start | bytes 4194304 | tf_op jit(solution)/shard_map/all_to_all | solution.py:412
  133.9 1.2 pad_maximum_fusion.2.r2
  135.1 0.2 copy-done.6
  135.3 2.7 %shard_map.107 = (bf16[2,128,512]{2,1,0:T(8,128)(2,1)S(1)}, bf16[2,128,512]{2,1,0:T(8,128)(2,1)S(1)}) custom-call(s32[5]{0:T(128)S(1)} %copy-done.8, bf16[144,2048]{1,0:T(8,128)(2,1)S(1)} %copy-done.6, bf16[144,2048]{1,0:T(8,128)(2,1)} %collective-permute-done.26.r1, bf16[144,2048]{1,0:T(8,128)(2,1)S(1)} %pad_maximum_fusion.2.r2, ...), custom_call_target="tpu_custom_call" | custom-call | tf_op jit(solution)/shard_map/pallas_call | solution.py:230
  138.0 2.4 %collective-permute-start.32 = (bf16[2,128,512]{2,1,0:T(8,128)(2,1)S(1)}, bf16[2,128,512]{2,1,0:T(8,128)(2,1)S(1)}, u32[]{:S(2)}, u32[]{:S(2)}) collective-permute-start(bf16[2,128,512]{2,1,0:T(8,128)(2,1)S(1)} %get-tuple-element.73), channel_id=1, source_target_pairs={{0,2},{2,0},{1,3},{3,1},{4,6},{6,4},{5,7},{7,5},{8,10},{10,8},{9,1... | collective-permute-start | bytes 786440 | tf_op jit(solution)/shard_map/ppermute | solution.py:332
  140.4 1.0 collective-permute-done.32.b_ref
  141.5 3.8 %shard_map.108 = (f32[128,2048]{1,0:T(8,128)S(1)}, bf16[128,2048]{1,0:T(8,128)(2,1)S(1)}) custom-call(s32[5]{0:T(128)S(1)} %copy-done.8, bf16[2,128,512]{2,1,0:T(8,128)(2,1)S(1)} %get-tuple-element.72.a_ref, bf16[2,128,512]{2,1,0:T(8,128)(2,1)S(1)} %collective-permute-done.32.b_ref, bf16[8,4,32,512]{3,2,1,0:T(8,128)(2,1)S(1)} %bitcast.45, ...), custom_call_target="tpu_custom_call" | custom-call | tf_op jit(solution)/shard_map/pallas_call | solution.py:269
  145.3 0.5 collective-permute-start.33
  145.9 0.5 fusion.3
  146.3 1.0 collective-permute-done.33
  147.3 1.2 add_convert_fusion
  148.5 9.7 %all-to-all-done.1 = bf16[8,64,2048]{2,1,0:T(8,128)(2,1)} async-done(((bf16[8,64,2048]{2,1,0:T(8,128)(2,1)}), bf16[8,64,2048]{2,1,0:T(8,128)(2,1)}, u32[]{:S(2)}, u32[]{:S(2)}) %all-to-all-start.1) | async-done | bytes 2097184 | tf_op jit(solution)/shard_map/all_to_all | solution.py:412
  158.3 3.5 %collective-permute-start.34 = (bf16[512,2048]{1,0:T(8,128)(2,1)}, bf16[512,2048]{1,0:T(8,128)(2,1)S(1)}, u32[]{:S(2)}, u32[]{:S(2)}) collective-permute-start(bf16[512,2048]{1,0:T(8,128)(2,1)} %bitcast.19.x_ref), channel_id=1, source_target_pairs={{0,2},{2,0},{1,3},{3,1},{4,6},{6,4},{5,7},{7,5},{8,10},{10,8},{9,1... | collective-permute-start | bytes 6291464 | tf_op jit(solution)/shard_map/ppermute | solution.py:332
  161.8 4.0 %shard_map.109.refs_0_ = f32[4,8,2,2,8,640]{5,4,3,2,1,0:T(8,128)} custom-call(s32[1]{0:T(128)} %bitcast.15.who, bf16[512,2048]{1,0:T(8,128)(2,1)} %bitcast.19.x_ref, bf16[2048,640]{1,0:T(8,128)(2,1)S(1)} %copy-done), custom_call_target="tpu_custom_call" | custom-call | flops 1342177280 | bytes 6291456 | tf_op jit(solution)/shard_map/pallas_call | solution.py:294
  165.8 2.8 %shard_map.110 = f32[4,8,2,2,8,640]{5,4,3,2,1,0:T(8,128)} custom-call(s32[1]{0:T(128)S(6)} %sub.3.who, bf16[512,2048]{1,0:T(8,128)(2,1)S(1)} %collective-permute-done.34.x_ref, bf16[2048,640]{1,0:T(8,128)(2,1)S(1)} %copy-done, f32[4,8,2,2,8,640]{5,4,3,2,1,0:T(8,128)} %shard_map.109.refs_0_), custom_call_target="tpu_custom_call", output_to_operand_aliasing={{}: (3, {})} | custom-call | flops 1342177280 | bytes 6291456 | tf_op jit(solution)/shard_map/pallas_call | solution.py:294
  (133 shorter events, 1.5 us)
Async XLA Ops:
  0.6 17.1 %collective-permute-start.7 = (bf16[128,2048]{1,0:T(8,128)(2,1)}, bf16[128,2048]{1,0:T(8,128)(2,1)S(1)}, u32[]{:S(2)}, u32[]{:S(2)}) collective-permute-start(bf16[128,2048]{1,0:T(8,128)(2,1)} %refs_0_.1), channel_id=1, source_target_pairs={{0,192},{64,0},{128,64},{192,128},{1,193},{65,1},{129,65},{193,129... | collective-permute-start | bytes 1572872 | tf_op jit(solution)/shard_map/ppermute | solution.py:332
  4.3 16.3 %collective-permute-start.8 = (bf16[128,2048]{1,0:T(8,128)(2,1)}, bf16[128,2048]{1,0:T(8,128)(2,1)S(1)}, u32[]{:S(2)}, u32[]{:S(2)}) collective-permute-start(bf16[128,2048]{1,0:T(8,128)(2,1)} %refs_0_.1), channel_id=1, source_target_pairs={{0,64},{64,128},{128,192},{192,0},{1,65},{65,129},{129,193},{193,1... | collective-permute-start | bytes 1572872 | tf_op jit(solution)/shard_map/ppermute | solution.py:332
  5.2 6.6 %collective-permute-start = (bf16[128,512]{1,0:T(8,128)(2,1)S(1)}, bf16[128,512]{1,0:T(8,128)(2,1)S(1)}, u32[]{:S(2)}, u32[]{:S(2)}) collective-permute-start(bf16[128,512]{1,0:T(8,128)(2,1)S(1)} %pad_maximum_fusion.3), channel_id=1, source_target_pairs={{0,4},{4,0},{1,5},{5,1},{2,6},{6,2},{3,7},{7,3},{8,12},{12,8},{9,1... | collective-permute-start | bytes 393224 | tf_op jit(solution)/shard_map/ppermute | solution.py:332
  11.9 16.6 %copy-start.24 = (bf16[384,512]{1,0:T(8,128)(2,1)}, bf16[384,512]{1,0:T(8,128)(2,1)S(1)}, u32[]{:S(2)}) copy-start(bf16[384,512]{1,0:T(8,128)(2,1)S(1)} %get-tuple-element.93.refs_5_) | copy-start | bytes 1179652
  11.9 13.9 %collective-permute-start.1 = (bf16[384,512]{1,0:T(8,128)(2,1)S(1)}, bf16[384,512]{1,0:T(8,128)(2,1)S(1)}, u32[]{:S(2)}, u32[]{:S(2)}) collective-permute-start(bf16[384,512]{1,0:T(8,128)(2,1)S(1)} %get-tuple-element.93.refs_5_), channel_id=1, source_target_pairs={{0,8},{8,16},{16,24},{24,32},{32,40},{40,48},{48,56},{56,0},{1,9},... | collective-permute-start | bytes 1179656 | tf_op jit(solution)/shard_map/ppermute | solution.py:332
  13.6 12.2 %collective-permute-start.4 = (bf16[384,512]{1,0:T(8,128)(2,1)S(1)}, bf16[384,512]{1,0:T(8,128)(2,1)S(1)}, u32[]{:S(2)}, u32[]{:S(2)}) collective-permute-start(bf16[384,512]{1,0:T(8,128)(2,1)S(1)} %get-tuple-element.93.refs_5_), channel_id=1, source_target_pairs={{0,56},{8,0},{16,8},{24,16},{32,24},{40,32},{48,40},{56,48},{1,57}... | collective-permute-start | bytes 1179656 | tf_op jit(solution)/shard_map/ppermute | solution.py:332
  17.7 10.8 %copy-start.22 = (bf16[128,2048]{1,0:T(8,128)(2,1)}, bf16[128,2048]{1,0:T(8,128)(2,1)S(1)}, u32[]{:S(2)}) copy-start(bf16[128,2048]{1,0:T(8,128)(2,1)S(1)} %collective-permute-done.7.refs_1_) | copy-start | bytes 1572868
  17.8 24.1 %collective-permute-start.10 = (bf16[64,2048]{1,0:T(8,128)(2,1)S(1)}, bf16[64,2048]{1,0:T(8,128)(2,1)S(1)}, u32[]{:S(2)}, u32[]{:S(2)}) collective-permute-start(bf16[64,2048]{1,0:T(8,128)(2,1)S(1)} %slice.238), channel_id=1, source_target_pairs={{0,192},{64,0},{128,64},{192,128},{1,193},{65,1},{129,65},{193,129... | collective-permute-start | bytes 786440 | tf_op jit(solution)/shard_map/ppermute | solution.py:332
  20.5 17.9 %copy-start.23 = (bf16[128,2048]{1,0:T(8,128)(2,1)}, bf16[128,2048]{1,0:T(8,128)(2,1)S(1)}, u32[]{:S(2)}) copy-start(bf16[128,2048]{1,0:T(8,128)(2,1)S(1)} %collective-permute-done.8.refs_2_) | copy-start | bytes 1572868
  20.6 21.4 %collective-permute-start.9 = (bf16[64,2048]{1,0:T(8,128)(2,1)S(1)}, bf16[64,2048]{1,0:T(8,128)(2,1)S(1)}, u32[]{:S(2)}, u32[]{:S(2)}) collective-permute-start(bf16[64,2048]{1,0:T(8,128)(2,1)S(1)} %slice.237), channel_id=1, source_target_pairs={{0,64},{64,128},{128,192},{192,0},{1,65},{65,129},{129,193},{193,1... | collective-permute-start | bytes 786440 | tf_op jit(solution)/shard_map/ppermute | solution.py:332
  25.7 12.7 %copy-start.15 = (bf16[384,512]{1,0:T(8,128)(2,1)}, bf16[384,512]{1,0:T(8,128)(2,1)S(1)}, u32[]{:S(2)}) copy-start(bf16[384,512]{1,0:T(8,128)(2,1)S(1)} %collective-permute-done.1.refs_6_) | copy-start | bytes 1179652
  25.7 10.0 %collective-permute-start.2 = (bf16[384,512]{1,0:T(8,128)(2,1)S(1)}, bf16[384,512]{1,0:T(8,128)(2,1)S(1)}, u32[]{:S(2)}, u32[]{:S(2)}) collective-permute-start(bf16[384,512]{1,0:T(8,128)(2,1)S(1)} %collective-permute-done.1.refs_6_), channel_id=1, source_target_pairs={{0,8},{8,16},{16,24},{24,32},{32,40},{40,48},{48,56},{56,0},{1,9},... | collective-permute-start | bytes 1179656 | tf_op jit(solution)/shard_map/ppermute | solution.py:332
  25.7 12.7 %copy-start.16 = (bf16[384,512]{1,0:T(8,128)(2,1)}, bf16[384,512]{1,0:T(8,128)(2,1)S(1)}, u32[]{:S(2)}) copy-start(bf16[384,512]{1,0:T(8,128)(2,1)S(1)} %collective-permute-done.4.refs_7_) | copy-start | bytes 1179652
  25.8 9.9 %collective-permute-start.5 = (bf16[384,512]{1,0:T(8,128)(2,1)S(1)}, bf16[384,512]{1,0:T(8,128)(2,1)S(1)}, u32[]{:S(2)}, u32[]{:S(2)}) collective-permute-start(bf16[384,512]{1,0:T(8,128)(2,1)S(1)} %collective-permute-done.4.refs_7_), channel_id=1, source_target_pairs={{0,56},{8,0},{16,8},{24,16},{32,24},{40,32},{48,40},{56,48},{1,57}... | collective-permute-start | bytes 1179656 | tf_op jit(solution)/shard_map/ppermute | solution.py:332
  35.7 11.7 %copy-start.17 = (bf16[384,512]{1,0:T(8,128)(2,1)}, bf16[384,512]{1,0:T(8,128)(2,1)S(1)}, u32[]{:S(2)}) copy-start(bf16[384,512]{1,0:T(8,128)(2,1)S(1)} %collective-permute-done.2.refs_8_) | copy-start | bytes 1179652
  35.7 9.0 %collective-permute-start.3 = (bf16[384,512]{1,0:T(8,128)(2,1)S(1)}, bf16[384,512]{1,0:T(8,128)(2,1)S(1)}, u32[]{:S(2)}, u32[]{:S(2)}) collective-permute-start(bf16[384,512]{1,0:T(8,128)(2,1)S(1)} %collective-permute-done.2.refs_8_), channel_id=1, source_target_pairs={{0,8},{8,16},{16,24},{24,32},{32,40},{40,48},{48,56},{56,0},{1,9},... | collective-permute-start | bytes 1179656 | tf_op jit(solution)/shard_map/ppermute | solution.py:332
  35.7 11.7 %copy-start.18 = (bf16[384,512]{1,0:T(8,128)(2,1)}, bf16[384,512]{1,0:T(8,128)(2,1)S(1)}, u32[]{:S(2)}) copy-start(bf16[384,512]{1,0:T(8,128)(2,1)S(1)} %collective-permute-done.5.refs_9_) | copy-start | bytes 1179652
  35.7 9.0 %collective-permute-start.6 = (bf16[384,512]{1,0:T(8,128)(2,1)S(1)}, bf16[384,512]{1,0:T(8,128)(2,1)S(1)}, u32[]{:S(2)}, u32[]{:S(2)}) collective-permute-start(bf16[384,512]{1,0:T(8,128)(2,1)S(1)} %collective-permute-done.5.refs_9_), channel_id=1, source_target_pairs={{0,56},{8,0},{16,8},{24,16},{32,24},{40,32},{48,40},{56,48},{1,57}... | collective-permute-start | bytes 1179656 | tf_op jit(solution)/shard_map/ppermute | solution.py:332
  38.5 23.2 %collective-permute-start.12 = (bf16[1280,512]{1,0:T(8,128)(2,1)S(1)}, bf16[1280,512]{1,0:T(8,128)(2,1)S(1)}, u32[]{:S(2)}, u32[]{:S(2)}) collective-permute-start(bf16[1280,512]{1,0:T(8,128)(2,1)S(1)} %slice_dynamic-update-slice_fusion), channel_id=1, source_target_pairs={{0,2},{2,0},{1,3},{3,1},{4,6},{6,4},{5,7},{7,5},{8,10},{10,8},{9,1... | collective-permute-start | bytes 3932168 | tf_op jit(solution)/shard_map/ppermute | solution.py:332
  41.9 11.2 %copy-start.29 = (bf16[64,2048]{1,0:T(8,128)(2,1)}, bf16[64,2048]{1,0:T(8,128)(2,1)S(1)}, u32[]{:S(2)}) copy-start(bf16[64,2048]{1,0:T(8,128)(2,1)S(1)} %collective-permute-done.10.refs_4_) | copy-start | bytes 786436
  41.9 7.9 %copy-start.30 = (bf16[64,2048]{1,0:T(8,128)(2,1)}, bf16[64,2048]{1,0:T(8,128)(2,1)S(1)}, u32[]{:S(2)}) copy-start(bf16[64,2048]{1,0:T(8,128)(2,1)S(1)} %collective-permute-done.9.refs_3_) | copy-start | bytes 786436
  44.7 13.9 %copy-start.13 = (bf16[384,512]{1,0:T(8,128)(2,1)}, bf16[384,512]{1,0:T(8,128)(2,1)S(1)}, u32[]{:S(2)}) copy-start(bf16[384,512]{1,0:T(8,128)(2,1)S(1)} %collective-permute-done.3.refs_11_) | copy-start | bytes 1179652
  44.7 13.9 %copy-start.14 = (bf16[384,512]{1,0:T(8,128)(2,1)}, bf16[384,512]{1,0:T(8,128)(2,1)S(1)}, u32[]{:S(2)}) copy-start(bf16[384,512]{1,0:T(8,128)(2,1)S(1)} %collective-permute-done.6.refs_12_) | copy-start | bytes 1179652
  44.8 5.1 %collective-permute-start.11 = (bf16[192,512]{1,0:T(8,128)(2,1)S(1)}, bf16[192,512]{1,0:T(8,128)(2,1)S(1)}, u32[]{:S(2)}, u32[]{:S(2)}) collective-permute-start(bf16[192,512]{1,0:T(8,128)(2,1)S(1)} %slice.193), channel_id=1, source_target_pairs={{0,56},{8,0},{16,8},{24,16},{32,24},{40,32},{48,40},{56,48},{1,57}... | collective-permute-start | bytes 589832 | tf_op jit(solution)/shard_map/ppermute | solution.py:332
  47.2 5.8 %collective-permute-start.13 = (bf16[192,512]{1,0:T(8,128)(2,1)S(1)}, bf16[192,512]{1,0:T(8,128)(2,1)S(1)}, u32[]{:S(2)}, u32[]{:S(2)}) collective-permute-start(bf16[192,512]{1,0:T(8,128)(2,1)S(1)} %slice.199), channel_id=1, source_target_pairs={{0,8},{8,16},{16,24},{24,32},{32,40},{40,48},{48,56},{56,0},{1,9},... | collective-permute-start | bytes 589832 | tf_op jit(solution)/shard_map/ppermute | solution.py:332
  49.8 11.9 %copy-start.21 = (bf16[192,512]{1,0:T(8,128)(2,1)}, bf16[192,512]{1,0:T(8,128)(2,1)S(1)}, u32[]{:S(2)}) copy-start(bf16[192,512]{1,0:T(8,128)(2,1)S(1)} %collective-permute-done.11.refs_14_) | copy-start | bytes 589828
  53.0 8.7 %copy-start.20 = (bf16[192,512]{1,0:T(8,128)(2,1)}, bf16[192,512]{1,0:T(8,128)(2,1)S(1)}, u32[]{:S(2)}) copy-start(bf16[192,512]{1,0:T(8,128)(2,1)S(1)} %collective-permute-done.13.refs_13_) | copy-start | bytes 589828
  53.1 8.6 %collective-permute-start.14 = (bf16[768,512]{1,0:T(8,128)(2,1)S(1)}, bf16[768,512]{1,0:T(8,128)(2,1)S(1)}, u32[]{:S(2)}, u32[]{:S(2)}) collective-permute-start(bf16[768,512]{1,0:T(8,128)(2,1)S(1)} %pad_maximum_fusion.1), channel_id=1, source_target_pairs={{0,2},{2,0},{1,3},{3,1},{4,6},{6,4},{5,7},{7,5},{8,10},{10,8},{9,1... | collective-permute-start | bytes 2359304 | tf_op jit(solution)/shard_map/ppermute | solution.py:332
  58.7 30.6 %collective-permute-start.19 = (bf16[8,4,32,512]{3,2,1,0:T(8,128)(2,1)S(1)}, bf16[8,4,32,512]{3,2,1,0:T(8,128)(2,1)S(1)}, u32[]{:S(2)}, u32[]{:S(2)}) collective-permute-start(bf16[8,4,32,512]{3,2,1,0:T(8,128)(2,1)S(1)} %bitcast.42), channel_id=1, source_target_pairs={{0,4},{4,0},{1,5},{5,1},{2,6},{6,2},{3,7},{7,3},{8,12},{12,8},{9,1... | collective-permute-start | bytes 3145736 | tf_op jit(solution)/shard_map/ppermute | solution.py:332
  59.2 30.5 %collective-permute-start.20 = (bf16[8,4,32,512]{3,2,1,0:T(8,128)(2,1)S(1)}, bf16[8,4,32,512]{3,2,1,0:T(8,128)(2,1)S(1)}, u32[]{:S(2)}, u32[]{:S(2)}) collective-permute-start(bf16[8,4,32,512]{3,2,1,0:T(8,128)(2,1)S(1)} %bitcast.43), channel_id=1, source_target_pairs={{0,5},{1,4},{4,1},{5,0},{2,7},{3,6},{6,3},{7,2},{8,13},{9,12},{12,... | collective-permute-start | bytes 3145736 | tf_op jit(solution)/shard_map/ppermute | solution.py:384
  86.0 3.9 %copy-start.9 = (bf16[128,2048]{1,0:T(8,128)(2,1)S(1)}, bf16[128,2048]{1,0:T(8,128)(2,1)}, u32[]{:S(2)}) copy-start(bf16[128,2048]{1,0:T(8,128)(2,1)} %param.9) | copy-start | bytes 1572868
  86.0 5.9 %collective-permute-start.15 = (bf16[32,2048]{1,0:T(8,128)(2,1)}, bf16[32,2048]{1,0:T(8,128)(2,1)S(1)}, u32[]{:S(2)}, u32[]{:S(2)}) collective-permute-start(bf16[32,2048]{1,0:T(8,128)(2,1)} %get-tuple-element.50), channel_id=1, source_target_pairs={{0,64},{64,128},{128,192},{192,0},{1,65},{65,129},{129,193},{193,1... | collective-permute-start | bytes 393224 | tf_op jit(solution)/shard_map/ppermute | solution.py:332
  86.1 9.3 %collective-permute-start.16 = (bf16[32,2048]{1,0:T(8,128)(2,1)}, bf16[32,2048]{1,0:T(8,128)(2,1)S(1)}, u32[]{:S(2)}, u32[]{:S(2)}) collective-permute-start(bf16[32,2048]{1,0:T(8,128)(2,1)} %get-tuple-element.51), channel_id=1, source_target_pairs={{0,128},{64,192},{128,0},{192,64},{1,129},{65,193},{129,1},{193,65... | collective-permute-start | bytes 393224 | tf_op jit(solution)/shard_map/ppermute | solution.py:332
  89.3 6.0 %collective-permute-start.17 = (bf16[32,2048]{1,0:T(8,128)(2,1)}, bf16[32,2048]{1,0:T(8,128)(2,1)S(1)}, u32[]{:S(2)}, u32[]{:S(2)}) collective-permute-start(bf16[32,2048]{1,0:T(8,128)(2,1)} %get-tuple-element.52), channel_id=1, source_target_pairs={{0,192},{64,0},{128,64},{192,128},{1,193},{65,1},{129,65},{193,129... | collective-permute-start | bytes 393224 | tf_op jit(solution)/shard_map/ppermute | solution.py:332
  89.4 6.0 %copy-start.31 = (bf16[64,2048]{1,0:T(8,128)(2,1)S(1)}, bf16[64,2048]{1,0:T(8,128)(2,1)}, u32[]{:S(2)}) copy-start(bf16[64,2048]{1,0:T(8,128)(2,1)} %get-tuple-element.58) | copy-start | bytes 786436
  89.4 6.0 %copy-start.7 = (bf16[32,2048]{1,0:T(8,128)(2,1)S(1)}, bf16[32,2048]{1,0:T(8,128)(2,1)}, u32[]{:S(2)}) copy-start(bf16[32,2048]{1,0:T(8,128)(2,1)} %get-tuple-element.49.r0) | copy-start | bytes 393220
  89.4 6.0 %copy-start.8 = (s32[5]{0:T(128)S(1)}, s32[5]{0:T(128)}, u32[]{:S(2)}) copy-start(s32[5]{0:T(128)} %stack.23.place) | copy-start | bytes 64
  89.4 13.5 %collective-permute-start.21 = (bf16[4,4,32,512]{3,2,1,0:T(8,128)(2,1)S(1)}, bf16[4,4,32,512]{3,2,1,0:T(8,128)(2,1)S(1)}, u32[]{:S(2)}, u32[]{:S(2)}) collective-permute-start(bf16[4,4,32,512]{3,2,1,0:T(8,128)(2,1)S(1)} %slice.249), channel_id=1, source_target_pairs={{0,5},{1,4},{4,1},{5,0},{2,7},{3,6},{6,3},{7,2},{8,13},{9,12},{12,... | collective-permute-start | bytes 1572872 | tf_op jit(solution)/shard_map/ppermute | solution.py:384
  89.8 13.2 %collective-permute-start.22 = (bf16[4,4,32,512]{3,2,1,0:T(8,128)(2,1)S(1)}, bf16[4,4,32,512]{3,2,1,0:T(8,128)(2,1)S(1)}, u32[]{:S(2)}, u32[]{:S(2)}) collective-permute-start(bf16[4,4,32,512]{3,2,1,0:T(8,128)(2,1)S(1)} %slice.250), channel_id=1, source_target_pairs={{0,4},{4,0},{1,5},{5,1},{2,6},{6,2},{3,7},{7,3},{8,12},{12,8},{9,1... | collective-permute-start | bytes 1572872 | tf_op jit(solution)/shard_map/ppermute | solution.py:332
  91.9 19.6 %collective-permute-start.25 = (bf16[80,2048]{1,0:T(8,128)(2,1)S(1)}, bf16[80,2048]{1,0:T(8,128)(2,1)}, u32[]{:S(2)}, u32[]{:S(2)}) collective-permute-start(bf16[80,2048]{1,0:T(8,128)(2,1)S(1)} %copy-done.28), channel_id=1, source_target_pairs={{0,192},{64,0},{128,64},{192,128},{1,193},{65,1},{129,65},{193,129... | collective-permute-start | bytes 983048 | tf_op jit(solution)/shard_map/ppermute | solution.py:332
  95.3 16.2 %collective-permute-start.24 = (bf16[64,2048]{1,0:T(8,128)(2,1)S(1)}, bf16[64,2048]{1,0:T(8,128)(2,1)}, u32[]{:S(2)}, u32[]{:S(2)}) collective-permute-start(bf16[64,2048]{1,0:T(8,128)(2,1)S(1)} %copy-done.31), channel_id=1, source_target_pairs={{0,64},{64,128},{128,192},{192,0},{1,65},{65,129},{129,193},{193,1... | collective-permute-start | bytes 786440 | tf_op jit(solution)/shard_map/ppermute | solution.py:332
  96.1 3.7 %collective-permute-start.18 = (bf16[2,16,512]{2,1,0:T(8,128)(2,1)S(1)}, bf16[2,16,512]{2,1,0:T(8,128)(2,1)S(1)}, u32[]{:S(2)}, u32[]{:S(2)}) collective-permute-start(bf16[2,16,512]{2,1,0:T(8,128)(2,1)S(1)} %get-tuple-element.55), channel_id=1, source_target_pairs={{0,2},{2,0},{1,3},{3,1},{4,6},{6,4},{5,7},{7,5},{8,10},{10,8},{9,1... | collective-permute-start | bytes 98312 | tf_op jit(solution)/shard_map/ppermute | solution.py:332
  103.0 3.4 %copy-start.1 = (bf16[4,4,32,512]{3,2,1,0:T(8,128)(2,1)}, bf16[4,4,32,512]{3,2,1,0:T(8,128)(2,1)S(1)}, u32[]{:S(2)}) copy-start(bf16[4,4,32,512]{3,2,1,0:T(8,128)(2,1)S(1)} %collective-permute-done.21.refs_3_) | copy-start | bytes 1572868
  103.0 3.4 %copy-start.3 = (bf16[4,4,32,512]{3,2,1,0:T(8,128)(2,1)}, bf16[4,4,32,512]{3,2,1,0:T(8,128)(2,1)S(1)}, u32[]{:S(2)}) copy-start(bf16[4,4,32,512]{3,2,1,0:T(8,128)(2,1)S(1)} %collective-permute-done.22.refs_4_) | copy-start | bytes 1572868
  103.0 8.8 %copy-start.25 = (f32[2048]{0:T(1024)S(1)}, f32[2048]{0:T(1024)}, u32[]{:S(2)}) copy-start(f32[2048]{0:T(1024)} %param.16) | copy-start | bytes 24580
  103.0 14.4 %copy-start.19 = (bf16[4,2048]{1,0:T(4,128)(2,1)S(1)}, bf16[4,2048]{1,0:T(4,128)(2,1)}, u32[]{:S(2)}) copy-start(bf16[4,2048]{1,0:T(4,128)(2,1)} %param.10) | copy-start | bytes 49156
  106.4 5.2 %collective-permute-start.23 = (bf16[16,2048]{1,0:T(8,128)(2,1)S(1)}, bf16[16,2048]{1,0:T(8,128)(2,1)S(1)}, u32[]{:S(2)}, u32[]{:S(2)}) collective-permute-start(bf16[16,2048]{1,0:T(8,128)(2,1)S(1)} %get-tuple-element.57), channel_id=1, source_target_pairs={{0,2},{2,0},{1,3},{3,1},{4,6},{6,4},{5,7},{7,5},{8,10},{10,8},{9,1... | collective-permute-start | bytes 196616 | tf_op jit(solution)/shard_map/ppermute | solution.py:332
  108.8 16.5 %collective-permute-start.26 = (bf16[144,2048]{1,0:T(8,128)(2,1)}, bf16[144,2048]{1,0:T(8,128)(2,1)}, u32[]{:S(2)}, u32[]{:S(2)}) collective-permute-start(bf16[144,2048]{1,0:T(8,128)(2,1)} %get-tuple-element.61), channel_id=1, source_target_pairs={{0,64},{64,128},{128,192},{192,0},{1,65},{65,129},{129,193},{193,1... | collective-permute-start | bytes 1769480 | tf_op jit(solution)/shard_map/ppermute | solution.py:332
  110.4 17.1 %collective-permute-start.27 = (bf16[144,2048]{1,0:T(8,128)(2,1)}, bf16[144,2048]{1,0:T(8,128)(2,1)}, u32[]{:S(2)}, u32[]{:S(2)}) collective-permute-start(bf16[144,2048]{1,0:T(8,128)(2,1)} %get-tuple-element.62), channel_id=1, source_target_pairs={{0,192},{64,0},{128,64},{192,128},{1,193},{65,1},{129,65},{193,129... | collective-permute-start | bytes 1769480 | tf_op jit(solution)/shard_map/ppermute | solution.py:332
  112.5 15.4 %all-to-all-start = ((bf16[8,8,2048]{2,1,0:T(8,128)(2,1)}), bf16[8,8,2048]{2,1,0:T(8,128)(2,1)S(1)}, u32[]{:S(2)}, u32[]{:S(2)}) async-start(bf16[8,8,2048]{2,1,0:T(8,128)(2,1)} %broadcast_in_dim.4), calls=%async_computation | async-start | bytes 524288 | tf_op jit(solution)/shard_map/all_to_all | solution.py:390
  117.4 16.5 %collective-permute-start.31 = (bf16[80,2048]{1,0:T(8,128)(2,1)}, bf16[80,2048]{1,0:T(8,128)(2,1)}, u32[]{:S(2)}, u32[]{:S(2)}) collective-permute-start(bf16[80,2048]{1,0:T(8,128)(2,1)} %collective-permute-done.25), channel_id=1, source_target_pairs={{0,192},{64,0},{128,64},{192,128},{1,193},{65,1},{129,65},{193,129... | collective-permute-start | bytes 983048 | tf_op jit(solution)/shard_map/ppermute | solution.py:332
  117.5 16.4 %collective-permute-start.30 = (bf16[64,2048]{1,0:T(8,128)(2,1)}, bf16[64,2048]{1,0:T(8,128)(2,1)}, u32[]{:S(2)}, u32[]{:S(2)}) collective-permute-start(bf16[64,2048]{1,0:T(8,128)(2,1)} %collective-permute-done.24), channel_id=1, source_target_pairs={{0,64},{64,128},{128,192},{192,0},{1,65},{65,129},{129,193},{193,1... | collective-permute-start | bytes 786440 | tf_op jit(solution)/shard_map/ppermute | solution.py:332
  119.0 21.4 %collective-permute-start.29 = (bf16[3,2048]{1,0:T(4,128)(2,1)S(1)}, bf16[3,2048]{1,0:T(4,128)(2,1)S(1)}, u32[]{:S(2)}, u32[]{:S(2)}) collective-permute-start(bf16[3,2048]{1,0:T(4,128)(2,1)S(1)} %get-tuple-element.103), channel_id=1, source_target_pairs={{2,0},{4,2},{6,4},{8,6},{10,8},{12,10},{14,12},{16,14},{18,16},{20... | collective-permute-start | bytes 36872 | tf_op jit(solution)/shard_map/ppermute | solution.py:324
  125.4 20.4 %collective-permute-start.28 = (bf16[3,2048]{1,0:T(4,128)(2,1)S(1)}, bf16[3,2048]{1,0:T(4,128)(2,1)S(1)}, u32[]{:S(2)}, u32[]{:S(2)}) collective-permute-start(bf16[3,2048]{1,0:T(4,128)(2,1)S(1)} %get-tuple-element.102), channel_id=1, source_target_pairs={{0,2},{2,4},{4,6},{6,8},{8,10},{10,12},{12,14},{14,16},{16,18},{18... | collective-permute-start | bytes 36872 | tf_op jit(solution)/shard_map/ppermute | solution.py:323
  129.5 28.8 %all-to-all-start.1 = ((bf16[8,64,2048]{2,1,0:T(8,128)(2,1)}), bf16[8,64,2048]{2,1,0:T(8,128)(2,1)}, u32[]{:S(2)}, u32[]{:S(2)}) async-start(bf16[8,64,2048]{2,1,0:T(8,128)(2,1)} %broadcast_in_dim.5), calls=%async_computation.1 | async-start | bytes 4194304 | tf_op jit(solution)/shard_map/all_to_all | solution.py:412
  135.2 5.1 %copy-start.10 = (bf16[128,2048]{1,0:T(8,128)(2,1)S(1)}, bf16[128,2048]{1,0:T(8,128)(2,1)}, u32[]{:S(2)}) copy-start(bf16[128,2048]{1,0:T(8,128)(2,1)} %param.9) | copy-start | bytes 1572868
  135.2 5.1 %copy-start.12 = (bf16[64,2048]{1,0:T(8,128)(2,1)S(1)}, bf16[64,2048]{1,0:T(8,128)(2,1)}, u32[]{:S(2)}) copy-start(bf16[64,2048]{1,0:T(8,128)(2,1)} %get-tuple-element.81) | copy-start | bytes 786436
  135.2 6.2 %copy-start.2 = (bf16[4,4,32,512]{3,2,1,0:T(8,128)(2,1)S(1)}, bf16[4,4,32,512]{3,2,1,0:T(8,128)(2,1)}, u32[]{:S(2)}) copy-start(bf16[4,4,32,512]{3,2,1,0:T(8,128)(2,1)} %copy-done.1) | copy-start | bytes 1572868
  135.2 6.3 %copy-start.4 = (bf16[4,4,32,512]{3,2,1,0:T(8,128)(2,1)S(1)}, bf16[4,4,32,512]{3,2,1,0:T(8,128)(2,1)}, u32[]{:S(2)}) copy-start(bf16[4,4,32,512]{3,2,1,0:T(8,128)(2,1)} %copy-done.3) | copy-start | bytes 1572868
  138.0 3.5 %collective-permute-start.32 = (bf16[2,128,512]{2,1,0:T(8,128)(2,1)S(1)}, bf16[2,128,512]{2,1,0:T(8,128)(2,1)S(1)}, u32[]{:S(2)}, u32[]{:S(2)}) collective-permute-start(bf16[2,128,512]{2,1,0:T(8,128)(2,1)S(1)} %get-tuple-element.73), channel_id=1, source_target_pairs={{0,2},{2,0},{1,3},{3,1},{4,6},{6,4},{5,7},{7,5},{8,10},{10,8},{9,1... | collective-permute-start | bytes 786440 | tf_op jit(solution)/shard_map/ppermute | solution.py:332
  141.5 4.3 %copy-start.11 = (bf16[64,2048]{1,0:T(8,128)(2,1)S(1)}, bf16[64,2048]{1,0:T(8,128)(2,1)}, u32[]{:S(2)}) copy-start(bf16[64,2048]{1,0:T(8,128)(2,1)} %get-tuple-element.80) | copy-start | bytes 786436
  145.3 2.0 %collective-permute-start.33 = (bf16[128,2048]{1,0:T(8,128)(2,1)S(1)}, bf16[128,2048]{1,0:T(8,128)(2,1)S(1)}, u32[]{:S(2)}, u32[]{:S(2)}) collective-permute-start(bf16[128,2048]{1,0:T(8,128)(2,1)S(1)} %get-tuple-element.75), channel_id=1, source_target_pairs={{0,2},{2,0},{1,3},{3,1},{4,6},{6,4},{5,7},{7,5},{8,10},{10,8},{9,1... | collective-permute-start | bytes 1572872 | tf_op jit(solution)/shard_map/ppermute | solution.py:332
  147.3 14.4 %copy-start = (bf16[2048,640]{1,0:T(8,128)(2,1)S(1)}, bf16[2048,640]{1,0:T(8,128)(2,1)}, u32[]{:S(2)}) copy-start(bf16[2048,640]{1,0:T(8,128)(2,1)} %w_ref.3) | copy-start | bytes 7864324
  158.3 7.5 %collective-permute-start.34 = (bf16[512,2048]{1,0:T(8,128)(2,1)}, bf16[512,2048]{1,0:T(8,128)(2,1)S(1)}, u32[]{:S(2)}, u32[]{:S(2)}) collective-permute-start(bf16[512,2048]{1,0:T(8,128)(2,1)} %bitcast.19.x_ref), channel_id=1, source_target_pairs={{0,2},{2,0},{1,3},{3,1},{4,6},{6,4},{5,7},{7,5},{8,10},{10,8},{9,1... | collective-permute-start | bytes 6291464 | tf_op jit(solution)/shard_map/ppermute | solution.py:332
  (5 other events, 7.2 us)

commit v5 on v4

--- a/solution.py
+++ b/solution.py
@@ -35,12 +35,14 @@
     n_kv = len(layout)
     q_refs, kv_refs, refs = refs[: NY + 1], refs[NY + 1 : NY + 1 + n_kv], refs[NY + 1 + n_kv :]
     outs, few_outs, refs = refs[: NY + 1], refs[NY + 1 : 2 * NY + 1], refs[2 * NY + 1 :]
-    kvs, qs, acc, m_s, l_s, stage, ahead, sems = refs
+    kvs, qs, acc, m_s, l_s, stage, ahead, sems, out_sems = refs[:9]
+    to_hbm = [pltpu.make_async_copy(v, o, out_sems.at[i]) for i, (v, o) in enumerate(zip(refs[9:], outs + few_outs))]
+    outs, few_outs = refs[9 : NY + 10], refs[NY + 10 :]
     y, z, xl, c = place[0], place[1], place[2], place[3]
-    copies = []
-
-    def copy(src, dst):
-        copies.append(pltpu.make_async_copy(src, dst, sems.at[len(copies)]))
+    first, second = [], []
+
+    def copy(src, dst, to=first):
+        to.append(pltpu.make_async_copy(src, dst, sems.at[len(first) + len(second)]))
 
     for ref, dy, halves in zip(q_refs, (0, 1, 3, 2, 2), ((0, 1), (0, 1), (0, 1), (0,), (1,))):
         for i, half in enumerate(halves):
@@ -53,13 +55,13 @@
                 if low < high:
                     slot = (2 * NZ * NX * NC - 1 - s) if half else s
                     dst = kvs.at[pl.ds(pl.multiple_of(slot * HALF + low - half * HALF, 16), high - low)]
-                    copy(ref.at[pl.ds(at + low - r0, high - low)], dst)
-    for cp in copies:
+                    copy(ref.at[pl.ds(at + low - r0, high - low)], dst, second if half else first)
+    for cp in first + second:
         cp.start()
     m_s[...] = jnp.full_like(m_s, NEG)
     l_s[...] = jnp.zeros_like(l_s)
     acc[...] = jnp.zeros_like(acc)
-    for cp in copies:
+    for cp in first:
         cp.wait()
 
     qs[...] = qs[...] * BF(1.0 / math.sqrt(HD))
@@ -125,7 +127,10 @@
         return carry
 
     ahead[...] = scores(*place_of(0), 0)
-    lax.fori_loop(0, n_whole, functools.partial(item, False), 0)
+    lax.fori_loop(0, NY * per - 1, functools.partial(item, False), 0)
+    for cp in second:
+        cp.wait()
+    lax.fori_loop(NY * per - 1, n_whole, functools.partial(item, False), 0)
     lax.fori_loop(n_whole, n_items, functools.partial(item, True), 0)
 
     lane = lax.broadcasted_iota(jnp.int32, (HALF, 128), 1)
@@ -157,21 +162,25 @@
             for p, v in enumerate(packed(blk)):
                 out[at : at + 16, p * 128 : (p + 1) * 128] = v
             out[at : at + 16, 384:] = jnp.zeros((16, HEADS * HD - 384), BF)
+        for i in (dy, NY + 1 + dy) + ((NY,) if dy == 2 else ()):
+            to_hbm[i].start()
+    for cp in to_hbm:
+        cp.wait()
 
 
 def attention(place, qs, kv):
     tok, width = qs[0].shape
     layout = [e for _, e in kv]
     hbm = pl.BlockSpec(memory_space=pl.ANY)
-    vm = pl.BlockSpec(memory_space=pltpu.VMEM)
     spans = [(r0, r0 + rows) for e in layout for _, (_, _, _, r0, rows) in e]
     n_copies = 2 * NY + sum(len([h for h in (0, 1) if max(a, h * HALF) < min(b, (h + 1) * HALF)]) for a, b in spans)
+    shapes = [jax.ShapeDtypeStruct((n, width), BF) for n in (tok + 16, tok + 16, HALF, tok + 16, HALF + 16)]
+    shapes += [jax.ShapeDtypeStruct((32, width), BF)] * NY
     return pl.pallas_call(
         functools.partial(attention_kernel, layout),
         in_specs=[pl.BlockSpec(memory_space=pltpu.SMEM)] + [hbm] * (len(qs) + len(kv)),
-        out_specs=[vm] * (2 * NY + 1),
-        out_shape=[jax.ShapeDtypeStruct((n, width), BF) for n in (tok + 16, tok + 16, HALF, tok + 16, HALF + 16)]
-        + [jax.ShapeDtypeStruct((32, width), BF)] * NY,
+        out_specs=[hbm] * len(shapes),
+        out_shape=shapes,
         scratch_shapes=[
             pltpu.VMEM((2 * SPAN, 2 * HD), BF),
             pltpu.VMEM((2 * NY, HALF, width), BF),
@@ -181,7 +190,9 @@
             pltpu.VMEM((6 * HALF, 128), F32),
             pltpu.VMEM((HB * HALF, BK), F32),
             pltpu.SemaphoreType.DMA((n_copies,)),
-        ],
+            pltpu.SemaphoreType.DMA((len(shapes),)),
+        ]
+        + [pltpu.VMEM(o.shape, BF) for o in shapes],
         compiler_params=pltpu.CompilerParams(vmem_limit_bytes=56 * 2**20),
         cost_estimate=pl.CostEstimate(flops=10**10, bytes_accessed=8 * 2**20, transcendentals=10**7),
     )(place, *qs, *[a for a, _ in kv])

time: 169 us -> 169 us (level)
  no operation moved by 1% of the time
where the time goes in v5:
time: 169 us; the launch traced here: 168 us
  starting transfers between devices  68.4 us (40%)
  waiting for transfers between devices  43.5 us (26%)
  Pallas kernels  39.4 us (23%)
  local copies, waits for them, and re-layouts  10.1 us (6%)
  other arithmetic  5.28 us (3%)
    ppermute x31, starting transfers between devices, shift(): return lax.ppermute(x, axis, [(i, (i + by) % count) for i in range(count)])  51 us
    ppermute x31, waiting for transfers between devices, shift(): return lax.ppermute(x, axis, [(i, (i + by) % count) for i in range(count)])  30.4 us
    pallas_call x1, Pallas kernels, attention(): pl.pallas_call(functools.partial(attention_kernel, layout), in_specs=[pl....  21.8 us
    all_to_all x1, waiting for transfers between devices, body(): every = lax.all_to_all(copies, ('y', 'xl'), 0, 0).reshape(-1, width)  9.75 us
    pallas_call x2, Pallas kernels, project(): pl.pallas_call(functools.partial(project_kernel, rows, [p for _, p in wei...  7.21 us
    pallas_call x2, Pallas kernels, lens(): pl.pallas_call(lens_kernel, grid_spec=pltpu.PrefetchScalarGridSpec(num_sc...  6.89 us
    all_to_all x1, starting transfers between devices, body(): lax.all_to_all(jnp.broadcast_to(a[None], (n,) + a.shape), axes, 0, 0)  4.82 us
    all_to_all x1, starting transfers between devices, body(): every = lax.all_to_all(copies, ('y', 'xl'), 0, 0).reshape(-1, width)  4.34 us
  transfers between devices with their start and end apart: 37, of which 14 were waited for; matrix products, arithmetic and copies ran while one was open for 8% of the time, Pallas kernels for 22%

profile of v5, /device:TPU:1, one launch (start us, length us, event | category | flops | bytes accessed | tf_op | source)
XLA Modules:
  0.0 168.0 jit_solution(12541578885638699078)
XLA Ops:
  0.6 3.6 %collective-permute-start.7 = (bf16[128,2048]{1,0:T(8,128)(2,1)}, bf16[128,2048]{1,0:T(8,128)(2,1)S(1)}, u32[]{:S(2)}, u32[]{:S(2)}) collective-permute-start(bf16[128,2048]{1,0:T(8,128)(2,1)} %refs_0_.1), channel_id=1, source_target_pairs={{0,192},{64,0},{128,64},{192,128},{1,193},{65,1},{129,65},{193,129... | collective-permute-start | bytes 1572872 | tf_op jit(solution)/shard_map/ppermute | solution.py:343
  4.3 0.9 pad_maximum_fusion.3
  5.2 1.3 collective-permute-start
  6.5 1.6 fusion.18
  8.1 1.0 slice_select_fusion
  9.1 0.9 fusion.20
  10.0 1.0 slice.236
  11.1 0.7 stack.23.place
  11.9 1.7 %collective-permute-start.1 = (bf16[384,512]{1,0:T(8,128)(2,1)S(1)}, bf16[384,512]{1,0:T(8,128)(2,1)S(1)}, u32[]{:S(2)}, u32[]{:S(2)}) collective-permute-start(bf16[384,512]{1,0:T(8,128)(2,1)S(1)} %get-tuple-element.93.refs_5_), channel_id=1, source_target_pairs={{0,8},{8,16},{16,24},{24,32},{32,40},{40,48},{48,56},{56,0},{1,9},... | collective-permute-start | bytes 1179656 | tf_op jit(solution)/shard_map/ppermute | solution.py:343
  13.6 4.0 %collective-permute-start.4 = (bf16[384,512]{1,0:T(8,128)(2,1)S(1)}, bf16[384,512]{1,0:T(8,128)(2,1)S(1)}, u32[]{:S(2)}, u32[]{:S(2)}) collective-permute-start(bf16[384,512]{1,0:T(8,128)(2,1)S(1)} %get-tuple-element.93.refs_5_), channel_id=1, source_target_pairs={{0,56},{8,0},{16,8},{24,16},{32,24},{40,32},{48,40},{56,48},{1,57}... | collective-permute-start | bytes 1179656 | tf_op jit(solution)/shard_map/ppermute | solution.py:343
  17.8 2.8 %collective-permute-start.10 = (bf16[64,2048]{1,0:T(8,128)(2,1)S(1)}, bf16[64,2048]{1,0:T(8,128)(2,1)S(1)}, u32[]{:S(2)}, u32[]{:S(2)}) collective-permute-start(bf16[64,2048]{1,0:T(8,128)(2,1)S(1)} %slice.238), channel_id=1, source_target_pairs={{0,192},{64,0},{128,64},{192,128},{1,193},{65,1},{129,65},{193,129... | collective-permute-start | bytes 786440 | tf_op jit(solution)/shard_map/ppermute | solution.py:343
  20.6 5.1 %collective-permute-done.1.refs_6_ = bf16[384,512]{1,0:T(8,128)(2,1)S(1)} collective-permute-done((bf16[384,512]{1,0:T(8,128)(2,1)S(1)}, bf16[384,512]{1,0:T(8,128)(2,1)S(1)}, u32[]{:S(2)}, u32[]{:S(2)}) %collective-permute-start.1) | collective-permute-done | bytes 393248 | tf_op jit(solution)/shard_map/ppermute | solution.py:343
  25.8 2.7 %collective-permute-start.5 = (bf16[384,512]{1,0:T(8,128)(2,1)S(1)}, bf16[384,512]{1,0:T(8,128)(2,1)S(1)}, u32[]{:S(2)}, u32[]{:S(2)}) collective-permute-start(bf16[384,512]{1,0:T(8,128)(2,1)S(1)} %collective-permute-done.4.refs_7_), channel_id=1, source_target_pairs={{0,56},{8,0},{16,8},{24,16},{32,24},{40,32},{48,40},{56,48},{1,57}... | collective-permute-start | bytes 1179656 | tf_op jit(solution)/shard_map/ppermute | solution.py:343
  28.5 7.2 %collective-permute-done.2.refs_8_ = bf16[384,512]{1,0:T(8,128)(2,1)S(1)} collective-permute-done((bf16[384,512]{1,0:T(8,128)(2,1)S(1)}, bf16[384,512]{1,0:T(8,128)(2,1)S(1)}, u32[]{:S(2)}, u32[]{:S(2)}) %collective-permute-start.2) | collective-permute-done | bytes 393248 | tf_op jit(solution)/shard_map/ppermute | solution.py:343
  35.7 2.7 %collective-permute-start.6 = (bf16[384,512]{1,0:T(8,128)(2,1)S(1)}, bf16[384,512]{1,0:T(8,128)(2,1)S(1)}, u32[]{:S(2)}, u32[]{:S(2)}) collective-permute-start(bf16[384,512]{1,0:T(8,128)(2,1)S(1)} %collective-permute-done.5.refs_9_), channel_id=1, source_target_pairs={{0,56},{8,0},{16,8},{24,16},{32,24},{40,32},{48,40},{56,48},{1,57}... | collective-permute-start | bytes 1179656 | tf_op jit(solution)/shard_map/ppermute | solution.py:343
  38.5 3.4 %collective-permute-start.12 = (bf16[1280,512]{1,0:T(8,128)(2,1)S(1)}, bf16[1280,512]{1,0:T(8,128)(2,1)S(1)}, u32[]{:S(2)}, u32[]{:S(2)}) collective-permute-start(bf16[1280,512]{1,0:T(8,128)(2,1)S(1)} %slice_dynamic-update-slice_fusion), channel_id=1, source_target_pairs={{0,2},{2,0},{1,3},{3,1},{4,6},{6,4},{5,7},{7,5},{8,10},{10,8},{9,1... | collective-permute-start | bytes 3932168 | tf_op jit(solution)/shard_map/ppermute | solution.py:343
  41.9 2.8 %collective-permute-done.3.refs_11_ = bf16[384,512]{1,0:T(8,128)(2,1)S(1)} collective-permute-done((bf16[384,512]{1,0:T(8,128)(2,1)S(1)}, bf16[384,512]{1,0:T(8,128)(2,1)S(1)}, u32[]{:S(2)}, u32[]{:S(2)}) %collective-permute-start.3) | collective-permute-done | bytes 393248 | tf_op jit(solution)/shard_map/ppermute | solution.py:343
  44.8 2.5 %collective-permute-start.11 = (bf16[192,512]{1,0:T(8,128)(2,1)S(1)}, bf16[192,512]{1,0:T(8,128)(2,1)S(1)}, u32[]{:S(2)}, u32[]{:S(2)}) collective-permute-start(bf16[192,512]{1,0:T(8,128)(2,1)S(1)} %slice.193), channel_id=1, source_target_pairs={{0,56},{8,0},{16,8},{24,16},{32,24},{40,32},{48,40},{56,48},{1,57}... | collective-permute-start | bytes 589832 | tf_op jit(solution)/shard_map/ppermute | solution.py:343
  47.4 2.4 %collective-permute-done.11.refs_14_ = bf16[192,512]{1,0:T(8,128)(2,1)S(1)} collective-permute-done((bf16[192,512]{1,0:T(8,128)(2,1)S(1)}, bf16[192,512]{1,0:T(8,128)(2,1)S(1)}, u32[]{:S(2)}, u32[]{:S(2)}) %collective-permute-start.11) | collective-permute-done | bytes 196640 | tf_op jit(solution)/shard_map/ppermute | solution.py:343
  49.9 3.2 %collective-permute-done.13.refs_13_ = bf16[192,512]{1,0:T(8,128)(2,1)S(1)} collective-permute-done((bf16[192,512]{1,0:T(8,128)(2,1)S(1)}, bf16[192,512]{1,0:T(8,128)(2,1)S(1)}, u32[]{:S(2)}, u32[]{:S(2)}) %collective-permute-start.13) | collective-permute-done | bytes 196640 | tf_op jit(solution)/shard_map/ppermute | solution.py:343
  53.1 5.5 %collective-permute-start.14 = (bf16[768,512]{1,0:T(8,128)(2,1)S(1)}, bf16[768,512]{1,0:T(8,128)(2,1)S(1)}, u32[]{:S(2)}, u32[]{:S(2)}) collective-permute-start(bf16[768,512]{1,0:T(8,128)(2,1)S(1)} %pad_maximum_fusion.1), channel_id=1, source_target_pairs={{0,2},{2,0},{1,3},{3,1},{4,6},{6,4},{5,7},{7,5},{8,10},{10,8},{9,1... | collective-permute-start | bytes 2359304 | tf_op jit(solution)/shard_map/ppermute | solution.py:343
  58.7 0.5 collective-permute-start.19
  59.2 2.5 %collective-permute-start.20 = (bf16[8,4,32,512]{3,2,1,0:T(8,128)(2,1)S(1)}, bf16[8,4,32,512]{3,2,1,0:T(8,128)(2,1)S(1)}, u32[]{:S(2)}, u32[]{:S(2)}) collective-permute-start(bf16[8,4,32,512]{3,2,1,0:T(8,128)(2,1)S(1)} %bitcast.43), channel_id=1, source_target_pairs={{0,5},{1,4},{4,1},{5,0},{2,7},{3,6},{6,3},{7,2},{8,13},{9,12},{12,... | collective-permute-start | bytes 3145736 | tf_op jit(solution)/shard_map/ppermute | solution.py:395
  61.7 1.0 copy-done.26
  62.8 0.9 copy-done.27
  63.7 21.8 %shard_map.104 = (bf16[144,2048]{1,0:T(8,128)(2,1)}, bf16[144,2048]{1,0:T(8,128)(2,1)}, bf16[64,2048]{1,0:T(8,128)(2,1)}, bf16[144,2048]{1,0:T(8,128)(2,1)}, bf1...) custom-call(s32[5]{0:T(128)} %stack.23.place, ...), custom_call_target="tpu_custom_call" | custom-call | flops 10000000000 | bytes 8388608 | tf_op jit(solution)/shard_map/pallas_call | solution.py:179
  85.6 3.2 %collective-permute-start.16 = (bf16[32,2048]{1,0:T(8,128)(2,1)}, bf16[32,2048]{1,0:T(8,128)(2,1)S(1)}, u32[]{:S(2)}, u32[]{:S(2)}) collective-permute-start(bf16[32,2048]{1,0:T(8,128)(2,1)} %get-tuple-element.51), channel_id=1, source_target_pairs={{0,128},{64,192},{128,0},{192,64},{1,129},{65,193},{129,1},{193,65... | collective-permute-start | bytes 393224 | tf_op jit(solution)/shard_map/ppermute | solution.py:343
  88.9 0.3 collective-permute-start.21
  89.4 0.9 fusion.16
  90.2 1.2 collective-permute-done.15.r1
  91.5 0.9 collective-permute-start.25
  92.3 2.5 %collective-permute-done.16.r2 = bf16[32,2048]{1,0:T(8,128)(2,1)S(1)} collective-permute-done((bf16[32,2048]{1,0:T(8,128)(2,1)}, bf16[32,2048]{1,0:T(8,128)(2,1)S(1)}, u32[]{:S(2)}, u32[]{:S(2)}) %collective-permute-start.16) | collective-permute-done | bytes 131104 | tf_op jit(solution)/shard_map/ppermute | solution.py:343
  94.9 0.8 shard_map.105
  95.7 3.1 %collective-permute-start.18 = (bf16[2,16,512]{2,1,0:T(8,128)(2,1)S(1)}, bf16[2,16,512]{2,1,0:T(8,128)(2,1)S(1)}, u32[]{:S(2)}, u32[]{:S(2)}) collective-permute-start(bf16[2,16,512]{2,1,0:T(8,128)(2,1)S(1)} %get-tuple-element.55), channel_id=1, source_target_pairs={{0,2},{2,0},{1,3},{3,1},{4,6},{6,4},{5,7},{7,5},{8,10},{10,8},{9,1... | collective-permute-start | bytes 98312 | tf_op jit(solution)/shard_map/ppermute | solution.py:343
  98.8 0.8 collective-permute-done.18.b_ref
  99.6 2.9 %collective-permute-done.21.refs_3_ = bf16[4,4,32,512]{3,2,1,0:T(8,128)(2,1)S(1)} collective-permute-done((bf16[4,4,32,512]{3,2,1,0:T(8,128)(2,1)S(1)}, bf16[4,4,32,512]{3,2,1,0:T(8,128)(2,1)S(1)}, u32[]{:S(2)}, u32[]{:S(2)}) %collective-permute-start.21) | collective-permute-done | bytes 524320 | tf_op jit(solution)/shard_map/ppermute | solution.py:395
  102.5 3.4 %shard_map.106 = (f32[16,2048]{1,0:T(8,128)S(1)}, bf16[16,2048]{1,0:T(8,128)(2,1)S(1)}) custom-call(s32[5]{0:T(128)S(1)} %copy-done.8, bf16[2,16,512]{2,1,0:T(8,128)(2,1)S(1)} %get-tuple-element.54.a_ref, bf16[2,16,512]{2,1,0:T(8,128)(2,1)S(1)} %collective-permute-done.18.b_ref, bf16[8,4,32,512]{3,2,1,0:T(8,128)(2,1)S(1)} %bitcast.44, ...), custom_call_target="tpu_custom_call" | custom-call | tf_op jit(solution)/shard_map/pallas_call | solution.py:280
  105.9 2.2 %collective-permute-start.23 = (bf16[16,2048]{1,0:T(8,128)(2,1)S(1)}, bf16[16,2048]{1,0:T(8,128)(2,1)S(1)}, u32[]{:S(2)}, u32[]{:S(2)}) collective-permute-start(bf16[16,2048]{1,0:T(8,128)(2,1)S(1)} %get-tuple-element.57), channel_id=1, source_target_pairs={{0,2},{2,0},{1,3},{3,1},{4,6},{6,4},{5,7},{7,5},{8,10},{10,8},{9,1... | collective-permute-start | bytes 196616 | tf_op jit(solution)/shard_map/ppermute | solution.py:343
  108.1 1.5 collective-permute-start.26
  109.7 1.2 collective-permute-start.27
  110.9 0.1 fusion.6
  111.1 0.7 broadcast_in_dim.4
  111.8 4.8 %all-to-all-start = ((bf16[8,8,2048]{2,1,0:T(8,128)(2,1)}), bf16[8,8,2048]{2,1,0:T(8,128)(2,1)S(1)}, u32[]{:S(2)}, u32[]{:S(2)}) async-start(bf16[8,8,2048]{2,1,0:T(8,128)(2,1)} %broadcast_in_dim.4), calls=%async_computation | async-start | bytes 524288 | tf_op jit(solution)/shard_map/all_to_all | solution.py:401
  116.8 1.5 collective-permute-start.30
  118.3 3.3 %collective-permute-start.29 = (bf16[3,2048]{1,0:T(4,128)(2,1)S(1)}, bf16[3,2048]{1,0:T(4,128)(2,1)S(1)}, u32[]{:S(2)}, u32[]{:S(2)}) collective-permute-start(bf16[3,2048]{1,0:T(4,128)(2,1)S(1)} %get-tuple-element.103), channel_id=1, source_target_pairs={{2,0},{4,2},{6,4},{8,6},{10,8},{12,10},{14,12},{16,14},{18,16},{20... | collective-permute-start | bytes 36872 | tf_op jit(solution)/shard_map/ppermute | solution.py:335
  121.6 3.0 %collective-permute-done.26.r1 = bf16[144,2048]{1,0:T(8,128)(2,1)} collective-permute-done((bf16[144,2048]{1,0:T(8,128)(2,1)}, bf16[144,2048]{1,0:T(8,128)(2,1)}, u32[]{:S(2)}, u32[]{:S(2)}) %collective-permute-start.26) | collective-permute-done | bytes 589856 | tf_op jit(solution)/shard_map/ppermute | solution.py:343
  124.7 2.1 %collective-permute-start.28 = (bf16[3,2048]{1,0:T(4,128)(2,1)S(1)}, bf16[3,2048]{1,0:T(4,128)(2,1)S(1)}, u32[]{:S(2)}, u32[]{:S(2)}) collective-permute-start(bf16[3,2048]{1,0:T(4,128)(2,1)S(1)} %get-tuple-element.102), channel_id=1, source_target_pairs={{0,2},{2,4},{4,6},{6,8},{8,10},{10,12},{12,14},{14,16},{16,18},{18... | collective-permute-start | bytes 36872 | tf_op jit(solution)/shard_map/ppermute | solution.py:334
  126.8 0.5 all-to-all-done
  127.2 1.6 broadcast_in_dim.5
  128.8 4.3 %all-to-all-start.1 = ((bf16[8,64,2048]{2,1,0:T(8,128)(2,1)}), bf16[8,64,2048]{2,1,0:T(8,128)(2,1)}, u32[]{:S(2)}, u32[]{:S(2)}) async-start(bf16[8,64,2048]{2,1,0:T(8,128)(2,1)} %broadcast_in_dim.5), calls=%async_computation.1 | async-start | bytes 4194304 | tf_op jit(solution)/shard_map/all_to_all | solution.py:423
  133.2 1.2 pad_maximum_fusion.2.r2
  134.4 0.2 copy-done.6
  134.6 2.7 %shard_map.107 = (bf16[2,128,512]{2,1,0:T(8,128)(2,1)S(1)}, bf16[2,128,512]{2,1,0:T(8,128)(2,1)S(1)}) custom-call(s32[5]{0:T(128)S(1)} %copy-done.8, bf16[144,2048]{1,0:T(8,128)(2,1)S(1)} %copy-done.6, bf16[144,2048]{1,0:T(8,128)(2,1)} %collective-permute-done.26.r1, bf16[144,2048]{1,0:T(8,128)(2,1)S(1)} %pad_maximum_fusion.2.r2, ...), custom_call_target="tpu_custom_call" | custom-call | tf_op jit(solution)/shard_map/pallas_call | solution.py:241
  137.3 2.4 %collective-permute-start.32 = (bf16[2,128,512]{2,1,0:T(8,128)(2,1)S(1)}, bf16[2,128,512]{2,1,0:T(8,128)(2,1)S(1)}, u32[]{:S(2)}, u32[]{:S(2)}) collective-permute-start(bf16[2,128,512]{2,1,0:T(8,128)(2,1)S(1)} %get-tuple-element.73), channel_id=1, source_target_pairs={{0,2},{2,0},{1,3},{3,1},{4,6},{6,4},{5,7},{7,5},{8,10},{10,8},{9,1... | collective-permute-start | bytes 786440 | tf_op jit(solution)/shard_map/ppermute | solution.py:343
  139.7 1.0 collective-permute-done.32.b_ref
  140.8 3.8 %shard_map.108 = (f32[128,2048]{1,0:T(8,128)S(1)}, bf16[128,2048]{1,0:T(8,128)(2,1)S(1)}) custom-call(s32[5]{0:T(128)S(1)} %copy-done.8, bf16[2,128,512]{2,1,0:T(8,128)(2,1)S(1)} %get-tuple-element.72.a_ref, bf16[2,128,512]{2,1,0:T(8,128)(2,1)S(1)} %collective-permute-done.32.b_ref, bf16[8,4,32,512]{3,2,1,0:T(8,128)(2,1)S(1)} %bitcast.45, ...), custom_call_target="tpu_custom_call" | custom-call | tf_op jit(solution)/shard_map/pallas_call | solution.py:280
  144.6 0.5 collective-permute-start.33
  145.2 0.5 fusion.3
  145.6 1.0 collective-permute-done.33
  146.6 1.2 add_convert_fusion
  147.8 9.7 %all-to-all-done.1 = bf16[8,64,2048]{2,1,0:T(8,128)(2,1)} async-done(((bf16[8,64,2048]{2,1,0:T(8,128)(2,1)}), bf16[8,64,2048]{2,1,0:T(8,128)(2,1)}, u32[]{:S(2)}, u32[]{:S(2)}) %all-to-all-start.1) | async-done | bytes 2097184 | tf_op jit(solution)/shard_map/all_to_all | solution.py:423
  157.6 3.5 %collective-permute-start.34 = (bf16[512,2048]{1,0:T(8,128)(2,1)}, bf16[512,2048]{1,0:T(8,128)(2,1)S(1)}, u32[]{:S(2)}, u32[]{:S(2)}) collective-permute-start(bf16[512,2048]{1,0:T(8,128)(2,1)} %bitcast.19.x_ref), channel_id=1, source_target_pairs={{0,2},{2,0},{1,3},{3,1},{4,6},{6,4},{5,7},{7,5},{8,10},{10,8},{9,1... | collective-permute-start | bytes 6291464 | tf_op jit(solution)/shard_map/ppermute | solution.py:343
  161.1 4.0 %shard_map.109.refs_0_ = f32[4,8,2,2,8,640]{5,4,3,2,1,0:T(8,128)} custom-call(s32[1]{0:T(128)} %bitcast.15.who, bf16[512,2048]{1,0:T(8,128)(2,1)} %bitcast.19.x_ref, bf16[2048,640]{1,0:T(8,128)(2,1)S(1)} %copy-done), custom_call_target="tpu_custom_call" | custom-call | flops 1342177280 | bytes 6291456 | tf_op jit(solution)/shard_map/pallas_call | solution.py:305
  165.1 2.8 %shard_map.110 = f32[4,8,2,2,8,640]{5,4,3,2,1,0:T(8,128)} custom-call(s32[1]{0:T(128)S(6)} %sub.3.who, bf16[512,2048]{1,0:T(8,128)(2,1)S(1)} %collective-permute-done.34.x_ref, bf16[2048,640]{1,0:T(8,128)(2,1)S(1)} %copy-done, f32[4,8,2,2,8,640]{5,4,3,2,1,0:T(8,128)} %shard_map.109.refs_0_), custom_call_target="tpu_custom_call", output_to_operand_aliasing={{}: (3, {})} | custom-call | flops 1342177280 | bytes 6291456 | tf_op jit(solution)/shard_map/pallas_call | solution.py:305
  (133 shorter events, 1.5 us)
Async XLA Ops:
  0.6 17.1 %collective-permute-start.7 = (bf16[128,2048]{1,0:T(8,128)(2,1)}, bf16[128,2048]{1,0:T(8,128)(2,1)S(1)}, u32[]{:S(2)}, u32[]{:S(2)}) collective-permute-start(bf16[128,2048]{1,0:T(8,128)(2,1)} %refs_0_.1), channel_id=1, source_target_pairs={{0,192},{64,0},{128,64},{192,128},{1,193},{65,1},{129,65},{193,129... | collective-permute-start | bytes 1572872 | tf_op jit(solution)/shard_map/ppermute | solution.py:343
  4.3 16.3 %collective-permute-start.8 = (bf16[128,2048]{1,0:T(8,128)(2,1)}, bf16[128,2048]{1,0:T(8,128)(2,1)S(1)}, u32[]{:S(2)}, u32[]{:S(2)}) collective-permute-start(bf16[128,2048]{1,0:T(8,128)(2,1)} %refs_0_.1), channel_id=1, source_target_pairs={{0,64},{64,128},{128,192},{192,0},{1,65},{65,129},{129,193},{193,1... | collective-permute-start | bytes 1572872 | tf_op jit(solution)/shard_map/ppermute | solution.py:343
  5.2 6.6 %collective-permute-start = (bf16[128,512]{1,0:T(8,128)(2,1)S(1)}, bf16[128,512]{1,0:T(8,128)(2,1)S(1)}, u32[]{:S(2)}, u32[]{:S(2)}) collective-permute-start(bf16[128,512]{1,0:T(8,128)(2,1)S(1)} %pad_maximum_fusion.3), channel_id=1, source_target_pairs={{0,4},{4,0},{1,5},{5,1},{2,6},{6,2},{3,7},{7,3},{8,12},{12,8},{9,1... | collective-permute-start | bytes 393224 | tf_op jit(solution)/shard_map/ppermute | solution.py:343
  11.9 16.6 %copy-start.24 = (bf16[384,512]{1,0:T(8,128)(2,1)}, bf16[384,512]{1,0:T(8,128)(2,1)S(1)}, u32[]{:S(2)}) copy-start(bf16[384,512]{1,0:T(8,128)(2,1)S(1)} %get-tuple-element.93.refs_5_) | copy-start | bytes 1179652
  11.9 13.9 %collective-permute-start.1 = (bf16[384,512]{1,0:T(8,128)(2,1)S(1)}, bf16[384,512]{1,0:T(8,128)(2,1)S(1)}, u32[]{:S(2)}, u32[]{:S(2)}) collective-permute-start(bf16[384,512]{1,0:T(8,128)(2,1)S(1)} %get-tuple-element.93.refs_5_), channel_id=1, source_target_pairs={{0,8},{8,16},{16,24},{24,32},{32,40},{40,48},{48,56},{56,0},{1,9},... | collective-permute-start | bytes 1179656 | tf_op jit(solution)/shard_map/ppermute | solution.py:343
  13.6 12.2 %collective-permute-start.4 = (bf16[384,512]{1,0:T(8,128)(2,1)S(1)}, bf16[384,512]{1,0:T(8,128)(2,1)S(1)}, u32[]{:S(2)}, u32[]{:S(2)}) collective-permute-start(bf16[384,512]{1,0:T(8,128)(2,1)S(1)} %get-tuple-element.93.refs_5_), channel_id=1, source_target_pairs={{0,56},{8,0},{16,8},{24,16},{32,24},{40,32},{48,40},{56,48},{1,57}... | collective-permute-start | bytes 1179656 | tf_op jit(solution)/shard_map/ppermute | solution.py:343
  17.7 10.8 %copy-start.22 = (bf16[128,2048]{1,0:T(8,128)(2,1)}, bf16[128,2048]{1,0:T(8,128)(2,1)S(1)}, u32[]{:S(2)}) copy-start(bf16[128,2048]{1,0:T(8,128)(2,1)S(1)} %collective-permute-done.7.refs_1_) | copy-start | bytes 1572868
  17.8 24.1 %collective-permute-start.10 = (bf16[64,2048]{1,0:T(8,128)(2,1)S(1)}, bf16[64,2048]{1,0:T(8,128)(2,1)S(1)}, u32[]{:S(2)}, u32[]{:S(2)}) collective-permute-start(bf16[64,2048]{1,0:T(8,128)(2,1)S(1)} %slice.238), channel_id=1, source_target_pairs={{0,192},{64,0},{128,64},{192,128},{1,193},{65,1},{129,65},{193,129... | collective-permute-start | bytes 786440 | tf_op jit(solution)/shard_map/ppermute | solution.py:343
  20.5 17.9 %copy-start.23 = (bf16[128,2048]{1,0:T(8,128)(2,1)}, bf16[128,2048]{1,0:T(8,128)(2,1)S(1)}, u32[]{:S(2)}) copy-start(bf16[128,2048]{1,0:T(8,128)(2,1)S(1)} %collective-permute-done.8.refs_2_) | copy-start | bytes 1572868
  20.6 21.4 %collective-permute-start.9 = (bf16[64,2048]{1,0:T(8,128)(2,1)S(1)}, bf16[64,2048]{1,0:T(8,128)(2,1)S(1)}, u32[]{:S(2)}, u32[]{:S(2)}) collective-permute-start(bf16[64,2048]{1,0:T(8,128)(2,1)S(1)} %slice.237), channel_id=1, source_target_pairs={{0,64},{64,128},{128,192},{192,0},{1,65},{65,129},{129,193},{193,1... | collective-permute-start | bytes 786440 | tf_op jit(solution)/shard_map/ppermute | solution.py:343
  25.7 12.7 %copy-start.15 = (bf16[384,512]{1,0:T(8,128)(2,1)}, bf16[384,512]{1,0:T(8,128)(2,1)S(1)}, u32[]{:S(2)}) copy-start(bf16[384,512]{1,0:T(8,128)(2,1)S(1)} %collective-permute-done.1.refs_6_) | copy-start | bytes 1179652
  25.7 10.0 %collective-permute-start.2 = (bf16[384,512]{1,0:T(8,128)(2,1)S(1)}, bf16[384,512]{1,0:T(8,128)(2,1)S(1)}, u32[]{:S(2)}, u32[]{:S(2)}) collective-permute-start(bf16[384,512]{1,0:T(8,128)(2,1)S(1)} %collective-permute-done.1.refs_6_), channel_id=1, source_target_pairs={{0,8},{8,16},{16,24},{24,32},{32,40},{40,48},{48,56},{56,0},{1,9},... | collective-permute-start | bytes 1179656 | tf_op jit(solution)/shard_map/ppermute | solution.py:343
  25.7 12.7 %copy-start.16 = (bf16[384,512]{1,0:T(8,128)(2,1)}, bf16[384,512]{1,0:T(8,128)(2,1)S(1)}, u32[]{:S(2)}) copy-start(bf16[384,512]{1,0:T(8,128)(2,1)S(1)} %collective-permute-done.4.refs_7_) | copy-start | bytes 1179652
  25.8 9.9 %collective-permute-start.5 = (bf16[384,512]{1,0:T(8,128)(2,1)S(1)}, bf16[384,512]{1,0:T(8,128)(2,1)S(1)}, u32[]{:S(2)}, u32[]{:S(2)}) collective-permute-start(bf16[384,512]{1,0:T(8,128)(2,1)S(1)} %collective-permute-done.4.refs_7_), channel_id=1, source_target_pairs={{0,56},{8,0},{16,8},{24,16},{32,24},{40,32},{48,40},{56,48},{1,57}... | collective-permute-start | bytes 1179656 | tf_op jit(solution)/shard_map/ppermute | solution.py:343
  35.7 11.7 %copy-start.17 = (bf16[384,512]{1,0:T(8,128)(2,1)}, bf16[384,512]{1,0:T(8,128)(2,1)S(1)}, u32[]{:S(2)}) copy-start(bf16[384,512]{1,0:T(8,128)(2,1)S(1)} %collective-permute-done.2.refs_8_) | copy-start | bytes 1179652
  35.7 9.0 %collective-permute-start.3 = (bf16[384,512]{1,0:T(8,128)(2,1)S(1)}, bf16[384,512]{1,0:T(8,128)(2,1)S(1)}, u32[]{:S(2)}, u32[]{:S(2)}) collective-permute-start(bf16[384,512]{1,0:T(8,128)(2,1)S(1)} %collective-permute-done.2.refs_8_), channel_id=1, source_target_pairs={{0,8},{8,16},{16,24},{24,32},{32,40},{40,48},{48,56},{56,0},{1,9},... | collective-permute-start | bytes 1179656 | tf_op jit(solution)/shard_map/ppermute | solution.py:343
  35.7 11.7 %copy-start.18 = (bf16[384,512]{1,0:T(8,128)(2,1)}, bf16[384,512]{1,0:T(8,128)(2,1)S(1)}, u32[]{:S(2)}) copy-start(bf16[384,512]{1,0:T(8,128)(2,1)S(1)} %collective-permute-done.5.refs_9_) | copy-start | bytes 1179652
  35.7 9.0 %collective-permute-start.6 = (bf16[384,512]{1,0:T(8,128)(2,1)S(1)}, bf16[384,512]{1,0:T(8,128)(2,1)S(1)}, u32[]{:S(2)}, u32[]{:S(2)}) collective-permute-start(bf16[384,512]{1,0:T(8,128)(2,1)S(1)} %collective-permute-done.5.refs_9_), channel_id=1, source_target_pairs={{0,56},{8,0},{16,8},{24,16},{32,24},{40,32},{48,40},{56,48},{1,57}... | collective-permute-start | bytes 1179656 | tf_op jit(solution)/shard_map/ppermute | solution.py:343
  38.5 23.2 %collective-permute-start.12 = (bf16[1280,512]{1,0:T(8,128)(2,1)S(1)}, bf16[1280,512]{1,0:T(8,128)(2,1)S(1)}, u32[]{:S(2)}, u32[]{:S(2)}) collective-permute-start(bf16[1280,512]{1,0:T(8,128)(2,1)S(1)} %slice_dynamic-update-slice_fusion), channel_id=1, source_target_pairs={{0,2},{2,0},{1,3},{3,1},{4,6},{6,4},{5,7},{7,5},{8,10},{10,8},{9,1... | collective-permute-start | bytes 3932168 | tf_op jit(solution)/shard_map/ppermute | solution.py:343
  41.9 11.2 %copy-start.29 = (bf16[64,2048]{1,0:T(8,128)(2,1)}, bf16[64,2048]{1,0:T(8,128)(2,1)S(1)}, u32[]{:S(2)}) copy-start(bf16[64,2048]{1,0:T(8,128)(2,1)S(1)} %collective-permute-done.10.refs_4_) | copy-start | bytes 786436
  41.9 7.9 %copy-start.30 = (bf16[64,2048]{1,0:T(8,128)(2,1)}, bf16[64,2048]{1,0:T(8,128)(2,1)S(1)}, u32[]{:S(2)}) copy-start(bf16[64,2048]{1,0:T(8,128)(2,1)S(1)} %collective-permute-done.9.refs_3_) | copy-start | bytes 786436
  44.7 13.9 %copy-start.13 = (bf16[384,512]{1,0:T(8,128)(2,1)}, bf16[384,512]{1,0:T(8,128)(2,1)S(1)}, u32[]{:S(2)}) copy-start(bf16[384,512]{1,0:T(8,128)(2,1)S(1)} %collective-permute-done.3.refs_11_) | copy-start | bytes 1179652
  44.7 13.9 %copy-start.14 = (bf16[384,512]{1,0:T(8,128)(2,1)}, bf16[384,512]{1,0:T(8,128)(2,1)S(1)}, u32[]{:S(2)}) copy-start(bf16[384,512]{1,0:T(8,128)(2,1)S(1)} %collective-permute-done.6.refs_12_) | copy-start | bytes 1179652
  44.8 5.1 %collective-permute-start.11 = (bf16[192,512]{1,0:T(8,128)(2,1)S(1)}, bf16[192,512]{1,0:T(8,128)(2,1)S(1)}, u32[]{:S(2)}, u32[]{:S(2)}) collective-permute-start(bf16[192,512]{1,0:T(8,128)(2,1)S(1)} %slice.193), channel_id=1, source_target_pairs={{0,56},{8,0},{16,8},{24,16},{32,24},{40,32},{48,40},{56,48},{1,57}... | collective-permute-start | bytes 589832 | tf_op jit(solution)/shard_map/ppermute | solution.py:343
  47.2 5.8 %collective-permute-start.13 = (bf16[192,512]{1,0:T(8,128)(2,1)S(1)}, bf16[192,512]{1,0:T(8,128)(2,1)S(1)}, u32[]{:S(2)}, u32[]{:S(2)}) collective-permute-start(bf16[192,512]{1,0:T(8,128)(2,1)S(1)} %slice.199), channel_id=1, source_target_pairs={{0,8},{8,16},{16,24},{24,32},{32,40},{40,48},{48,56},{56,0},{1,9},... | collective-permute-start | bytes 589832 | tf_op jit(solution)/shard_map/ppermute | solution.py:343
  49.8 11.9 %copy-start.21 = (bf16[192,512]{1,0:T(8,128)(2,1)}, bf16[192,512]{1,0:T(8,128)(2,1)S(1)}, u32[]{:S(2)}) copy-start(bf16[192,512]{1,0:T(8,128)(2,1)S(1)} %collective-permute-done.11.refs_14_) | copy-start | bytes 589828
  53.0 8.7 %copy-start.20 = (bf16[192,512]{1,0:T(8,128)(2,1)}, bf16[192,512]{1,0:T(8,128)(2,1)S(1)}, u32[]{:S(2)}) copy-start(bf16[192,512]{1,0:T(8,128)(2,1)S(1)} %collective-permute-done.13.refs_13_) | copy-start | bytes 589828
  53.1 8.6 %collective-permute-start.14 = (bf16[768,512]{1,0:T(8,128)(2,1)S(1)}, bf16[768,512]{1,0:T(8,128)(2,1)S(1)}, u32[]{:S(2)}, u32[]{:S(2)}) collective-permute-start(bf16[768,512]{1,0:T(8,128)(2,1)S(1)} %pad_maximum_fusion.1), channel_id=1, source_target_pairs={{0,2},{2,0},{1,3},{3,1},{4,6},{6,4},{5,7},{7,5},{8,10},{10,8},{9,1... | collective-permute-start | bytes 2359304 | tf_op jit(solution)/shard_map/ppermute | solution.py:343
  58.7 30.2 %collective-permute-start.19 = (bf16[8,4,32,512]{3,2,1,0:T(8,128)(2,1)S(1)}, bf16[8,4,32,512]{3,2,1,0:T(8,128)(2,1)S(1)}, u32[]{:S(2)}, u32[]{:S(2)}) collective-permute-start(bf16[8,4,32,512]{3,2,1,0:T(8,128)(2,1)S(1)} %bitcast.42), channel_id=1, source_target_pairs={{0,4},{4,0},{1,5},{5,1},{2,6},{6,2},{3,7},{7,3},{8,12},{12,8},{9,1... | collective-permute-start | bytes 3145736 | tf_op jit(solution)/shard_map/ppermute | solution.py:343
  59.2 30.0 %collective-permute-start.20 = (bf16[8,4,32,512]{3,2,1,0:T(8,128)(2,1)S(1)}, bf16[8,4,32,512]{3,2,1,0:T(8,128)(2,1)S(1)}, u32[]{:S(2)}, u32[]{:S(2)}) collective-permute-start(bf16[8,4,32,512]{3,2,1,0:T(8,128)(2,1)S(1)} %bitcast.43), channel_id=1, source_target_pairs={{0,5},{1,4},{4,1},{5,0},{2,7},{3,6},{6,3},{7,2},{8,13},{9,12},{12,... | collective-permute-start | bytes 3145736 | tf_op jit(solution)/shard_map/ppermute | solution.py:395
  85.5 3.9 %copy-start.9 = (bf16[128,2048]{1,0:T(8,128)(2,1)S(1)}, bf16[128,2048]{1,0:T(8,128)(2,1)}, u32[]{:S(2)}) copy-start(bf16[128,2048]{1,0:T(8,128)(2,1)} %param.9) | copy-start | bytes 1572868
  85.5 6.0 %collective-permute-start.15 = (bf16[32,2048]{1,0:T(8,128)(2,1)}, bf16[32,2048]{1,0:T(8,128)(2,1)S(1)}, u32[]{:S(2)}, u32[]{:S(2)}) collective-permute-start(bf16[32,2048]{1,0:T(8,128)(2,1)} %get-tuple-element.50), channel_id=1, source_target_pairs={{0,64},{64,128},{128,192},{192,0},{1,65},{65,129},{129,193},{193,1... | collective-permute-start | bytes 393224 | tf_op jit(solution)/shard_map/ppermute | solution.py:343
  85.6 9.3 %collective-permute-start.16 = (bf16[32,2048]{1,0:T(8,128)(2,1)}, bf16[32,2048]{1,0:T(8,128)(2,1)S(1)}, u32[]{:S(2)}, u32[]{:S(2)}) collective-permute-start(bf16[32,2048]{1,0:T(8,128)(2,1)} %get-tuple-element.51), channel_id=1, source_target_pairs={{0,128},{64,192},{128,0},{192,64},{1,129},{65,193},{129,1},{193,65... | collective-permute-start | bytes 393224 | tf_op jit(solution)/shard_map/ppermute | solution.py:343
  88.8 6.0 %collective-permute-start.17 = (bf16[32,2048]{1,0:T(8,128)(2,1)}, bf16[32,2048]{1,0:T(8,128)(2,1)S(1)}, u32[]{:S(2)}, u32[]{:S(2)}) collective-permute-start(bf16[32,2048]{1,0:T(8,128)(2,1)} %get-tuple-element.52), channel_id=1, source_target_pairs={{0,192},{64,0},{128,64},{192,128},{1,193},{65,1},{129,65},{193,129... | collective-permute-start | bytes 393224 | tf_op jit(solution)/shard_map/ppermute | solution.py:343
  88.9 6.0 %copy-start.31 = (bf16[64,2048]{1,0:T(8,128)(2,1)S(1)}, bf16[64,2048]{1,0:T(8,128)(2,1)}, u32[]{:S(2)}) copy-start(bf16[64,2048]{1,0:T(8,128)(2,1)} %get-tuple-element.58) | copy-start | bytes 786436
  88.9 6.0 %copy-start.7 = (bf16[32,2048]{1,0:T(8,128)(2,1)S(1)}, bf16[32,2048]{1,0:T(8,128)(2,1)}, u32[]{:S(2)}) copy-start(bf16[32,2048]{1,0:T(8,128)(2,1)} %get-tuple-element.49.r0) | copy-start | bytes 393220
  88.9 6.0 %copy-start.8 = (s32[5]{0:T(128)S(1)}, s32[5]{0:T(128)}, u32[]{:S(2)}) copy-start(s32[5]{0:T(128)} %stack.23.place) | copy-start | bytes 64
  88.9 13.5 %collective-permute-start.21 = (bf16[4,4,32,512]{3,2,1,0:T(8,128)(2,1)S(1)}, bf16[4,4,32,512]{3,2,1,0:T(8,128)(2,1)S(1)}, u32[]{:S(2)}, u32[]{:S(2)}) collective-permute-start(bf16[4,4,32,512]{3,2,1,0:T(8,128)(2,1)S(1)} %slice.249), channel_id=1, source_target_pairs={{0,5},{1,4},{4,1},{5,0},{2,7},{3,6},{6,3},{7,2},{8,13},{9,12},{12,... | collective-permute-start | bytes 1572872 | tf_op jit(solution)/shard_map/ppermute | solution.py:395
  89.3 13.2 %collective-permute-start.22 = (bf16[4,4,32,512]{3,2,1,0:T(8,128)(2,1)S(1)}, bf16[4,4,32,512]{3,2,1,0:T(8,128)(2,1)S(1)}, u32[]{:S(2)}, u32[]{:S(2)}) collective-permute-start(bf16[4,4,32,512]{3,2,1,0:T(8,128)(2,1)S(1)} %slice.250), channel_id=1, source_target_pairs={{0,4},{4,0},{1,5},{5,1},{2,6},{6,2},{3,7},{7,3},{8,12},{12,8},{9,1... | collective-permute-start | bytes 1572872 | tf_op jit(solution)/shard_map/ppermute | solution.py:343
  91.5 19.4 %collective-permute-start.25 = (bf16[80,2048]{1,0:T(8,128)(2,1)S(1)}, bf16[80,2048]{1,0:T(8,128)(2,1)}, u32[]{:S(2)}, u32[]{:S(2)}) collective-permute-start(bf16[80,2048]{1,0:T(8,128)(2,1)S(1)} %copy-done.28), channel_id=1, source_target_pairs={{0,192},{64,0},{128,64},{192,128},{1,193},{65,1},{129,65},{193,129... | collective-permute-start | bytes 983048 | tf_op jit(solution)/shard_map/ppermute | solution.py:343
  94.9 16.0 %collective-permute-start.24 = (bf16[64,2048]{1,0:T(8,128)(2,1)S(1)}, bf16[64,2048]{1,0:T(8,128)(2,1)}, u32[]{:S(2)}, u32[]{:S(2)}) collective-permute-start(bf16[64,2048]{1,0:T(8,128)(2,1)S(1)} %copy-done.31), channel_id=1, source_target_pairs={{0,64},{64,128},{128,192},{192,0},{1,65},{65,129},{129,193},{193,1... | collective-permute-start | bytes 786440 | tf_op jit(solution)/shard_map/ppermute | solution.py:343
  95.7 3.9 %collective-permute-start.18 = (bf16[2,16,512]{2,1,0:T(8,128)(2,1)S(1)}, bf16[2,16,512]{2,1,0:T(8,128)(2,1)S(1)}, u32[]{:S(2)}, u32[]{:S(2)}) collective-permute-start(bf16[2,16,512]{2,1,0:T(8,128)(2,1)S(1)} %get-tuple-element.55), channel_id=1, source_target_pairs={{0,2},{2,0},{1,3},{3,1},{4,6},{6,4},{5,7},{7,5},{8,10},{10,8},{9,1... | collective-permute-start | bytes 98312 | tf_op jit(solution)/shard_map/ppermute | solution.py:343
  102.5 3.4 %copy-start.1 = (bf16[4,4,32,512]{3,2,1,0:T(8,128)(2,1)}, bf16[4,4,32,512]{3,2,1,0:T(8,128)(2,1)S(1)}, u32[]{:S(2)}) copy-start(bf16[4,4,32,512]{3,2,1,0:T(8,128)(2,1)S(1)} %collective-permute-done.21.refs_3_) | copy-start | bytes 1572868
  102.5 3.4 %copy-start.3 = (bf16[4,4,32,512]{3,2,1,0:T(8,128)(2,1)}, bf16[4,4,32,512]{3,2,1,0:T(8,128)(2,1)S(1)}, u32[]{:S(2)}) copy-start(bf16[4,4,32,512]{3,2,1,0:T(8,128)(2,1)S(1)} %collective-permute-done.22.refs_4_) | copy-start | bytes 1572868
  102.5 8.6 %copy-start.25 = (f32[2048]{0:T(1024)S(1)}, f32[2048]{0:T(1024)}, u32[]{:S(2)}) copy-start(f32[2048]{0:T(1024)} %param.16) | copy-start | bytes 24580
  102.5 14.2 %copy-start.19 = (bf16[4,2048]{1,0:T(4,128)(2,1)S(1)}, bf16[4,2048]{1,0:T(4,128)(2,1)}, u32[]{:S(2)}) copy-start(bf16[4,2048]{1,0:T(4,128)(2,1)} %param.10) | copy-start | bytes 49156
  105.9 5.0 %collective-permute-start.23 = (bf16[16,2048]{1,0:T(8,128)(2,1)S(1)}, bf16[16,2048]{1,0:T(8,128)(2,1)S(1)}, u32[]{:S(2)}, u32[]{:S(2)}) collective-permute-start(bf16[16,2048]{1,0:T(8,128)(2,1)S(1)} %get-tuple-element.57), channel_id=1, source_target_pairs={{0,2},{2,0},{1,3},{3,1},{4,6},{6,4},{5,7},{7,5},{8,10},{10,8},{9,1... | collective-permute-start | bytes 196616 | tf_op jit(solution)/shard_map/ppermute | solution.py:343
  108.1 16.5 %collective-permute-start.26 = (bf16[144,2048]{1,0:T(8,128)(2,1)}, bf16[144,2048]{1,0:T(8,128)(2,1)}, u32[]{:S(2)}, u32[]{:S(2)}) collective-permute-start(bf16[144,2048]{1,0:T(8,128)(2,1)} %get-tuple-element.61), channel_id=1, source_target_pairs={{0,64},{64,128},{128,192},{192,0},{1,65},{65,129},{129,193},{193,1... | collective-permute-start | bytes 1769480 | tf_op jit(solution)/shard_map/ppermute | solution.py:343
  109.7 17.1 %collective-permute-start.27 = (bf16[144,2048]{1,0:T(8,128)(2,1)}, bf16[144,2048]{1,0:T(8,128)(2,1)}, u32[]{:S(2)}, u32[]{:S(2)}) collective-permute-start(bf16[144,2048]{1,0:T(8,128)(2,1)} %get-tuple-element.62), channel_id=1, source_target_pairs={{0,192},{64,0},{128,64},{192,128},{1,193},{65,1},{129,65},{193,129... | collective-permute-start | bytes 1769480 | tf_op jit(solution)/shard_map/ppermute | solution.py:343
  111.8 15.4 %all-to-all-start = ((bf16[8,8,2048]{2,1,0:T(8,128)(2,1)}), bf16[8,8,2048]{2,1,0:T(8,128)(2,1)S(1)}, u32[]{:S(2)}, u32[]{:S(2)}) async-start(bf16[8,8,2048]{2,1,0:T(8,128)(2,1)} %broadcast_in_dim.4), calls=%async_computation | async-start | bytes 524288 | tf_op jit(solution)/shard_map/all_to_all | solution.py:401
  116.7 16.5 %collective-permute-start.31 = (bf16[80,2048]{1,0:T(8,128)(2,1)}, bf16[80,2048]{1,0:T(8,128)(2,1)}, u32[]{:S(2)}, u32[]{:S(2)}) collective-permute-start(bf16[80,2048]{1,0:T(8,128)(2,1)} %collective-permute-done.25), channel_id=1, source_target_pairs={{0,192},{64,0},{128,64},{192,128},{1,193},{65,1},{129,65},{193,129... | collective-permute-start | bytes 983048 | tf_op jit(solution)/shard_map/ppermute | solution.py:343
  116.8 16.4 %collective-permute-start.30 = (bf16[64,2048]{1,0:T(8,128)(2,1)}, bf16[64,2048]{1,0:T(8,128)(2,1)}, u32[]{:S(2)}, u32[]{:S(2)}) collective-permute-start(bf16[64,2048]{1,0:T(8,128)(2,1)} %collective-permute-done.24), channel_id=1, source_target_pairs={{0,64},{64,128},{128,192},{192,0},{1,65},{65,129},{129,193},{193,1... | collective-permute-start | bytes 786440 | tf_op jit(solution)/shard_map/ppermute | solution.py:343
  118.3 21.4 %collective-permute-start.29 = (bf16[3,2048]{1,0:T(4,128)(2,1)S(1)}, bf16[3,2048]{1,0:T(4,128)(2,1)S(1)}, u32[]{:S(2)}, u32[]{:S(2)}) collective-permute-start(bf16[3,2048]{1,0:T(4,128)(2,1)S(1)} %get-tuple-element.103), channel_id=1, source_target_pairs={{2,0},{4,2},{6,4},{8,6},{10,8},{12,10},{14,12},{16,14},{18,16},{20... | collective-permute-start | bytes 36872 | tf_op jit(solution)/shard_map/ppermute | solution.py:335
  124.7 20.4 %collective-permute-start.28 = (bf16[3,2048]{1,0:T(4,128)(2,1)S(1)}, bf16[3,2048]{1,0:T(4,128)(2,1)S(1)}, u32[]{:S(2)}, u32[]{:S(2)}) collective-permute-start(bf16[3,2048]{1,0:T(4,128)(2,1)S(1)} %get-tuple-element.102), channel_id=1, source_target_pairs={{0,2},{2,4},{4,6},{6,8},{8,10},{10,12},{12,14},{14,16},{16,18},{18... | collective-permute-start | bytes 36872 | tf_op jit(solution)/shard_map/ppermute | solution.py:334
  128.8 28.8 %all-to-all-start.1 = ((bf16[8,64,2048]{2,1,0:T(8,128)(2,1)}), bf16[8,64,2048]{2,1,0:T(8,128)(2,1)}, u32[]{:S(2)}, u32[]{:S(2)}) async-start(bf16[8,64,2048]{2,1,0:T(8,128)(2,1)} %broadcast_in_dim.5), calls=%async_computation.1 | async-start | bytes 4194304 | tf_op jit(solution)/shard_map/all_to_all | solution.py:423
  134.5 5.1 %copy-start.10 = (bf16[128,2048]{1,0:T(8,128)(2,1)S(1)}, bf16[128,2048]{1,0:T(8,128)(2,1)}, u32[]{:S(2)}) copy-start(bf16[128,2048]{1,0:T(8,128)(2,1)} %param.9) | copy-start | bytes 1572868
  134.5 5.1 %copy-start.12 = (bf16[64,2048]{1,0:T(8,128)(2,1)S(1)}, bf16[64,2048]{1,0:T(8,128)(2,1)}, u32[]{:S(2)}) copy-start(bf16[64,2048]{1,0:T(8,128)(2,1)} %get-tuple-element.81) | copy-start | bytes 786436
  134.5 6.2 %copy-start.2 = (bf16[4,4,32,512]{3,2,1,0:T(8,128)(2,1)S(1)}, bf16[4,4,32,512]{3,2,1,0:T(8,128)(2,1)}, u32[]{:S(2)}) copy-start(bf16[4,4,32,512]{3,2,1,0:T(8,128)(2,1)} %copy-done.1) | copy-start | bytes 1572868
  134.6 6.3 %copy-start.4 = (bf16[4,4,32,512]{3,2,1,0:T(8,128)(2,1)S(1)}, bf16[4,4,32,512]{3,2,1,0:T(8,128)(2,1)}, u32[]{:S(2)}) copy-start(bf16[4,4,32,512]{3,2,1,0:T(8,128)(2,1)} %copy-done.3) | copy-start | bytes 1572868
  137.3 3.5 %collective-permute-start.32 = (bf16[2,128,512]{2,1,0:T(8,128)(2,1)S(1)}, bf16[2,128,512]{2,1,0:T(8,128)(2,1)S(1)}, u32[]{:S(2)}, u32[]{:S(2)}) collective-permute-start(bf16[2,128,512]{2,1,0:T(8,128)(2,1)S(1)} %get-tuple-element.73), channel_id=1, source_target_pairs={{0,2},{2,0},{1,3},{3,1},{4,6},{6,4},{5,7},{7,5},{8,10},{10,8},{9,1... | collective-permute-start | bytes 786440 | tf_op jit(solution)/shard_map/ppermute | solution.py:343
  140.8 4.3 %copy-start.11 = (bf16[64,2048]{1,0:T(8,128)(2,1)S(1)}, bf16[64,2048]{1,0:T(8,128)(2,1)}, u32[]{:S(2)}) copy-start(bf16[64,2048]{1,0:T(8,128)(2,1)} %get-tuple-element.80) | copy-start | bytes 786436
  144.6 2.0 %collective-permute-start.33 = (bf16[128,2048]{1,0:T(8,128)(2,1)S(1)}, bf16[128,2048]{1,0:T(8,128)(2,1)S(1)}, u32[]{:S(2)}, u32[]{:S(2)}) collective-permute-start(bf16[128,2048]{1,0:T(8,128)(2,1)S(1)} %get-tuple-element.75), channel_id=1, source_target_pairs={{0,2},{2,0},{1,3},{3,1},{4,6},{6,4},{5,7},{7,5},{8,10},{10,8},{9,1... | collective-permute-start | bytes 1572872 | tf_op jit(solution)/shard_map/ppermute | solution.py:343
  146.6 14.4 %copy-start = (bf16[2048,640]{1,0:T(8,128)(2,1)S(1)}, bf16[2048,640]{1,0:T(8,128)(2,1)}, u32[]{:S(2)}) copy-start(bf16[2048,640]{1,0:T(8,128)(2,1)} %w_ref.3) | copy-start | bytes 7864324
  157.6 7.5 %collective-permute-start.34 = (bf16[512,2048]{1,0:T(8,128)(2,1)}, bf16[512,2048]{1,0:T(8,128)(2,1)S(1)}, u32[]{:S(2)}, u32[]{:S(2)}) collective-permute-start(bf16[512,2048]{1,0:T(8,128)(2,1)} %bitcast.19.x_ref), channel_id=1, source_target_pairs={{0,2},{2,0},{1,3},{3,1},{4,6},{6,4},{5,7},{7,5},{8,10},{10,8},{9,1... | collective-permute-start | bytes 6291464 | tf_op jit(solution)/shard_map/ppermute | solution.py:343
  (5 other events, 7.2 us)
